TPU v7x, 32 devices: a whole 2x2x4 slice. The times are simulated.
32 devices in a mesh: node: 8 (over y, x, core), local: 4 (over z).
Axes of the slice: x: 2, y: 2, z: 4, core: 2. Of those that a mesh axis runs over, the one named last changes fastest.
Arguments:
- tokens_x: bfloat16 [4096, 2048], P(('node', 'local')), may hold values from -6 to 6
- grad_out: bfloat16 [4096, 2048], P(('node', 'local')), may hold values from -6 to 6
- expert_ids: int32 [4096, 8], P(('node', 'local')), may hold values from 0 to 31, all different within a row; in each aligned block of 128 rows (0 to 127, 128 to 255, ...) at most 33 rows name the same one
- probs: bfloat16 [4096, 8], P(('node', 'local')), may hold values from 0.049804688 to 0.34960938
- w_gate: bfloat16 [32, 2048, 768], P(('node', 'local')), may hold values from -0.125 to 0.125
- w_up: bfloat16 [32, 2048, 768], P(('node', 'local')), may hold values from -0.125 to 0.125
- w_down: bfloat16 [32, 768, 2048], P(('node', 'local')), may hold values from -0.21875 to 0.21875
Outputs:
- grad_x: bfloat16 [4096, 2048], P(('node', 'local'))
- grad_probs: bfloat16 [4096, 8], P(('node', 'local'))
- grad_gate: bfloat16 [32, 2048, 768], P(('node', 'local'))
- grad_up: bfloat16 [32, 2048, 768], P(('node', 'local'))
- grad_down: bfloat16 [32, 768, 2048], P(('node', 'local'))
Inputs may be any that keep to these rules, and one draw needn't show every extreme that they name: `expert_ids`: each row names 8 different experts; among the 128 tokens of one device no expert is named more than 33 times, a bound that some block reaches.
All inputs are finite; a program needn't handle non-finite values.
Results may differ from a plain program's by a relative error of at most 0.0065.
Values may be sent and summed in bfloat16 or wider, within the bound.
No kernel may reach another device: no remote copies, remote signals or barrier semaphores. Data moves between devices by JAX's collectives and lax.ppermute only.
A program may use at most 128 MiB of HBM per device.

v0:
```python
import jax
import jax.numpy as jnp
from jax import lax
from jax.sharding import PartitionSpec as P


def expert_backward(rows_x, rows_dy, rows_p, gate_e, up_e, down_e):
    gate_pre = jnp.dot(rows_x, gate_e, preferred_element_type=jnp.float32)
    up_pre = jnp.dot(rows_x, up_e, preferred_element_type=jnp.float32)
    sigmoid_g = jax.nn.sigmoid(gate_pre)
    activated = gate_pre * sigmoid_g
    hidden_f = activated * up_pre
    hidden_grad = lax.dot_general(
        rows_dy, down_e, (((1,), (1,)), ((), ())), preferred_element_type=jnp.float32
    )
    prob_grad = jnp.sum(hidden_grad * hidden_f, axis=1).astype(jnp.bfloat16)
    weight_col = rows_p.astype(jnp.float32)[:, None]
    scaled_grad = hidden_grad * weight_col
    weighted_hidden = (hidden_f * weight_col).astype(jnp.bfloat16)
    up_rows = (scaled_grad * activated).astype(jnp.bfloat16)
    gate_rows = (scaled_grad * up_pre * sigmoid_g * (1.0 + gate_pre * (1.0 - sigmoid_g))).astype(
        jnp.bfloat16
    )
    input_grad = lax.dot_general(
        gate_rows, gate_e, (((1,), (1,)), ((), ())), preferred_element_type=jnp.float32
    )
    input_grad = input_grad + lax.dot_general(
        up_rows, up_e, (((1,), (1,)), ((), ())), preferred_element_type=jnp.float32
    )
    input_grad = input_grad.astype(jnp.bfloat16)
    gate_wgrad = lax.dot_general(
        rows_x, gate_rows, (((0,), (0,)), ((), ())), preferred_element_type=jnp.float32
    ).astype(jnp.bfloat16)
    up_wgrad = lax.dot_general(
        rows_x, up_rows, (((0,), (0,)), ((), ())), preferred_element_type=jnp.float32
    ).astype(jnp.bfloat16)
    down_wgrad = lax.dot_general(
        weighted_hidden, rows_dy, (((0,), (0,)), ((), ())), preferred_element_type=jnp.float32
    ).astype(jnp.bfloat16)
    return (input_grad, prob_grad, gate_wgrad, up_wgrad, down_wgrad)


def shards(tokens_x, grad_out, expert_ids, probs, w_gate, w_up, w_down):
    node_count = lax.axis_size("node")
    local_count = lax.axis_size("local")
    experts = node_count * local_count
    tok_count, top_count = expert_ids.shape
    width = tokens_x.shape[1]
    capacity = tok_count * top_count // experts + 1
    flat_ids = expert_ids.reshape(-1)
    row_count = flat_ids.shape[0]
    one_hot = (flat_ids[:, None] == jnp.arange(experts, dtype=jnp.int32)[None, :]).astype(jnp.int32)
    earlier = jnp.cumsum(one_hot, axis=0) - 1
    slot_index = jnp.sum(earlier * one_hot, axis=1)
    target = flat_ids * capacity + slot_index
    source_row = (
        jnp.full((experts * capacity,), row_count, jnp.int32)
        .at[target]
        .set(jnp.arange(row_count, dtype=jnp.int32))
    )
    source_token = source_row // top_count
    padded_x = jnp.concatenate([tokens_x, jnp.zeros((1, width), jnp.bfloat16)], axis=0)
    padded_dy = jnp.concatenate([grad_out, jnp.zeros((1, width), jnp.bfloat16)], axis=0)
    padded_p = jnp.concatenate([probs.reshape(-1), jnp.zeros((1,), jnp.bfloat16)], axis=0)
    send_x = padded_x[source_token]
    send_dy = padded_dy[source_token]
    send_p = padded_p[source_row]
    grid_rows = (node_count, local_count, capacity, width)
    grid_probs = (node_count, local_count, capacity)
    recv_x, recv_dy, recv_p = (
        lax.all_to_all(
            lax.all_to_all(
                send_x.reshape(grid_rows), "node", split_axis=0, concat_axis=0, tiled=True
            ),
            "local",
            split_axis=1,
            concat_axis=1,
            tiled=True,
        ),
        lax.all_to_all(
            lax.all_to_all(
                send_dy.reshape(grid_rows), "node", split_axis=0, concat_axis=0, tiled=True
            ),
            "local",
            split_axis=1,
            concat_axis=1,
            tiled=True,
        ),
        lax.all_to_all(
            lax.all_to_all(
                send_p.reshape(grid_probs), "node", split_axis=0, concat_axis=0, tiled=True
            ),
            "local",
            split_axis=1,
            concat_axis=1,
            tiled=True,
        ),
    )
    input_grad, prob_grad, gate_wgrad, up_wgrad, down_wgrad = expert_backward(
        recv_x.reshape(-1, width),
        recv_dy.reshape(-1, width),
        recv_p.reshape(-1),
        w_gate[0],
        w_up[0],
        w_down[0],
    )
    back_x, back_p = (
        lax.all_to_all(
            lax.all_to_all(
                input_grad.reshape(grid_rows), "node", split_axis=0, concat_axis=0, tiled=True
            ),
            "local",
            split_axis=1,
            concat_axis=1,
            tiled=True,
        ),
        lax.all_to_all(
            lax.all_to_all(
                prob_grad.reshape(grid_probs), "node", split_axis=0, concat_axis=0, tiled=True
            ),
            "local",
            split_axis=1,
            concat_axis=1,
            tiled=True,
        ),
    )
    back_x = back_x.reshape(experts * capacity, width)
    back_p = back_p.reshape(experts * capacity)
    token_parts = back_x[target].reshape(tok_count, top_count, width)
    grad_x = jnp.sum(token_parts.astype(jnp.float32), axis=1).astype(jnp.bfloat16)
    grad_probs = back_p[target].reshape(tok_count, top_count)
    return (grad_x, grad_probs, gate_wgrad[None], up_wgrad[None], down_wgrad[None])


def solution(mesh):
    in_specs = (
        P(("node", "local"), None),
        P(("node", "local"), None),
        P(("node", "local"), None),
        P(("node", "local"), None),
        P(("node", "local"), None, None),
        P(("node", "local"), None, None),
        P(("node", "local"), None, None),
    )
    out_specs = (
        P(("node", "local"), None),
        P(("node", "local"), None),
        P(("node", "local"), None, None),
        P(("node", "local"), None, None),
        P(("node", "local"), None, None),
    )
    return jax.shard_map(shards, mesh=mesh, in_specs=in_specs, out_specs=out_specs, check_vma=False)
```

profile of v0, /device:TPU:0, one launch (start us, length us, event | category | flops | bytes accessed | tf_op | source)
XLA Modules:
  0.0 629.4 jit_solution(7537977050049652586)
XLA Ops:
  3.7 9.0 %reduce-window.6 = s32[32,8,128]{2,1,0:T(8,128)S(1)} reduce-window(s32[32,8,128]{2,1,0:T(8,128)S(1)} %fusion.18, s32[]{:T(128)} %constant.17.clone.1), window={size=1x1x128 pad=0_0x0_0x127_0}, to_apply=%region_0.0 | reduce-window | flops 4161536 | bytes 262148 | tf_op jit(solution)/shard_map/reduce-window
  13.2 4.3 scatter_custom_fusion
  17.6 6.9 %gather_fusion.1 = bf16[1056]{0:T(1024)(128)(2,1)S(1)} fusion(bf16[1025]{0:T(1024)(128)(2,1)S(1)} %pad_maximum_fusion, s32[2048]{0:T(1024)S(1)} %get-tuple-element.25), kind=kCustom, calls=%fused_computation.1 | custom fusion | bytes 8448 | tf_op jit(solution)/shard_map/gather | solution.py:67
  24.7 9.7 %all_to_all.50 = bf16[8,4,33]{2,1,0:T(4,128)(2,1)S(1)} all-to-all(bf16[8,4,33]{2,1,0:T(4,128)(2,1)S(1)} %reshape.106), channel_id=1, replica_groups=mesh['node'=8,'local'=4] {'node'}, dimensions={0} | all-to-all | bytes 4224 | tf_op jit(solution)/shard_map/all_to_all | solution.py:90
  35.0 4.9 all-to-all-start.3
  41.8 11.6 %gather_fusion = bf16[1056,2048]{1,0:T(8,128)(2,1)} fusion(bf16[129,2048]{1,0:T(8,128)(2,1)} %concatenate.9, s32[2048]{0:T(1024)S(1)} %get-tuple-element.26), kind=kCustom, calls=%fused_computation | custom fusion | bytes 8654976 | tf_op jit(solution)/shard_map/gather | solution.py:66
  53.4 5.6 reshape.103
  59.0 8.0 %copy.40 = bf16[8,4,33,2048]{3,1,2,0:T(4,128)(2,1)} copy(bf16[8,4,33,2048]{3,2,1,0:T(8,128)(2,1)} %reshape.103) | data formatting | bytes 8650752 | tf_op jit(solution)/shard_map/reshape | solution.py:82
  67.0 4.8 all-to-all-start
  71.8 1.9 concatenate.11
  73.7 11.6 %gather_fusion.2 = bf16[1056,2048]{1,0:T(8,128)(2,1)} fusion(bf16[129,2048]{1,0:T(8,128)(2,1)} %concatenate.11, s32[2048]{0:T(1024)S(1)} %get-tuple-element.26), kind=kCustom, calls=%fused_computation.2 | custom fusion | bytes 8654976 | tf_op jit(solution)/shard_map/gather | solution.py:65
  85.3 5.6 reshape.107
  90.9 7.9 %copy.46 = bf16[8,4,33,2048]{3,1,2,0:T(4,128)(2,1)} copy(bf16[8,4,33,2048]{3,2,1,0:T(8,128)(2,1)} %reshape.107) | data formatting | bytes 8650752 | tf_op jit(solution)/shard_map/reshape | solution.py:73
  98.9 23.5 %all-to-all-done = bf16[8,4,33,2048]{3,1,2,0:T(4,128)(2,1)} async-done(((bf16[8,4,33,2048]{3,1,2,0:T(4,128)(2,1)}), bf16[8,4,33,2048]{3,1,2,0:T(4,128)(2,1)}, u32[]{:S(2)}, u32[]{:S(2)}) %all-to-all-start) | async-done | bytes 4325408 | tf_op jit(solution)/shard_map/all_to_all | solution.py:81
  122.3 4.6 all-to-all-start.4
  126.9 6.6 %copy.41 = bf16[8,4,33,2048]{3,0,2,1:T(8,128)(2,1)} copy(bf16[8,4,33,2048]{3,1,2,0:T(4,128)(2,1)} %all-to-all-done) | data formatting | bytes 8650752 | tf_op jit(solution)/shard_map/all_to_all | solution.py:81
  133.6 43.9 %all-to-all-done.4 = bf16[8,4,33,2048]{3,1,2,0:T(4,128)(2,1)} async-done(((bf16[8,4,33,2048]{3,1,2,0:T(4,128)(2,1)}), bf16[8,4,33,2048]{3,1,2,0:T(4,128)(2,1)}, u32[]{:S(2)}, u32[]{:S(2)}) %all-to-all-start.4) | async-done | bytes 4325408 | tf_op jit(solution)/shard_map/all_to_all | solution.py:72
  177.5 5.1 all-to-all-start.1
  182.6 6.7 %copy.47 = bf16[8,4,33,2048]{3,0,2,1:T(8,128)(2,1)} copy(bf16[8,4,33,2048]{3,1,2,0:T(4,128)(2,1)} %all-to-all-done.4) | data formatting | bytes 8650752 | tf_op jit(solution)/shard_map/all_to_all | solution.py:72
  189.2 86.8 %all-to-all-done.1 = bf16[8,4,33,2048]{3,0,2,1:T(8,128)(2,1)} async-done(((bf16[8,4,33,2048]{3,0,2,1:T(8,128)(2,1)}), bf16[8,4,33,2048]{3,0,2,1:T(8,128)(2,1)}, u32[]{:S(2)}, u32[]{:S(2)}) %all-to-all-start.1) | async-done | bytes 4325408 | tf_op jit(solution)/shard_map/all_to_all | solution.py:80
  276.0 5.3 all-to-all-start.5
  281.5 7.0 %copy.42 = bf16[8,4,33,2048]{3,2,1,0:T(8,128)(2,1)} copy(bf16[8,4,33,2048]{3,0,2,1:T(8,128)(2,1)} %all-to-all-done.1) | data formatting | bytes 8650752 | tf_op jit(solution)/shard_map/all_to_all | solution.py:80
  288.4 5.6 reshape.104
  294.0 82.7 %all-to-all-done.5 = bf16[8,4,33,2048]{3,0,2,1:T(8,128)(2,1)} async-done(((bf16[8,4,33,2048]{3,0,2,1:T(8,128)(2,1)}), bf16[8,4,33,2048]{3,0,2,1:T(8,128)(2,1)}, u32[]{:S(2)}, u32[]{:S(2)}) %all-to-all-start.5) | async-done | bytes 4325408 | tf_op jit(solution)/shard_map/all_to_all | solution.py:71
  376.8 7.0 %copy.48 = bf16[8,4,33,2048]{3,2,1,0:T(8,128)(2,1)} copy(bf16[8,4,33,2048]{3,0,2,1:T(8,128)(2,1)} %all-to-all-done.5) | data formatting | bytes 8650752 | tf_op jit(solution)/shard_map/all_to_all | solution.py:71
  383.7 5.7 reshape.108
  389.4 5.6 fusion.4
  395.1 3.5 fusion.7
  398.7 6.3 multiply_reduce_fusion
  405.7 5.4 all-to-all-start.8
  411.1 5.1 fusion.2
  416.2 5.2 fusion
  421.4 5.6 reshape.109
  427.0 7.9 %copy.49 = bf16[8,4,33,2048]{3,1,2,0:T(4,128)(2,1)} copy(bf16[8,4,33,2048]{3,2,1,0:T(8,128)(2,1)} %reshape.109) | data formatting | bytes 8650752 | tf_op jit(solution)/shard_map/reshape | solution.py:110
  435.0 4.6 all-to-all-start.6
  440.2 49.8 %all-to-all-done.6 = bf16[8,4,33,2048]{3,1,2,0:T(4,128)(2,1)} async-done(((bf16[8,4,33,2048]{3,1,2,0:T(4,128)(2,1)}), bf16[8,4,33,2048]{3,1,2,0:T(4,128)(2,1)}, u32[]{:S(2)}, u32[]{:S(2)}) %all-to-all-start.6) | async-done | bytes 4325408 | tf_op jit(solution)/shard_map/all_to_all | solution.py:109
  490.1 3.2 all-to-all-start.9
  493.3 6.6 %copy.50 = bf16[8,4,33,2048]{3,0,2,1:T(8,128)(2,1)} copy(bf16[8,4,33,2048]{3,1,2,0:T(4,128)(2,1)} %all-to-all-done.6) | data formatting | bytes 8650752 | tf_op jit(solution)/shard_map/all_to_all | solution.py:109
  500.0 5.4 all-to-all-start.7
  505.4 8.2 %fusion.11 = bf16[1,2048,768]{2,1,0:T(8,128)(2,1)} fusion(bf16[1056,2048]{1,0:T(8,128)(2,1)} %reshape.108, bf16[1056,768]{1,0:T(8,128)(2,1)S(1)} %copy-done.10), kind=kOutput, calls=%fused_computation.27 | convolution fusion | flops 3323461632 | bytes 9093120 | tf_op jit(solution)/shard_map/dot_general | solution.py:31
  513.7 5.7 fusion.12
  519.4 6.2 fusion.13
  525.9 6.8 %gather_fusion.4 = bf16[1024]{0:T(1024)(128)(2,1)S(1)} fusion(bf16[1056]{0:T(1024)(128)(2,1)S(1)} %reshape.112, s32[1024]{0:T(1024)S(1)} %broadcast_clamp_fusion), kind=kCustom, calls=%fused_computation.4 | custom fusion | bytes 8192 | tf_op jit(solution)/shard_map/gather | solution.py:131
  533.4 65.1 %all-to-all-done.7 = bf16[8,4,33,2048]{3,0,2,1:T(8,128)(2,1)} async-done(((bf16[8,4,33,2048]{3,0,2,1:T(8,128)(2,1)}), bf16[8,4,33,2048]{3,0,2,1:T(8,128)(2,1)}, u32[]{:S(2)}, u32[]{:S(2)}) %all-to-all-start.7) | async-done | bytes 4325408 | tf_op jit(solution)/shard_map/all_to_all | solution.py:108
  598.6 7.0 %copy.51 = bf16[8,4,33,2048]{3,2,1,0:T(8,128)(2,1)} copy(bf16[8,4,33,2048]{3,0,2,1:T(8,128)(2,1)} %all-to-all-done.7) | data formatting | bytes 8650752 | tf_op jit(solution)/shard_map/all_to_all | solution.py:108
  605.6 5.6 reshape.110
  611.2 12.0 %gather_fusion.3 = bf16[1024,2048]{1,0:T(8,128)(2,1)} fusion(bf16[1056,2048]{1,0:T(8,128)(2,1)} %reshape.110, s32[1024]{0:T(1024)S(1)} %broadcast_clamp_fusion), kind=kCustom, calls=%fused_computation.3 | custom fusion | bytes 8392704 | tf_op jit(solution)/shard_map/gather | solution.py:129
  623.2 5.9 bitcast_reduce_fusion
  (81 shorter events, 8.9 us)
Async XLA Ops:
  0.6 388.8 %copy-start = (bf16[1,2048,768]{2,1,0:T(8,128)(2,1)S(1)}, bf16[1,2048,768]{2,1,0:T(8,128)(2,1)}, u32[]{:S(2)}) copy-start(bf16[1,2048,768]{2,1,0:T(8,128)(2,1)} %param.11) | copy-start | bytes 9437188
  35.0 32.0 %all-to-all-start.3 = ((bf16[4,2,132]{2,1,0:T(2,128)(2,1)}), bf16[4,2,132]{2,1,0:T(2,128)(2,1)S(1)}, u32[]{:S(2)}, u32[]{:S(2)}) async-start(bf16[4,2,132]{2,1,0:T(2,128)(2,1)} %reshape.168), calls=%async_computation.3 | async-start | bytes 8192 | tf_op jit(solution)/shard_map/all_to_all | solution.py:89
  67.0 55.3 %all-to-all-start = ((bf16[8,4,33,2048]{3,1,2,0:T(4,128)(2,1)}), bf16[8,4,33,2048]{3,1,2,0:T(4,128)(2,1)}, u32[]{:S(2)}, u32[]{:S(2)}) async-start(bf16[8,4,33,2048]{3,1,2,0:T(4,128)(2,1)} %copy.40), calls=%async_computation | async-start | bytes 8650752 | tf_op jit(solution)/shard_map/all_to_all | solution.py:81
  122.3 55.1 %all-to-all-start.4 = ((bf16[8,4,33,2048]{3,1,2,0:T(4,128)(2,1)}), bf16[8,4,33,2048]{3,1,2,0:T(4,128)(2,1)}, u32[]{:S(2)}, u32[]{:S(2)}) async-start(bf16[8,4,33,2048]{3,1,2,0:T(4,128)(2,1)} %copy.46), calls=%async_computation.4 | async-start | bytes 8650752 | tf_op jit(solution)/shard_map/all_to_all | solution.py:72
  177.5 98.5 %all-to-all-start.1 = ((bf16[8,4,33,2048]{3,0,2,1:T(8,128)(2,1)}), bf16[8,4,33,2048]{3,0,2,1:T(8,128)(2,1)}, u32[]{:S(2)}, u32[]{:S(2)}) async-start(bf16[8,4,33,2048]{3,0,2,1:T(8,128)(2,1)} %copy.41), calls=%async_computation.1 | async-start | bytes 8650752 | tf_op jit(solution)/shard_map/all_to_all | solution.py:80
  276.0 100.8 %all-to-all-start.5 = ((bf16[8,4,33,2048]{3,0,2,1:T(8,128)(2,1)}), bf16[8,4,33,2048]{3,0,2,1:T(8,128)(2,1)}, u32[]{:S(2)}, u32[]{:S(2)}) async-start(bf16[8,4,33,2048]{3,0,2,1:T(8,128)(2,1)} %copy.47), calls=%async_computation.5 | async-start | bytes 8650752 | tf_op jit(solution)/shard_map/all_to_all | solution.py:71
  389.4 5.6 copy-start.2
  389.4 5.6 copy-start.4
  389.4 9.2 %slice-start = ((s8[4325376]{0:T(1024)(128)(4,1)}), s8[4194304]{0:T(1024)(128)(4,1)S(1)}, s32[]{:S(2)}) async-start(s8[4325376]{0:T(1024)(128)(4,1)} %bitcast.58), calls=%async_computation.10 | async-start | bytes 8388608
  395.0 3.6 copy-start.6
  395.0 3.6 slice-start.1
  395.0 3.6 copy-start.3
  398.7 6.3 copy-start.8
  405.7 29.3 %all-to-all-start.8 = ((bf16[8,4,33]{2,1,0:T(4,128)(2,1)}), bf16[8,4,33]{2,1,0:T(4,128)(2,1)S(1)}, u32[]{:S(2)}, u32[]{:S(2)}) async-start(bf16[8,4,33]{2,1,0:T(4,128)(2,1)} %convert_element_type.52), calls=%async_computation.8 | async-start | bytes 16384 | tf_op jit(solution)/shard_map/all_to_all | solution.py:118
  411.1 5.2 copy-start.5
  411.1 5.2 copy-start.11
  435.0 55.1 %all-to-all-start.6 = ((bf16[8,4,33,2048]{3,1,2,0:T(4,128)(2,1)}), bf16[8,4,33,2048]{3,1,2,0:T(4,128)(2,1)}, u32[]{:S(2)}, u32[]{:S(2)}) async-start(bf16[8,4,33,2048]{3,1,2,0:T(4,128)(2,1)} %copy.49), calls=%async_computation.6 | async-start | bytes 8650752 | tf_op jit(solution)/shard_map/all_to_all | solution.py:109
  490.1 9.9 %all-to-all-start.9 = ((bf16[4,2,132]{2,1,0:T(2,128)(2,1)}), bf16[4,2,132]{2,1,0:T(2,128)(2,1)S(1)}, u32[]{:S(2)}, u32[]{:S(2)}) async-start(bf16[4,2,132]{2,1,0:T(2,128)(2,1)} %reshape.170), calls=%async_computation.9 | async-start | bytes 8192 | tf_op jit(solution)/shard_map/all_to_all | solution.py:117
  499.9 5.4 copy-start.10
  500.0 13.7 %slice-start.4 = ((s8[4325376]{0:T(1024)(128)(4,1)}), s8[131072]{0:T(1024)(128)(4,1)S(1)}, s32[]{:S(2)}) async-start(s8[4325376]{0:T(1024)(128)(4,1)} %bitcast.62), calls=%async_computation.14 | async-start | bytes 262144
  500.0 98.6 %all-to-all-start.7 = ((bf16[8,4,33,2048]{3,0,2,1:T(8,128)(2,1)}), bf16[8,4,33,2048]{3,0,2,1:T(8,128)(2,1)}, u32[]{:S(2)}, u32[]{:S(2)}) async-start(bf16[8,4,33,2048]{3,0,2,1:T(8,128)(2,1)} %copy.50), calls=%async_computation.7 | async-start | bytes 8650752 | tf_op jit(solution)/shard_map/all_to_all | solution.py:108
  505.4 8.2 %slice-start.5 = ((s8[4325376]{0:T(1024)(128)(4,1)}), s8[4194304]{0:T(1024)(128)(4,1)S(1)}, s32[]{:S(2)}) async-start(s8[4325376]{0:T(1024)(128)(4,1)} %bitcast.62), calls=%async_computation.15 | async-start | bytes 8388608
  505.4 8.2 %copy-start.12 = (bf16[1056,768]{1,0:T(8,128)(2,1)S(1)}, bf16[1056,768]{1,0:T(8,128)(2,1)}, u32[]{:S(2)}) copy-start(bf16[1056,768]{1,0:T(8,128)(2,1)} %get-tuple-element.22) | copy-start | bytes 4866052
  505.4 14.0 %slice-start.2 = ((s8[4325376]{0:T(1024)(128)(4,1)}), s8[4194304]{0:T(1024)(128)(4,1)S(1)}, s32[]{:S(2)}) async-start(s8[4325376]{0:T(1024)(128)(4,1)} %bitcast.60), calls=%async_computation.12 | async-start | bytes 8388608
  513.7 5.8 slice-start.3
  513.7 5.8 copy-start.7
  513.7 5.8 copy-start.9
  611.2 17.9 %copy-start.1 = (bf16[1,2048,768]{2,1,0:T(8,128)(2,1)S(1)}, bf16[1,2048,768]{2,1,0:T(8,128)(2,1)}, u32[]{:S(2)}) copy-start(bf16[1,2048,768]{2,1,0:T(8,128)(2,1)} %param.11) | copy-start | bytes 9437188
where the time goes:
time: 638 us; the launch traced here: 629 us
  waiting for transfers between devices  352 us (55%)
  local copies, waits for them, and re-layouts  161 us (25%)
  matrix products  45.9 us (7%)
  starting transfers between devices  43.2 us (7%)
  other arithmetic  16 us (3%)
  blocking collectives  9.67 us (2%)
    all_to_all x1, waiting for transfers between devices, shards(): lax.all_to_all(lax.all_to_all(send_dy.reshape(grid_rows), 'node', split_a...  86.8 us
    all_to_all x1, waiting for transfers between devices, shards(): lax.all_to_all(lax.all_to_all(send_x.reshape(grid_rows), 'node', split_ax...  82.7 us
    all_to_all x1, waiting for transfers between devices, shards(): lax.all_to_all(lax.all_to_all(input_grad.reshape(grid_rows), 'node', spli...  65.1 us
    all_to_all x1, waiting for transfers between devices, shards(): lax.all_to_all(input_grad.reshape(grid_rows), 'node', split_axis=0, conca...  49.8 us
    all_to_all x1, waiting for transfers between devices, shards(): lax.all_to_all(send_x.reshape(grid_rows), 'node', split_axis=0, concat_ax...  43.9 us
    all_to_all x1, waiting for transfers between devices, shards(): lax.all_to_all(send_dy.reshape(grid_rows), 'node', split_axis=0, concat_a...  23.5 us
    reshape x2, local copies, waits for them, and re-layouts, shards(): send_dy.reshape(grid_rows)  13.6 us
    reshape x2, local copies, waits for them, and re-layouts, shards(): send_x.reshape(grid_rows)  13.5 us
  transfers between devices with their start and end apart: 9, of which 6 were waited for; matrix products, arithmetic and copies ran while one was open for 22% of the time, Pallas kernels for 0%

commit v1 on v0

v1 whole, which is shorter than its diff:
```python
import functools

import jax
import jax.numpy as jnp
from jax import lax
from jax.experimental import pallas as pl
from jax.experimental.pallas import tpu as pltpu
from jax.sharding import PartitionSpec as P

F32 = jnp.float32
BF16 = jnp.bfloat16
NT = (((1,), (1,)), ((), ()))
TN = (((0,), (0,)), ((), ()))
LANES = 128
EXTRA = 16
TAIL = 8


def pad_to(value, unit):
    return -(-value // unit) * unit


class Rows:
    def __init__(self, cap):
        self.slots = 2 * cap
        self.base = self.slots // 16 * 16
        self.shift = self.slots - self.base
        self.group = pad_to(self.slots + self.shift + 1, 8)
        self.prob = 2 * self.slots
        self.message = max(pad_to(self.prob + 1, 8), self.base + self.group)


def iota(shape, dim):
    return lax.broadcasted_iota(jnp.int32, shape, dim)


def eye(rows):
    return jnp.where(iota((rows, LANES), 0) == iota((rows, LANES), 1), 1.0, 0.0).astype(BF16)


def ranks(info_ref, w_refs, first, targets):
    place = iota((EXTRA, LANES), 0) == info_ref[0]
    lines = []
    for j in range(targets):
        lane = pl.multiple_of(info_ref[1 + j] * LANES, LANES)
        parts = []
        for w in w_refs:
            part = w[first : first + EXTRA, pl.ds(lane, LANES)].astype(F32)
            parts.append(jnp.sum(jnp.where(place, part, 0.0), axis=0, keepdims=True))
        lines.append(jnp.concatenate(parts, axis=1))
    tokens = lines[0].shape[1]
    lines.append(jnp.zeros((pad_to(targets, 8) - targets, tokens), F32))
    probs = jnp.concatenate([line for line in lines if line.shape[0]], axis=0)
    named = probs != 0.0
    upto = jnp.where(iota((tokens, tokens), 0) <= iota((tokens, tokens), 1), 1.0, 0.0).astype(BF16)
    count = jnp.dot(jnp.where(named, 1.0, 0.0).astype(BF16), upto, preferred_element_type=F32)
    return probs, jnp.where(named, count, -999.0)


def pick(rank, j, rows, start=0):
    slot = (iota((rows, rank.shape[1]), 0) + (1 - start)).astype(F32)
    return jnp.where(slot == rank[j : j + 1, :], 1.0, 0.0).astype(BF16)


def pack_kernel(nodes, locals_, x_ref, dy_ref, ids_ref, probs_ref, out_ref):
    tokens, width = x_ref.shape
    out_ref[:tokens, :] = x_ref[...]
    out_ref[tokens : 2 * tokens, :] = dy_ref[...]
    place = iota((EXTRA, tokens), 0)
    for n in range(width // tokens):
        line = jnp.zeros((EXTRA, tokens), F32)
        if n < nodes:
            for k in range(ids_ref.shape[0]):
                hit = (place < locals_) & (ids_ref[k : k + 1, :] == place + n * locals_)
                line = line + jnp.where(hit, probs_ref[k : k + 1, :], 0.0)
        out_ref[2 * tokens :, n * tokens : (n + 1) * tokens] = line.astype(BF16)


def dispatch_kernel(at, targets, info_ref, mine_ref, sibling_ref, *outs):
    tokens = (mine_ref.shape[0] - EXTRA) // 2
    width = mine_ref.shape[1]
    blocks = (mine_ref, sibling_ref)
    probs, rank = ranks(info_ref, blocks, 2 * tokens, targets)
    picks, lines = [], []
    for j in range(targets):
        x = pick(rank, j, at.message)
        dy = pick(rank, j, at.message, at.slots)
        picks.append(
            jnp.concatenate([x[:, :tokens], dy[:, :tokens], x[:, tokens:], dy[:, tokens:]], axis=1)
        )
        lines.append(
            lax.dot_general(
                probs.astype(BF16), pick(rank, j, LANES), NT, preferred_element_type=F32
            )[j : j + 1, :]
        )
    picks = jnp.concatenate(picks, axis=0)
    step = next(s for s in (512, 256, 128) if width % s == 0)
    for start in range(0, width, step):
        rows = jnp.concatenate([b[: 2 * tokens, start : start + step] for b in blocks], axis=0)
        out = jnp.dot(picks, rows, preferred_element_type=F32)
        for j in range(targets):
            part = out[j * at.message : (j + 1) * at.message]
            if start == 0:
                line = jnp.concatenate([lines[j], jnp.zeros((1, step - LANES), F32)], axis=1)
                part = jnp.where(iota(part.shape, 0) == at.prob, line, part)
            outs[j][:, start : start + step] = part.astype(BF16)


def combine_kernel(at, targets, info_ref, mine_ref, sibling_ref, *refs):
    rets_ref, keep_ref, send_ref = refs
    chips = [info_ref[1 + j] // 2 for j in range(targets)]
    tokens = keep_ref.shape[0] - TAIL
    width = keep_ref.shape[1]
    _, rank = ranks(info_ref, (mine_ref, sibling_ref), 0, targets)
    picks = [pick(rank, j, at.group) for j in range(targets)]
    step = next(s for s in (512, 256, 128) if width % s == 0)
    for start in range(0, width, step):
        total = None
        for j in range(targets):
            part = lax.dot_general(
                picks[j], rets_ref[chips[j], :, start : start + step], TN, preferred_element_type=F32
            )
            total = part if total is None else total + part
        keep_ref[:tokens, start : start + step] = total[:tokens].astype(BF16)
        send_ref[:tokens, start : start + step] = total[tokens:].astype(BF16)
    row = iota((TAIL, LANES), 0)
    for n in range(width // LANES):
        keep = send = jnp.zeros((TAIL, LANES), F32)
        if n < targets:
            tail = rets_ref[chips[n], at.group - 8 :, :LANES]
            line = jnp.dot(tail, pick(rank, n, LANES), preferred_element_type=F32)[7:8]
            keep = jnp.where(row == 0, line[:, :tokens], keep)
            send = jnp.where(row == 1, line[:, tokens:], send)
        keep_ref[tokens:, n * LANES : (n + 1) * LANES] = keep.astype(BF16)
        send_ref[tokens:, n * LANES : (n + 1) * LANES] = send.astype(BF16)


def expert_kernel(at, sources, aliased, info_ref, *refs):
    msgs, refs = refs[:sources], refs[sources:]
    gate_ref, up_ref, down_t_ref, gate_t_ref, up_t_ref = refs[:5]
    refs = refs[5 + aliased :]
    ret_ref, x_all, dy_all, hp_ref, du_ref, dg_ref, p_ref, dx_ref, pg_ref, moved_ref = refs
    step = pl.program_id(0)
    rows, tile = hp_ref.shape
    group, shift = at.group, at.shift

    @pl.when(step == 0)
    def _():
        x_all[...] = jnp.concatenate([m[:group, :] for m in msgs], axis=0)
        dy_all[...] = jnp.concatenate([m[at.base : at.base + group, :] for m in msgs], axis=0)
        first = at.prob // 8 * 8
        for i, m in enumerate(msgs):
            p = lax.dot_general(
                eye(group), m[first : first + 8, :LANES], NT, preferred_element_type=F32
            )
            line = at.prob - first
            p_ref[i * group : (i + 1) * group, :] = p[:, line : line + 1] + jnp.zeros(
                (group, LANES), F32
            )

    x, dy = x_all[...], dy_all[...]
    p = p_ref[:, :1]
    g = jnp.dot(x, gate_ref[0], preferred_element_type=F32)
    u = jnp.dot(x, up_ref[0], preferred_element_type=F32)
    moved_ref[:rows, :] = jnp.dot(dy, down_t_ref[...], preferred_element_type=F32)
    moved_ref[rows:, :] = jnp.zeros((8, tile), F32)
    dh = moved_ref[shift : shift + rows, :]
    s = jax.nn.sigmoid(g)
    a = g * s
    h = a * u
    sd = dh * p
    pg = jnp.sum(dh * h, axis=1, keepdims=True)
    du = (sd * a).astype(BF16)
    dg = (sd * u * s * (1.0 + g * (1.0 - s))).astype(BF16)
    du_ref[...] = du
    dg_ref[...] = dg
    moved_ref[:8, :] = jnp.zeros((8, tile), F32)
    moved_ref[shift : shift + rows, :] = h * p
    hp_ref[...] = moved_ref[:rows, :].astype(BF16)
    dx = jnp.dot(dg, gate_t_ref[...], preferred_element_type=F32)
    dx = dx + jnp.dot(du, up_t_ref[...], preferred_element_type=F32)

    @pl.when(step == 0)
    def _():
        dx_ref[...] = dx
        pg_ref[...] = pg + jnp.zeros_like(pg_ref)

    @pl.when(step > 0)
    def _():
        dx_ref[...] += dx
        pg_ref[...] += pg

    @pl.when(step == pl.num_programs(0) - 1)
    def _():
        last = iota((8, LANES), 0) == 7
        for i in range(sources):
            chip = info_ref[1 + i] // 2
            part = slice(i * group, (i + 1) * group)
            line = lax.dot_general(
                pg_ref[part, :].astype(BF16), eye(group), TN, preferred_element_type=F32
            )[:1]
            ret_ref[chip] = dx_ref[part, :].astype(BF16)
            tail = jnp.where(last, line, dx_ref[(i + 1) * group - 8 : (i + 1) * group, :LANES])
            ret_ref[chip, group - 8 :, :LANES] = tail.astype(BF16)


def whole(shape):
    return pl.BlockSpec(shape, lambda *_: (0,) * len(shape), pipeline_mode=pl.Buffered(1))


def params(mib):
    return pltpu.CompilerParams(vmem_limit_bytes=mib * 1024 * 1024)


COST = pl.CostEstimate(flops=1024, bytes_accessed=1024, transcendentals=0)


SMEM = pl.BlockSpec(memory_space=pltpu.SMEM)


def call(kernel, info, operands, out_shape, in_specs=None):
    return pl.pallas_call(
        kernel,
        grid=(1,),
        in_specs=([SMEM] if info is not None else [])
        + (in_specs or [whole(a.shape) for a in operands]),
        out_specs=[whole(s.shape) for s in out_shape],
        out_shape=out_shape,
        compiler_params=params(20),
        cost_estimate=COST,
    )(*([info] if info is not None else []), *operands)


def pack(x, dy, ids_t, probs_t, nodes, locals_):
    tokens, width = x.shape
    shape = jax.ShapeDtypeStruct((2 * tokens + EXTRA, width), BF16)
    kernel = functools.partial(pack_kernel, nodes, locals_)
    return call(kernel, None, [x, dy, ids_t, probs_t], [shape])[0]


def dispatch(at, targets, info, mine, sibling):
    height, width = mine.shape
    shapes = [jax.ShapeDtypeStruct((at.message, width), BF16)] * targets
    kernel = functools.partial(dispatch_kernel, at, targets)
    return call(kernel, info, [mine, sibling], shapes)


def combine(at, info, mine, sibling, rets):
    height, width = mine.shape
    tokens = (height - EXTRA) // 2
    shapes = [jax.ShapeDtypeStruct((tokens + TAIL, width), BF16)] * 2
    kernel = functools.partial(combine_kernel, at, rets.shape[0])
    extra = pl.BlockSpec((EXTRA, width), lambda *_: (2 * tokens // EXTRA, 0))
    specs = [extra, extra, whole(rets.shape)]
    return call(kernel, info, [mine, sibling, rets], shapes, specs)


def expert(at, info, msgs, weights, saved, chunk, chunks):
    sources = len(msgs)
    width = msgs[0].shape[1]
    hidden = weights[0].shape[2]
    tile = next(t for t in (256, 128) if hidden % t == 0)
    rows = sources * at.group
    gate_spec = pl.BlockSpec((1, width, tile), lambda f: (0, 0, f))
    down_t_spec = pl.BlockSpec((width, tile), lambda f: (0, f))
    up_t_spec = pl.BlockSpec((tile, width), lambda f: (f, 0))
    wide_spec = pl.BlockSpec(
        (rows, width), lambda f: (chunk, 0), pipeline_mode=pl.Buffered(1)
    )
    thin_spec = pl.BlockSpec((rows, tile), lambda f: (chunk, f))
    out_shape = [jax.ShapeDtypeStruct((sources, at.group, width), BF16)]
    out_specs = [whole(s.shape) for s in out_shape] + [wide_spec] * 2 + [thin_spec] * 3
    out_shape += [jax.ShapeDtypeStruct((chunks * rows, width), BF16)] * 2
    out_shape += [jax.ShapeDtypeStruct((chunks * rows, hidden), BF16)] * 3
    in_specs = [SMEM] + [whole(m.shape) for m in msgs] + [gate_spec] * 2 + [down_t_spec] + [up_t_spec] * 2
    aliases = {}
    if saved:
        aliases = {len(in_specs) + i: 1 + i for i in range(5)}
        in_specs += [pl.BlockSpec(memory_space=pl.ANY)] * 5
    out = pl.pallas_call(
        functools.partial(expert_kernel, at, sources, len(saved)),
        grid=(hidden // tile,),
        in_specs=in_specs,
        out_specs=out_specs,
        out_shape=out_shape,
        input_output_aliases=aliases,
        scratch_shapes=[
            pltpu.VMEM((rows, LANES), F32),
            pltpu.VMEM((rows, width), F32),
            pltpu.VMEM((rows, LANES), F32),
            pltpu.VMEM((rows + 8, tile), F32),
        ],
        compiler_params=params(30),
        cost_estimate=COST,
    )(info, *msgs, *weights, *saved)
    return out[0], out[1:]


def shards(tokens_x, grad_out, expert_ids, probs, w_gate, w_up, w_down):
    nodes, locals_ = lax.axis_size("node"), lax.axis_size("local")
    experts = nodes * locals_
    tokens, top = expert_ids.shape
    width = tokens_x.shape[1]
    at = Rows(tokens * top // experts + 1)
    node, local = lax.axis_index("node"), lax.axis_index("local")
    both = ("node", "local")
    chips = list(range(0, nodes, 2))
    targets = len(chips)

    def swap(value, dn=0, dz=0):
        pairs = [
            (n * locals_ + z, (n ^ dn) * locals_ + (z ^ dz))
            for n in range(nodes)
            for z in range(locals_)
        ]
        return lax.ppermute(value, both, pairs)

    same_core = [list(range(core, nodes, 2)) for core in range(2)]

    def back(value):
        return lax.all_to_all(
            value, "node", split_axis=0, concat_axis=0, axis_index_groups=same_core, tiled=True
        )

    def fence(*values):
        return lax.optimization_barrier(values)

    ids_t = expert_ids.T
    info = jnp.concatenate([local[None], node ^ jnp.array(chips, jnp.int32)]).astype(jnp.int32)
    payload = pack(tokens_x, grad_out, ids_t, probs.T.astype(F32), nodes, locals_)

    def sisters(block):
        return swap(block, 1)

    def fill(block, sister):
        return dispatch(at, targets, info, block, sister)

    def send(msgs):
        return [msgs[0]] + [swap(msgs[j], chips[j]) for j in range(1, targets)]

    def turn(token):
        down, gate, up, _ = fence(w_down, w_gate, w_up, token)
        return [w_gate, w_up, down[0].T, gate[0].T, up[0].T]

    def work(c, msgs, weights, saved):
        return expert(at, info, msgs, weights, saved, c, locals_)

    def merge(block, sister, ret):
        return combine(at, info, block, sister, ret)

    (go,) = fence(node < nodes)

    def at_once(step, *args):
        shapes = jax.eval_shape(step, *args)
        idle = lambda *_: jax.tree.map(lambda v: jnp.zeros(v.shape, v.dtype), shapes)
        return lax.cond(go, step, idle, *args)

    def prepare(block):
        def step(block):
            sister = sisters(block)
            return sister, fill(block, sister)

        return at_once(step, block)

    def home(parts):
        def step(keep, other):
            return (keep.astype(F32) + swap(other, 1).astype(F32)).astype(BF16)

        return at_once(step, *parts)

    def wgrad(a, b):
        return lax.dot_general(a, b, TN, preferred_element_type=F32).astype(BF16)

    if locals_ == 4:
        b0 = payload
        b1, b2 = swap(b0, 0, 1), swap(b0, 0, 2)
        s0, m0 = prepare(b0)
        p0 = send(m0)
        weights = turn(m0[0])
        b1, weights = fence(b1, weights)
        s1, m1 = prepare(b1)
        p0, m1 = fence(p0, m1)
        p1 = send(m1)
        s2, m2 = prepare(b2)
        p0, m2 = fence(p0, m2)
        r0, saved = work(0, p0, weights, ())
        p1, m2, b2, r0, saved = fence(p1, m2, b2, r0, saved)
        p2 = send(m2)
        b3 = swap(b2, 0, 1)
        r1, saved = work(1, p1, weights, saved)
        b3, r1 = fence(b3, r1)
        s3, m3 = prepare(b3)
        p2, m3, r1, saved = fence(p2, m3, r1, saved)
        p3 = send(m3)
        r1 = back(r1)
        r2, saved = work(2, p2, weights, saved)
        p3, r1, r2, saved = fence(p3, r1, r2, saved)
        r2 = back(r2)
        r3, saved = work(3, p3, weights, saved)
        r2, r3, r1, saved, r0 = fence(r2, r3, r1, saved, r0)
        t2 = home(merge(b2, s2, r2))
        t2, r3, r1, saved, r0 = fence(t2, r3, r1, saved, r0)
        r3 = back(r3)
        t2 = swap(t2, 0, 2)
        x_all, dy_all, hp, du, dg = saved
        t1 = home(merge(b1, s1, r1))
        gate_wgrad = wgrad(x_all, dg)
        r3, t1, r0, gate_wgrad = fence(r3, t1, r0, gate_wgrad)
        t3 = home(merge(b3, s3, r3))
        t3, r0, t1, x_all, dy_all, hp, du = fence(t3, r0, t1, x_all, dy_all, hp, du)
        t1 = swap(t1, 0, 1)
        t3 = swap(t3, 0, 3)
        r0 = back(r0)
        up_wgrad = wgrad(x_all, du)
        down_wgrad = wgrad(hp, dy_all)
        r0, up_wgrad, down_wgrad = fence(r0, up_wgrad, down_wgrad)
        t0 = home(merge(b0, s0, r0))
        t0, t1, t2, t3 = fence(t0, t1, t2, t3)
        totals = [t0, t1, t2, t3]
    else:
        weights, saved, totals = turn(payload), (), []
        for c in range(locals_):
            block = swap(payload, 0, c) if c else payload
            sister, msgs = prepare(block)
            ret, saved = work(c, send(msgs), weights, saved)
            total = home(merge(block, sister, back(ret)))
            totals.append(swap(total, 0, c) if c else total)
        x_all, dy_all, hp, du, dg = saved
        gate_wgrad, up_wgrad = wgrad(x_all, dg), wgrad(x_all, du)
        down_wgrad = wgrad(hp, dy_all)

    total = functools.reduce(
        lambda a, b: a + b, [totals[c][:tokens].astype(F32) for c in range(locals_)]
    )
    grad_x = total.astype(BF16)
    tails = jnp.stack([totals[c][tokens : tokens + 2, : targets * LANES] for c in range(locals_)])
    tails = tails.reshape(locals_, 2, targets, tokens)
    apart = ids_t ^ (node * locals_ + local)
    grad_probs = jnp.zeros((top, tokens), F32)
    for c in range(locals_):
        for dl in range(2):
            for j in range(targets):
                name = (chips[j] + dl) * locals_ + c
                grad_probs = jnp.where(apart == name, tails[c, dl, j].astype(F32)[None], grad_probs)
    grad_probs = grad_probs.T.astype(BF16)
    return (grad_x, grad_probs, gate_wgrad[None], up_wgrad[None], down_wgrad[None])


def solution(mesh):
    row, cube = P(("node", "local"), None), P(("node", "local"), None, None)
    return jax.shard_map(
        shards,
        mesh=mesh,
        in_specs=(row, row, row, row, cube, cube, cube),
        out_specs=(row, row, cube, cube, cube),
        check_vma=False,
    )
```

time: 638 us -> 285 us (0.45); the launches traced: 629 us -> 283 us
  waiting for transfers between devices: 352 us -> 59.7 us
  local copies, waits for them, and re-layouts: 161 us -> 64.8 us
  Pallas kernels: 0 us -> 86.1 us
  matrix products: 45.9 us -> 24.2 us
  other arithmetic: 16 us -> 6.11 us
  blocking collectives: 9.67 us -> 0 us
    all_to_all x9 -> x4, waiting for transfers between devices: 352 us -> 0.01 us  [back(): lax.all_to_all(value, 'node', split_axis=0, concat_axis=0, axis_index_gro...]
    pallas_call x0 -> x13, Pallas kernels: none -> 86.1 us  [the longest x4 56.2 us: expert(): pl.pallas_call(functools.partial(expert_kernel, at, sources, len(saved)),...]
    ppermute x0 -> x26, waiting for transfers between devices: none -> 59.7 us  [swap(): return lax.ppermute(value, both, pairs)]
    reshape x13 -> x0, local copies, waits for them, and re-layouts: 57.9 us -> none  [the longest x2 13.6 us: shards(): send_dy.reshape(grid_rows)]
    gather x5 -> x0, local copies, waits for them, and re-layouts: 49 us -> none  [the longest x1 12 us: shards(): token_parts = back_x[target].reshape(tok_count, top_count, width)]
    unnamed x45 -> x90, local copies, waits for them, and re-layouts: 3.98 us -> 50.4 us
    all_to_all x9 -> x0, local copies, waits for them, and re-layouts: 40.9 us -> none  [the longest x1 7.04 us: shards(): lax.all_to_all(lax.all_to_all(input_grad.reshape(grid_rows), 'node', spli...]
    all_to_all x9 -> x4, starting transfers between devices: 43.2 us -> 16.9 us  [back(): lax.all_to_all(value, 'node', split_axis=0, concat_axis=0, axis_index_gro...]
  transfers between devices with their start and end apart: 9 -> 30, of which waited for: 6 -> 12; matrix products, arithmetic and copies ran while one was open for 22% -> 13% of each run, Pallas kernels for 0% -> 29%
where the time goes in v1:
time: 285 us; the launch traced here: 283 us
  Pallas kernels  86.1 us (30%)
  local copies, waits for them, and re-layouts  64.8 us (23%)
  waiting for transfers between devices  59.7 us (21%)
  starting transfers between devices  41.5 us (15%)
  matrix products  24.2 us (8%)
  other arithmetic  6.11 us (2%)
    ppermute x26, waiting for transfers between devices, swap(): return lax.ppermute(value, both, pairs)  59.7 us
    pallas_call x4, Pallas kernels, expert(): pl.pallas_call(functools.partial(expert_kernel, at, sources, len(saved)),...  56.2 us
    unnamed x90, local copies, waits for them, and re-layouts  50.4 us
    pallas_call x9, Pallas kernels, call(): pl.pallas_call(kernel, grid=(1,), in_specs=([SMEM] if info is not None el...  29.9 us
    ppermute x26, starting transfers between devices, swap(): return lax.ppermute(value, both, pairs)  24.6 us
    dot_general x3, matrix products, wgrad(): return lax.dot_general(a, b, TN, preferred_element_type=F32).astype(BF16)  24.2 us
    all_to_all x4, starting transfers between devices, back(): lax.all_to_all(value, 'node', split_axis=0, concat_axis=0, axis_index_gro...  16.9 us
    optimization_barrier x3, local copies, waits for them, and re-layouts, fence(): return lax.optimization_barrier(values)  12.3 us
  transfers between devices with their start and end apart: 30, of which 12 were waited for; matrix products, arithmetic and copies ran while one was open for 13% of the time, Pallas kernels for 29%

profile of v1, /device:TPU:0, one launch (start us, length us, event | category | flops | bytes accessed | tf_op | source)
XLA Modules:
  0.0 283.4 jit_solution(13249220169362376027)
XLA Ops:
  5.2 3.0 %collective-permute-start.11 = (bf16[272,2048]{1,0:T(8,128)(2,1)}, bf16[272,2048]{1,0:T(8,128)(2,1)}, u32[]{:S(2)}, u32[]{:S(2)}) collective-permute-start(bf16[272,2048]{1,0:T(8,128)(2,1)} %shard_map.119.mine_ref), channel_id=1, source_target_pairs={{0,1},{1,0},{2,3},{3,2},{4,5},{5,4},{6,7},{7,6},{8,9},{9,8},{10,11... | collective-permute-start | bytes 3342344 | tf_op jit(solution)/shard_map/ppermute | solution.py:316
  8.2 2.6 collective-permute-start.15
  10.9 7.5 %conditional.8 = (bf16[272,2048]{1,0:T(8,128)(2,1)}, bf16[136,2048]{1,0:T(8,128)(2,1)}, bf16[136,2048]{1,0:T(8,128)(2,1)}, bf16[136,2048]{1,0:T(8,128)(2,1)}, bf16[136,2048]{1,0:T(8,128)(2,1)}) conditional(s32[]{:T(128)} %convert_element_type.398, () %tuple.75, (bf16[272,2048]{1,0:T(8,128)(2,1)}, s32[5]{0:T(128)S(1)}) %tuple.76), branch_computations={%region_0.0_spmd, %region_1.0_spmd} | conditional | flops 1024 | bytes 4457552 | solution.py:356
  10.9 3.1 %collective-permute-done.sibling_ref = bf16[272,2048]{1,0:T(8,128)(2,1)} collective-permute-done((bf16[272,2048]{1,0:T(8,128)(2,1)}, bf16[272,2048]{1,0:T(8,128)(2,1)}, u32[]{:S(2)}, u32[]{:S(2)}) %collective-permute-start) | collective-permute-done | bytes 1114144 | tf_op jit(solution)/shard_map/cond/branch_1_fun/ppermute | solution.py:316
  14.0 4.4 %branch_1_fun.4 = (bf16[136,2048]{1,0:T(8,128)(2,1)}, bf16[136,2048]{1,0:T(8,128)(2,1)}, bf16[136,2048]{1,0:T(8,128)(2,1)}, bf16[136,2048]{1,0:T(8,128)(2,1)}) custom-call(s32[5]{0:T(128)S(1)} %get-tuple-element.42.info_ref, bf16[272,2048]{1,0:T(8,128)(2,1)} %get-tuple-element.40.mine_ref, bf16[272,2048]{1,0:T(8,128)(2,1)} %collective-permute-done.sibling_ref), custom_call_target="tpu_custom_call" | custom-call | flops 1024 | bytes 1024 | tf_op jit(solution)/shard_map/cond/branch_1_fun/pallas_call | solution.py:222
  21.9 4.8 %copy.28 = bf16[1,768,2048]{1,2,0:T(8,128)(2,1)} copy(bf16[1,768,2048]{2,1,0:T(8,128)(2,1)} %param.30) | data formatting | bytes 6291456 | tf_op jit(solution)/shard_map/optimization_barrier | solution.py:326
  26.7 2.9 %copy.29 = bf16[1,2048,768]{1,2,0:T(8,128)(2,1)} copy(bf16[1,2048,768]{2,1,0:T(8,128)(2,1)S(1)} %copy-done) | data formatting | bytes 6291456 | tf_op jit(solution)/shard_map/optimization_barrier | solution.py:326
  29.5 4.6 %copy.30 = bf16[1,2048,768]{1,2,0:T(8,128)(2,1)} copy(bf16[1,2048,768]{2,1,0:T(8,128)(2,1)} %refs_5_.3) | data formatting | bytes 6291456 | tf_op jit(solution)/shard_map/optimization_barrier | solution.py:326
  34.1 22.7 %collective-permute-done.11.mine_ref = bf16[272,2048]{1,0:T(8,128)(2,1)} collective-permute-done((bf16[272,2048]{1,0:T(8,128)(2,1)}, bf16[272,2048]{1,0:T(8,128)(2,1)}, u32[]{:S(2)}, u32[]{:S(2)}) %collective-permute-start.11) | collective-permute-done | bytes 1114144 | tf_op jit(solution)/shard_map/ppermute | solution.py:316
  56.9 7.5 %conditional.9 = (bf16[272,2048]{1,0:T(8,128)(2,1)}, bf16[136,2048]{1,0:T(8,128)(2,1)}, bf16[136,2048]{1,0:T(8,128)(2,1)}, bf16[136,2048]{1,0:T(8,128)(2,1)}, bf16[136,2048]{1,0:T(8,128)(2,1)}) conditional(s32[]{:T(128)} %convert_element_type.398, () %tuple.78, (bf16[272,2048]{1,0:T(8,128)(2,1)}, s32[5]{0:T(128)S(1)}) %tuple.81), branch_computations={%region_2.0_spmd, %region_3.0_spmd} | conditional | flops 1024 | bytes 4457552 | solution.py:356
  56.9 3.1 %collective-permute-done.1.sibling_ref = bf16[272,2048]{1,0:T(8,128)(2,1)} collective-permute-done((bf16[272,2048]{1,0:T(8,128)(2,1)}, bf16[272,2048]{1,0:T(8,128)(2,1)}, u32[]{:S(2)}, u32[]{:S(2)}) %collective-permute-start.1) | collective-permute-done | bytes 1114144 | tf_op jit(solution)/shard_map/cond/branch_1_fun/ppermute | solution.py:316
  60.0 4.4 %branch_1_fun.5 = (bf16[136,2048]{1,0:T(8,128)(2,1)}, bf16[136,2048]{1,0:T(8,128)(2,1)}, bf16[136,2048]{1,0:T(8,128)(2,1)}, bf16[136,2048]{1,0:T(8,128)(2,1)}) custom-call(s32[5]{0:T(128)S(1)} %get-tuple-element.51.info_ref, bf16[272,2048]{1,0:T(8,128)(2,1)} %get-tuple-element.50.mine_ref, bf16[272,2048]{1,0:T(8,128)(2,1)} %collective-permute-done.1.sibling_ref), custom_call_target="tpu_custom_call" | custom-call | flops 1024 | bytes 1024 | tf_op jit(solution)/shard_map/cond/branch_1_fun/pallas_call | solution.py:222
  68.0 7.6 %conditional.10 = (bf16[272,2048]{1,0:T(8,128)(2,1)}, bf16[136,2048]{1,0:T(8,128)(2,1)}, bf16[136,2048]{1,0:T(8,128)(2,1)}, bf16[136,2048]{1,0:T(8,128)(2,1)}, bf16[136,2048]{1,0:T(8,128)(2,1)}) conditional(s32[]{:T(128)} %convert_element_type.398, () %tuple.83, (bf16[272,2048]{1,0:T(8,128)(2,1)}, s32[5]{0:T(128)S(1)}) %tuple.84), branch_computations={%region_4.0_spmd, %region_5.0_spmd} | conditional | flops 1024 | bytes 4457552 | solution.py:356
  68.0 3.1 %collective-permute-done.2.sibling_ref = bf16[272,2048]{1,0:T(8,128)(2,1)} collective-permute-done((bf16[272,2048]{1,0:T(8,128)(2,1)}, bf16[272,2048]{1,0:T(8,128)(2,1)}, u32[]{:S(2)}, u32[]{:S(2)}) %collective-permute-start.2) | collective-permute-done | bytes 1114144 | tf_op jit(solution)/shard_map/cond/branch_1_fun/ppermute | solution.py:316
  71.1 4.5 %branch_1_fun.6 = (bf16[136,2048]{1,0:T(8,128)(2,1)}, bf16[136,2048]{1,0:T(8,128)(2,1)}, bf16[136,2048]{1,0:T(8,128)(2,1)}, bf16[136,2048]{1,0:T(8,128)(2,1)}) custom-call(s32[5]{0:T(128)S(1)} %get-tuple-element.57.info_ref, bf16[272,2048]{1,0:T(8,128)(2,1)} %get-tuple-element.56.mine_ref, bf16[272,2048]{1,0:T(8,128)(2,1)} %collective-permute-done.2.sibling_ref), custom_call_target="tpu_custom_call" | custom-call | flops 1024 | bytes 1024 | tf_op jit(solution)/shard_map/cond/branch_1_fun/pallas_call | solution.py:222
  75.5 1.9 copy-done.1
  77.4 1.9 copy-done.4
  79.3 1.9 copy-done.7
  83.1 14.1 %shard_map.120 = (bf16[4,72,2048]{2,1,0:T(8,128)(2,1)S(1)}, bf16[1152,2048]{1,0:T(8,128)(2,1)}, bf16[1152,2048]{1,0:T(8,128)(2,1)}, bf16[1152,768]{1,0:T(8,128)(...) custom-call(s32[5]{0:T(128)S(1)} %pad_add_fusion.info_ref, ...), custom_call_target="tpu_custom_call" | custom-call | flops 1024 | bytes 1024 | tf_op jit(solution)/shard_map/pallas_call | solution.py:280
  101.8 14.0 %shard_map.121 = (bf16[4,72,2048]{2,1,0:T(8,128)(2,1)S(1)}, bf16[1152,2048]{1,0:T(8,128)(2,1)}, bf16[1152,2048]{1,0:T(8,128)(2,1)}, bf16[1152,768]{1,0:T(8,128)(...) custom-call(s32[5]{0:T(128)S(1)} %pad_add_fusion.info_ref, ...), custom_call_target="tpu_custom_call", output_to_operand_aliasing={{1}: (10, {}), {2}: (11, {}), {3}: (12, {}), {4}: (13, {}),... | custom-call | flops 1024 | bytes 1024 | tf_op jit(solution)/shard_map/pallas_call | solution.py:280
  116.9 8.3 %collective-permute-done.16.mine_ref = bf16[272,2048]{1,0:T(8,128)(2,1)} collective-permute-done((bf16[272,2048]{1,0:T(8,128)(2,1)}, bf16[272,2048]{1,0:T(8,128)(2,1)}, u32[]{:S(2)}, u32[]{:S(2)}) %collective-permute-start.16) | collective-permute-done | bytes 1114144 | tf_op jit(solution)/shard_map/ppermute | solution.py:316
  125.2 7.6 %conditional.11 = (bf16[272,2048]{1,0:T(8,128)(2,1)}, bf16[136,2048]{1,0:T(8,128)(2,1)}, bf16[136,2048]{1,0:T(8,128)(2,1)}, bf16[136,2048]{1,0:T(8,128)(2,1)}, bf16[136,2048]{1,0:T(8,128)(2,1)}) conditional(s32[]{:T(128)} %convert_element_type.398, () %tuple.88, (bf16[272,2048]{1,0:T(8,128)(2,1)}, s32[5]{0:T(128)S(1)}) %tuple.89), branch_computations={%region_6.0_spmd, %region_7.0_spmd} | conditional | flops 1024 | bytes 4457552 | solution.py:356
  125.3 3.1 %collective-permute-done.3.sibling_ref = bf16[272,2048]{1,0:T(8,128)(2,1)} collective-permute-done((bf16[272,2048]{1,0:T(8,128)(2,1)}, bf16[272,2048]{1,0:T(8,128)(2,1)}, u32[]{:S(2)}, u32[]{:S(2)}) %collective-permute-start.3) | collective-permute-done | bytes 1114144 | tf_op jit(solution)/shard_map/cond/branch_1_fun/ppermute | solution.py:316
  128.4 4.4 %branch_1_fun.7 = (bf16[136,2048]{1,0:T(8,128)(2,1)}, bf16[136,2048]{1,0:T(8,128)(2,1)}, bf16[136,2048]{1,0:T(8,128)(2,1)}, bf16[136,2048]{1,0:T(8,128)(2,1)}) custom-call(s32[5]{0:T(128)S(1)} %get-tuple-element.63.info_ref, bf16[272,2048]{1,0:T(8,128)(2,1)} %get-tuple-element.62.mine_ref, bf16[272,2048]{1,0:T(8,128)(2,1)} %collective-permute-done.3.sibling_ref), custom_call_target="tpu_custom_call" | custom-call | flops 1024 | bytes 1024 | tf_op jit(solution)/shard_map/cond/branch_1_fun/pallas_call | solution.py:222
  132.8 4.3 %all-to-all-start = ((bf16[4,72,2048]{2,1,0:T(8,128)(2,1)}), bf16[4,72,2048]{2,1,0:T(8,128)(2,1)}, u32[]{:S(2)}, u32[]{:S(2)}) async-start(bf16[4,72,2048]{2,1,0:T(8,128)(2,1)} %copy-done.32), calls=%async_computation | async-start | bytes 2359296 | tf_op jit(solution)/shard_map/all_to_all | solution.py:321
  137.1 2.0 collective-permute-start.20
  152.6 14.2 %shard_map.122 = (bf16[4,72,2048]{2,1,0:T(8,128)(2,1)S(1)}, bf16[1152,2048]{1,0:T(8,128)(2,1)}, bf16[1152,2048]{1,0:T(8,128)(2,1)}, bf16[1152,768]{1,0:T(8,128)(...) custom-call(s32[5]{0:T(128)S(1)} %pad_add_fusion.info_ref, ...), custom_call_target="tpu_custom_call", output_to_operand_aliasing={{1}: (10, {}), {2}: (11, {}), {3}: (12, {}), {4}: (13, {}),... | custom-call | flops 1024 | bytes 1024 | tf_op jit(solution)/shard_map/pallas_call | solution.py:280
  173.2 4.2 %collective-permute-done.22.refs_3_ = bf16[136,2048]{1,0:T(8,128)(2,1)S(1)} collective-permute-done((bf16[136,2048]{1,0:T(8,128)(2,1)}, bf16[136,2048]{1,0:T(8,128)(2,1)S(1)}, u32[]{:S(2)}, u32[]{:S(2)}) %collective-permute-start.22) | collective-permute-done | bytes 557088 | tf_op jit(solution)/shard_map/ppermute | solution.py:316
  178.3 4.3 %all-to-all-start.1 = ((bf16[4,72,2048]{2,1,0:T(8,128)(2,1)}), bf16[4,72,2048]{2,1,0:T(8,128)(2,1)}, u32[]{:S(2)}, u32[]{:S(2)}) async-start(bf16[4,72,2048]{2,1,0:T(8,128)(2,1)} %copy-done.33), calls=%async_computation.1 | async-start | bytes 2359296 | tf_op jit(solution)/shard_map/all_to_all | solution.py:321
  197.7 14.0 %shard_map.123 = (bf16[4,72,2048]{2,1,0:T(8,128)(2,1)}, bf16[1152,2048]{1,0:T(8,128)(2,1)}, bf16[1152,2048]{1,0:T(8,128)(2,1)}, bf16[1152,768]{1,0:T(8,128)(2,1)...) custom-call(s32[5]{0:T(128)S(1)} %pad_add_fusion.info_ref, ...), custom_call_target="tpu_custom_call", output_to_operand_aliasing={{1}: (10, {}), {2}: (11, {}), {3}: (12, {}), {4}: (13, {}),... | custom-call | flops 1024 | bytes 1024 | tf_op jit(solution)/shard_map/pallas_call | solution.py:280
  215.3 2.8 shard_map.124
  218.1 3.0 %conditional.12 = (bf16[136,2048]{1,0:T(8,128)(2,1)}) conditional(s32[]{:T(128)} %convert_element_type.398, () %tuple.90, (bf16[136,2048]{1,0:T(8,128)(2,1)S(1)}, bf16[136,2048]{1,0:T(8,128)(2,1)S(1)}) %shard_map.124), branch_computations={%region_8.0_spmd, %region_9.0_spmd} | conditional | flops 1114112 | bytes 3899440 | solution.py:356
  218.2 1.9 collective-permute-done.4
  221.2 4.2 %all-to-all-start.2 = ((bf16[4,72,2048]{2,1,0:T(8,128)(2,1)}), bf16[4,72,2048]{2,1,0:T(8,128)(2,1)S(1)}, u32[]{:S(2)}, u32[]{:S(2)}) async-start(bf16[4,72,2048]{2,1,0:T(8,128)(2,1)} %get-tuple-element.347), calls=%async_computation.2 | async-start | bytes 2359296 | tf_op jit(solution)/shard_map/all_to_all | solution.py:321
  226.8 3.6 %shard_map.125 = (bf16[136,2048]{1,0:T(8,128)(2,1)S(1)}, bf16[136,2048]{1,0:T(8,128)(2,1)}) custom-call(s32[5]{0:T(128)S(1)} %pad_add_fusion.info_ref, bf16[272,2048]{1,0:T(8,128)(2,1)} %collective-permute-done.11.mine_ref, bf16[272,2048]{1,0:T(8,128)(2,1)} %get-tuple-element.348.sibling_ref, bf16[4,72,2048]{2,1,0:T(8,128)(2,1)} %all-to-all-done.refs_0_), custom_call_target="tpu_custom_call" | custom-call | flops 1024 | bytes 1024 | tf_op jit(solution)/shard_map/pallas_call | solution.py:222
  230.4 3.1 %conditional.13 = (bf16[136,2048]{1,0:T(8,128)(2,1)}) conditional(s32[]{:T(128)} %convert_element_type.398, () %tuple.95, (bf16[136,2048]{1,0:T(8,128)(2,1)S(1)}, bf16[136,2048]{1,0:T(8,128)(2,1)}) %shard_map.125), branch_computations={%region_10.0_spmd, %region_11.0_spmd} | conditional | flops 1114112 | bytes 3899440 | solution.py:356
  230.4 2.2 collective-permute-done.5
  233.5 8.1 %convolution_convert_fusion.2 = bf16[2048,768]{1,0:T(8,128)(2,1)} fusion(bf16[1152,2048]{1,0:T(8,128)(2,1)} %get-tuple-element.360, bf16[1152,768]{1,0:T(8,128)(2,1)S(1)} %copy-done.30), kind=kOutput, calls=%fused_computation.6 | convolution fusion | flops 3625451520 | bytes 9633792 | tf_op jit(solution)/shard_map/dot_general | solution.py:372
  241.6 2.3 shard_map.126
  244.0 2.2 conditional.14
  246.2 4.2 %all-to-all-start.3 = ((bf16[4,72,2048]{2,1,0:T(8,128)(2,1)}), bf16[4,72,2048]{2,1,0:T(8,128)(2,1)S(1)}, u32[]{:S(2)}, u32[]{:S(2)}) async-start(bf16[4,72,2048]{2,1,0:T(8,128)(2,1)} %copy-done.31), calls=%async_computation.3 | async-start | bytes 2359296 | tf_op jit(solution)/shard_map/all_to_all | solution.py:321
  253.3 8.1 %convolution_convert_fusion.1 = bf16[2048,768]{1,0:T(8,128)(2,1)} fusion(bf16[1152,2048]{1,0:T(8,128)(2,1)} %get-tuple-element.360, bf16[1152,768]{1,0:T(8,128)(2,1)S(1)} %copy-done.24), kind=kOutput, calls=%fused_computation.5 | convolution fusion | flops 3625451520 | bytes 9633792 | tf_op jit(solution)/shard_map/dot_general | solution.py:372
  261.4 8.0 %convolution_convert_fusion = bf16[768,2048]{1,0:T(8,128)(2,1)} fusion(bf16[1152,768]{1,0:T(8,128)(2,1)S(1)} %copy-done.18, bf16[1152,2048]{1,0:T(8,128)(2,1)} %get-tuple-element.363), kind=kOutput, calls=%fused_computation.4 | convolution fusion | flops 3625451520 | bytes 9633792 | tf_op jit(solution)/shard_map/dot_general | solution.py:372
  269.4 2.3 shard_map.127
  271.7 2.2 conditional.15
  271.8 1.9 collective-permute-done.7
  273.9 4.1 %collective-permute-done.25 = bf16[136,2048]{1,0:T(8,128)(2,1)} collective-permute-done((bf16[136,2048]{1,0:T(8,128)(2,1)S(1)}, bf16[136,2048]{1,0:T(8,128)(2,1)}, u32[]{:S(2)}, u32[]{:S(2)}) %collective-permute-start.25) | collective-permute-done | bytes 557088 | tf_op jit(solution)/shard_map/ppermute | solution.py:316
  279.4 2.5 add_convert_fusion.4
  (148 shorter events, 70.6 us)
Async XLA Ops:
  5.2 51.6 %collective-permute-start.11 = (bf16[272,2048]{1,0:T(8,128)(2,1)}, bf16[272,2048]{1,0:T(8,128)(2,1)}, u32[]{:S(2)}, u32[]{:S(2)}) collective-permute-start(bf16[272,2048]{1,0:T(8,128)(2,1)} %shard_map.119.mine_ref), channel_id=1, source_target_pairs={{0,1},{1,0},{2,3},{3,2},{4,5},{5,4},{6,7},{7,6},{8,9},{9,8},{10,11... | collective-permute-start | bytes 3342344 | tf_op jit(solution)/shard_map/ppermute | solution.py:316
  8.2 59.7 %collective-permute-start.15 = (bf16[272,2048]{1,0:T(8,128)(2,1)}, bf16[272,2048]{1,0:T(8,128)(2,1)}, u32[]{:S(2)}, u32[]{:S(2)}) collective-permute-start(bf16[272,2048]{1,0:T(8,128)(2,1)} %shard_map.119.mine_ref), channel_id=1, source_target_pairs={{0,2},{1,3},{2,0},{3,1},{4,6},{5,7},{6,4},{7,5},{8,10},{9,11},{10,... | collective-permute-start | bytes 3342344 | tf_op jit(solution)/shard_map/ppermute | solution.py:316
  10.9 3.1 %collective-permute-start = (bf16[272,2048]{1,0:T(8,128)(2,1)}, bf16[272,2048]{1,0:T(8,128)(2,1)}, u32[]{:S(2)}, u32[]{:S(2)}) collective-permute-start(bf16[272,2048]{1,0:T(8,128)(2,1)} %get-tuple-element.40.mine_ref), channel_id=1, source_target_pairs={{0,4},{1,5},{2,6},{3,7},{4,0},{5,1},{6,2},{7,3},{8,12},{9,13},{10,... | collective-permute-start | bytes 3342344 | tf_op jit(solution)/shard_map/cond/branch_1_fun/ppermute | solution.py:316
  18.4 46.0 %collective-permute-start.8 = (bf16[136,2048]{1,0:T(8,128)(2,1)}, bf16[136,2048]{1,0:T(8,128)(2,1)}, u32[]{:S(2)}, u32[]{:S(2)}) collective-permute-start(bf16[136,2048]{1,0:T(8,128)(2,1)} %get-tuple-element.230), channel_id=1, source_target_pairs={{0,8},{1,9},{2,10},{3,11},{4,12},{5,13},{6,14},{7,15},{8,0},{9,1},... | collective-permute-start | bytes 1671176 | tf_op jit(solution)/shard_map/ppermute | solution.py:316
  19.9 44.5 %collective-permute-start.9 = (bf16[136,2048]{1,0:T(8,128)(2,1)}, bf16[136,2048]{1,0:T(8,128)(2,1)}, u32[]{:S(2)}, u32[]{:S(2)}) collective-permute-start(bf16[136,2048]{1,0:T(8,128)(2,1)} %get-tuple-element.231), channel_id=1, source_target_pairs={{0,16},{1,17},{2,18},{3,19},{4,20},{5,21},{6,22},{7,23},{8,24},{9,... | collective-permute-start | bytes 1671176 | tf_op jit(solution)/shard_map/ppermute | solution.py:316
  21.4 43.0 %collective-permute-start.10 = (bf16[136,2048]{1,0:T(8,128)(2,1)}, bf16[136,2048]{1,0:T(8,128)(2,1)}, u32[]{:S(2)}, u32[]{:S(2)}) collective-permute-start(bf16[136,2048]{1,0:T(8,128)(2,1)} %get-tuple-element.232), channel_id=1, source_target_pairs={{0,24},{1,25},{2,26},{3,27},{4,28},{5,29},{6,30},{7,31},{8,16},{9,... | collective-permute-start | bytes 1671176 | tf_op jit(solution)/shard_map/ppermute | solution.py:316
  21.9 4.8 %copy-start = (bf16[1,2048,768]{2,1,0:T(8,128)(2,1)S(1)}, bf16[1,2048,768]{2,1,0:T(8,128)(2,1)}, u32[]{:S(2)}) copy-start(bf16[1,2048,768]{2,1,0:T(8,128)(2,1)} %refs_4_.3) | copy-start | bytes 9437188
  56.9 3.1 %collective-permute-start.1 = (bf16[272,2048]{1,0:T(8,128)(2,1)}, bf16[272,2048]{1,0:T(8,128)(2,1)}, u32[]{:S(2)}, u32[]{:S(2)}) collective-permute-start(bf16[272,2048]{1,0:T(8,128)(2,1)} %get-tuple-element.50.mine_ref), channel_id=1, source_target_pairs={{0,4},{1,5},{2,6},{3,7},{4,0},{5,1},{6,2},{7,3},{8,12},{9,13},{10,... | collective-permute-start | bytes 3342344 | tf_op jit(solution)/shard_map/cond/branch_1_fun/ppermute | solution.py:316
  64.4 33.8 %collective-permute-start.12 = (bf16[136,2048]{1,0:T(8,128)(2,1)}, bf16[136,2048]{1,0:T(8,128)(2,1)}, u32[]{:S(2)}, u32[]{:S(2)}) collective-permute-start(bf16[136,2048]{1,0:T(8,128)(2,1)} %get-tuple-element.242), channel_id=1, source_target_pairs={{0,8},{1,9},{2,10},{3,11},{4,12},{5,13},{6,14},{7,15},{8,0},{9,1},... | collective-permute-start | bytes 1671176 | tf_op jit(solution)/shard_map/ppermute | solution.py:316
  66.1 32.1 %collective-permute-start.13 = (bf16[136,2048]{1,0:T(8,128)(2,1)}, bf16[136,2048]{1,0:T(8,128)(2,1)}, u32[]{:S(2)}, u32[]{:S(2)}) collective-permute-start(bf16[136,2048]{1,0:T(8,128)(2,1)} %get-tuple-element.243), channel_id=1, source_target_pairs={{0,16},{1,17},{2,18},{3,19},{4,20},{5,21},{6,22},{7,23},{8,24},{9,... | collective-permute-start | bytes 1671176 | tf_op jit(solution)/shard_map/ppermute | solution.py:316
  67.7 30.6 %collective-permute-start.14 = (bf16[136,2048]{1,0:T(8,128)(2,1)}, bf16[136,2048]{1,0:T(8,128)(2,1)}, u32[]{:S(2)}, u32[]{:S(2)}) collective-permute-start(bf16[136,2048]{1,0:T(8,128)(2,1)} %get-tuple-element.244), channel_id=1, source_target_pairs={{0,24},{1,25},{2,26},{3,27},{4,28},{5,29},{6,30},{7,31},{8,16},{9,... | collective-permute-start | bytes 1671176 | tf_op jit(solution)/shard_map/ppermute | solution.py:316
  68.0 3.1 %collective-permute-start.2 = (bf16[272,2048]{1,0:T(8,128)(2,1)}, bf16[272,2048]{1,0:T(8,128)(2,1)}, u32[]{:S(2)}, u32[]{:S(2)}) collective-permute-start(bf16[272,2048]{1,0:T(8,128)(2,1)} %get-tuple-element.56.mine_ref), channel_id=1, source_target_pairs={{0,4},{1,5},{2,6},{3,7},{4,0},{5,1},{6,2},{7,3},{8,12},{9,13},{10,... | collective-permute-start | bytes 3342344 | tf_op jit(solution)/shard_map/cond/branch_1_fun/ppermute | solution.py:316
  75.5 1.9 copy-start.1
  77.4 1.9 copy-start.4
  79.3 1.9 copy-start.7
  81.2 1.9 copy-start.10
  83.1 18.8 %copy-start.44 = (bf16[136,2048]{1,0:T(8,128)(2,1)S(1)}, bf16[136,2048]{1,0:T(8,128)(2,1)}, u32[]{:S(2)}) copy-start(bf16[136,2048]{1,0:T(8,128)(2,1)} %get-tuple-element.273.refs_0_) | copy-start | bytes 1671172
  98.2 27.0 %collective-permute-start.16 = (bf16[272,2048]{1,0:T(8,128)(2,1)}, bf16[272,2048]{1,0:T(8,128)(2,1)}, u32[]{:S(2)}, u32[]{:S(2)}) collective-permute-start(bf16[272,2048]{1,0:T(8,128)(2,1)} %collective-permute-done.15.mine_ref), channel_id=1, source_target_pairs={{0,1},{1,0},{2,3},{3,2},{4,5},{5,4},{6,7},{7,6},{8,9},{9,8},{10,11... | collective-permute-start | bytes 3342344 | tf_op jit(solution)/shard_map/ppermute | solution.py:316
  98.3 34.5 %collective-permute-start.17 = (bf16[136,2048]{1,0:T(8,128)(2,1)}, bf16[136,2048]{1,0:T(8,128)(2,1)}, u32[]{:S(2)}, u32[]{:S(2)}) collective-permute-start(bf16[136,2048]{1,0:T(8,128)(2,1)} %get-tuple-element.287), channel_id=1, source_target_pairs={{0,8},{1,9},{2,10},{3,11},{4,12},{5,13},{6,14},{7,15},{8,0},{9,1},... | collective-permute-start | bytes 1671176 | tf_op jit(solution)/shard_map/ppermute | solution.py:316
  100.0 32.8 %collective-permute-start.18 = (bf16[136,2048]{1,0:T(8,128)(2,1)}, bf16[136,2048]{1,0:T(8,128)(2,1)}, u32[]{:S(2)}, u32[]{:S(2)}) collective-permute-start(bf16[136,2048]{1,0:T(8,128)(2,1)} %get-tuple-element.288), channel_id=1, source_target_pairs={{0,16},{1,17},{2,18},{3,19},{4,20},{5,21},{6,22},{7,23},{8,24},{9,... | collective-permute-start | bytes 1671176 | tf_op jit(solution)/shard_map/ppermute | solution.py:316
  101.5 31.2 %collective-permute-start.19 = (bf16[136,2048]{1,0:T(8,128)(2,1)}, bf16[136,2048]{1,0:T(8,128)(2,1)}, u32[]{:S(2)}, u32[]{:S(2)}) collective-permute-start(bf16[136,2048]{1,0:T(8,128)(2,1)} %get-tuple-element.289), channel_id=1, source_target_pairs={{0,24},{1,25},{2,26},{3,27},{4,28},{5,29},{6,30},{7,31},{8,16},{9,... | collective-permute-start | bytes 1671176 | tf_op jit(solution)/shard_map/ppermute | solution.py:316
  116.9 8.3 %copy-start.13 = (bf16[1152,768]{1,0:T(8,128)(2,1)}, bf16[1152,768]{1,0:T(8,128)(2,1)S(1)}, u32[]{:S(2)}) copy-start(bf16[1152,768]{1,0:T(8,128)(2,1)S(1)} %get-tuple-element.311.refs_11_) | copy-start | bytes 5308420
  116.9 8.3 %copy-start.19 = (bf16[1152,768]{1,0:T(8,128)(2,1)}, bf16[1152,768]{1,0:T(8,128)(2,1)S(1)}, u32[]{:S(2)}) copy-start(bf16[1152,768]{1,0:T(8,128)(2,1)S(1)} %get-tuple-element.312.refs_12_) | copy-start | bytes 5308420
  116.9 8.3 %copy-start.25 = (bf16[1152,768]{1,0:T(8,128)(2,1)}, bf16[1152,768]{1,0:T(8,128)(2,1)S(1)}, u32[]{:S(2)}) copy-start(bf16[1152,768]{1,0:T(8,128)(2,1)S(1)} %get-tuple-element.313.refs_13_) | copy-start | bytes 5308420
  125.2 3.2 %collective-permute-start.3 = (bf16[272,2048]{1,0:T(8,128)(2,1)}, bf16[272,2048]{1,0:T(8,128)(2,1)}, u32[]{:S(2)}, u32[]{:S(2)}) collective-permute-start(bf16[272,2048]{1,0:T(8,128)(2,1)} %get-tuple-element.62.mine_ref), channel_id=1, source_target_pairs={{0,4},{1,5},{2,6},{3,7},{4,0},{5,1},{6,2},{7,3},{8,12},{9,13},{10,... | collective-permute-start | bytes 3342344 | tf_op jit(solution)/shard_map/cond/branch_1_fun/ppermute | solution.py:316
  132.8 45.5 %all-to-all-start = ((bf16[4,72,2048]{2,1,0:T(8,128)(2,1)}), bf16[4,72,2048]{2,1,0:T(8,128)(2,1)}, u32[]{:S(2)}, u32[]{:S(2)}) async-start(bf16[4,72,2048]{2,1,0:T(8,128)(2,1)} %copy-done.32), calls=%async_computation | async-start | bytes 2359296 | tf_op jit(solution)/shard_map/all_to_all | solution.py:321
  137.1 34.5 %collective-permute-start.20 = (bf16[136,2048]{1,0:T(8,128)(2,1)}, bf16[136,2048]{1,0:T(8,128)(2,1)S(1)}, u32[]{:S(2)}, u32[]{:S(2)}) collective-permute-start(bf16[136,2048]{1,0:T(8,128)(2,1)} %get-tuple-element.301), channel_id=1, source_target_pairs={{0,8},{1,9},{2,10},{3,11},{4,12},{5,13},{6,14},{7,15},{8,0},{9,1},... | collective-permute-start | bytes 1671176 | tf_op jit(solution)/shard_map/ppermute | solution.py:316
  139.1 33.3 %collective-permute-start.21 = (bf16[136,2048]{1,0:T(8,128)(2,1)}, bf16[136,2048]{1,0:T(8,128)(2,1)S(1)}, u32[]{:S(2)}, u32[]{:S(2)}) collective-permute-start(bf16[136,2048]{1,0:T(8,128)(2,1)} %get-tuple-element.302), channel_id=1, source_target_pairs={{0,16},{1,17},{2,18},{3,19},{4,20},{5,21},{6,22},{7,23},{8,24},{9,... | collective-permute-start | bytes 1671176 | tf_op jit(solution)/shard_map/ppermute | solution.py:316
  140.5 36.9 %collective-permute-start.22 = (bf16[136,2048]{1,0:T(8,128)(2,1)}, bf16[136,2048]{1,0:T(8,128)(2,1)S(1)}, u32[]{:S(2)}, u32[]{:S(2)}) collective-permute-start(bf16[136,2048]{1,0:T(8,128)(2,1)} %get-tuple-element.303), channel_id=1, source_target_pairs={{0,24},{1,25},{2,26},{3,27},{4,28},{5,29},{6,30},{7,31},{8,16},{9,... | collective-permute-start | bytes 1671176 | tf_op jit(solution)/shard_map/ppermute | solution.py:316
  140.6 1.9 copy-start.2
  178.3 37.1 %all-to-all-start.1 = ((bf16[4,72,2048]{2,1,0:T(8,128)(2,1)}), bf16[4,72,2048]{2,1,0:T(8,128)(2,1)}, u32[]{:S(2)}, u32[]{:S(2)}) async-start(bf16[4,72,2048]{2,1,0:T(8,128)(2,1)} %copy-done.33), calls=%async_computation.1 | async-start | bytes 2359296 | tf_op jit(solution)/shard_map/all_to_all | solution.py:321
  182.5 1.9 copy-start.3
  184.4 1.9 copy-start.6
  186.3 1.9 copy-start.9
  188.2 1.9 copy-start.12
  218.1 2.0 collective-permute-start.4
  221.2 20.5 %all-to-all-start.2 = ((bf16[4,72,2048]{2,1,0:T(8,128)(2,1)}), bf16[4,72,2048]{2,1,0:T(8,128)(2,1)S(1)}, u32[]{:S(2)}, u32[]{:S(2)}) async-start(bf16[4,72,2048]{2,1,0:T(8,128)(2,1)} %get-tuple-element.347), calls=%async_computation.2 | async-start | bytes 2359296 | tf_op jit(solution)/shard_map/all_to_all | solution.py:321
  225.3 48.6 %collective-permute-start.24 = (bf16[136,2048]{1,0:T(8,128)(2,1)}, bf16[136,2048]{1,0:T(8,128)(2,1)}, u32[]{:S(2)}, u32[]{:S(2)}) collective-permute-start(bf16[136,2048]{1,0:T(8,128)(2,1)} %get-tuple-element.463), channel_id=1, source_target_pairs={{0,2},{1,3},{2,0},{3,1},{4,6},{5,7},{6,4},{7,5},{8,10},{9,11},{10,... | collective-permute-start | bytes 1671176 | tf_op jit(solution)/shard_map/ppermute | solution.py:316
  230.4 3.1 %copy-start.30 = (bf16[1152,768]{1,0:T(8,128)(2,1)S(1)}, bf16[1152,768]{1,0:T(8,128)(2,1)}, u32[]{:S(2)}) copy-start(bf16[1152,768]{1,0:T(8,128)(2,1)} %copy-done.29) | copy-start | bytes 5308420
  230.4 2.2 collective-permute-start.5
  244.0 9.3 %copy-start.24 = (bf16[1152,768]{1,0:T(8,128)(2,1)S(1)}, bf16[1152,768]{1,0:T(8,128)(2,1)}, u32[]{:S(2)}) copy-start(bf16[1152,768]{1,0:T(8,128)(2,1)} %copy-done.23) | copy-start | bytes 5308420
  244.0 2.0 collective-permute-start.6
  246.2 23.2 %all-to-all-start.3 = ((bf16[4,72,2048]{2,1,0:T(8,128)(2,1)}), bf16[4,72,2048]{2,1,0:T(8,128)(2,1)S(1)}, u32[]{:S(2)}, u32[]{:S(2)}) async-start(bf16[4,72,2048]{2,1,0:T(8,128)(2,1)} %copy-done.31), calls=%async_computation.3 | async-start | bytes 2359296 | tf_op jit(solution)/shard_map/all_to_all | solution.py:321
  250.4 11.0 %copy-start.18 = (bf16[1152,768]{1,0:T(8,128)(2,1)S(1)}, bf16[1152,768]{1,0:T(8,128)(2,1)}, u32[]{:S(2)}) copy-start(bf16[1152,768]{1,0:T(8,128)(2,1)} %copy-done.17) | copy-start | bytes 5308420
  250.4 23.5 %collective-permute-start.23 = (bf16[136,2048]{1,0:T(8,128)(2,1)}, bf16[136,2048]{1,0:T(8,128)(2,1)}, u32[]{:S(2)}, u32[]{:S(2)}) collective-permute-start(bf16[136,2048]{1,0:T(8,128)(2,1)} %get-tuple-element.464), channel_id=1, source_target_pairs={{0,1},{1,0},{2,3},{3,2},{4,5},{5,4},{6,7},{7,6},{8,9},{9,8},{10,11... | collective-permute-start | bytes 1671176 | tf_op jit(solution)/shard_map/ppermute | solution.py:316
  252.1 25.9 %collective-permute-start.25 = (bf16[136,2048]{1,0:T(8,128)(2,1)S(1)}, bf16[136,2048]{1,0:T(8,128)(2,1)}, u32[]{:S(2)}, u32[]{:S(2)}) collective-permute-start(bf16[136,2048]{1,0:T(8,128)(2,1)S(1)} %get-tuple-element.465), channel_id=1, source_target_pairs={{0,3},{1,2},{2,1},{3,0},{4,7},{5,6},{6,5},{7,4},{8,11},{9,10},{10,... | collective-permute-start | bytes 1671176 | tf_op jit(solution)/shard_map/ppermute | solution.py:316
  271.7 2.0 collective-permute-start.7
  273.9 8.8 %copy-start.43 = (s32[128,8]{0,1:T(8,128)S(1)}, s32[128,8]{0,1:T(8,128)}, u32[]{:S(2)}) copy-start(s32[128,8]{0,1:T(8,128)} %param.26) | copy-start | bytes 12292
  (27 other events, 33.4 us)

commit v2 on v1

v2 whole, which is shorter than its diff:
```python
import functools

import jax
import jax.numpy as jnp
from jax import lax
from jax.experimental import pallas as pl
from jax.experimental.pallas import tpu as pltpu
from jax.sharding import PartitionSpec as P

F32 = jnp.float32
BF16 = jnp.bfloat16
NT = (((1,), (1,)), ((), ()))
TN = (((0,), (0,)), ((), ()))
LANES = 128
EXTRA = 16
TAIL = 8


def pad_to(value, unit):
    return -(-value // unit) * unit


class Rows:
    def __init__(self, cap):
        self.slots = 2 * cap
        self.base = self.slots // 16 * 16
        self.shift = self.slots - self.base
        self.group = pad_to(self.slots + self.shift + 1, 8)
        self.prob = 2 * self.slots
        self.message = max(pad_to(self.prob + 1, 8), self.base + self.group)


def iota(shape, dim):
    return lax.broadcasted_iota(jnp.int32, shape, dim)


def eye(rows):
    return jnp.where(iota((rows, LANES), 0) == iota((rows, LANES), 1), 1.0, 0.0).astype(BF16)


def ranks(info_ref, w_refs, first, targets):
    place = iota((EXTRA, LANES), 0) == info_ref[0]
    lines = []
    for j in range(targets):
        lane = pl.multiple_of(info_ref[1 + j] * LANES, LANES)
        parts = []
        for w in w_refs:
            part = w[first : first + EXTRA, pl.ds(lane, LANES)].astype(F32)
            parts.append(jnp.sum(jnp.where(place, part, 0.0), axis=0, keepdims=True))
        lines.append(jnp.concatenate(parts, axis=1))
    tokens = lines[0].shape[1]
    lines.append(jnp.zeros((pad_to(targets, 8) - targets, tokens), F32))
    probs = jnp.concatenate([line for line in lines if line.shape[0]], axis=0)
    named = probs != 0.0
    upto = jnp.where(iota((tokens, tokens), 0) <= iota((tokens, tokens), 1), 1.0, 0.0).astype(BF16)
    count = jnp.dot(jnp.where(named, 1.0, 0.0).astype(BF16), upto, preferred_element_type=F32)
    return probs, jnp.where(named, count, -999.0)


def pick(rank, j, rows, start=0):
    slot = (iota((rows, rank.shape[1]), 0) + (1 - start)).astype(F32)
    return jnp.where(slot == rank[j : j + 1, :], 1.0, 0.0).astype(BF16)


def pack_kernel(nodes, locals_, x_ref, dy_ref, ids_ref, probs_ref, out_ref):
    tokens, width = x_ref.shape
    out_ref[:tokens, :] = x_ref[...]
    out_ref[tokens : 2 * tokens, :] = dy_ref[...]
    place = iota((EXTRA, tokens), 0)
    ids, probs = ids_ref[...], probs_ref[...].astype(F32)
    for n in range(width // tokens):
        line = jnp.zeros((EXTRA, tokens), F32)
        if n < nodes:
            for k in range(ids.shape[0]):
                hit = (place < locals_) & (ids[k : k + 1, :] == place + n * locals_)
                line = line + jnp.where(hit, probs[k : k + 1, :], 0.0)
        out_ref[2 * tokens :, n * tokens : (n + 1) * tokens] = line.astype(BF16)


def finish_kernel(chips, locals_, info_ref, ids_ref, *refs):
    totals, (grad_x_ref, grad_probs_ref) = refs[:-2], refs[-2:]
    tokens, width = grad_x_ref.shape
    step = next(s for s in (512, 256, 128) if width % s == 0)
    for start in range(0, width, step):
        cols = slice(start, start + step)
        total = totals[0][:tokens, cols].astype(F32)
        for t in totals[1:]:
            total = total + t[:tokens, cols].astype(F32)
        grad_x_ref[:, cols] = total.astype(BF16)
    apart = ids_ref[...] ^ info_ref[0]
    grads = jnp.zeros(apart.shape, F32)
    for c, t in enumerate(totals):
        for j, chip in enumerate(chips):
            tail = t[tokens:, j * LANES : (j + 1) * LANES].astype(F32)
            for dl in range(2):
                here = apart == (chip + dl) * locals_ + c
                grads = jnp.where(here, tail[dl : dl + 1, :], grads)
    grad_probs_ref[...] = grads.astype(BF16)


def dispatch_kernel(at, targets, info_ref, mine_ref, sibling_ref, *outs):
    tokens = (mine_ref.shape[0] - EXTRA) // 2
    width = mine_ref.shape[1]
    blocks = (mine_ref, sibling_ref)
    probs, rank = ranks(info_ref, blocks, 2 * tokens, targets)
    picks, lines = [], []
    for j in range(targets):
        x = pick(rank, j, at.message)
        dy = pick(rank, j, at.message, at.slots)
        picks.append(
            jnp.concatenate([x[:, :tokens], dy[:, :tokens], x[:, tokens:], dy[:, tokens:]], axis=1)
        )
        lines.append(
            lax.dot_general(
                probs.astype(BF16), pick(rank, j, LANES), NT, preferred_element_type=F32
            )[j : j + 1, :]
        )
    picks = jnp.concatenate(picks, axis=0)
    step = next(s for s in (1024, 512, 256, 128) if width % s == 0)
    for start in range(0, width, step):
        rows = jnp.concatenate([b[: 2 * tokens, start : start + step] for b in blocks], axis=0)
        out = jnp.dot(picks, rows, preferred_element_type=F32)
        for j in range(targets):
            part = out[j * at.message : (j + 1) * at.message]
            if start == 0:
                line = jnp.concatenate([lines[j], jnp.zeros((1, step - LANES), F32)], axis=1)
                part = jnp.where(iota(part.shape, 0) == at.prob, line, part)
            if len(outs) == targets:
                outs[j][:, start : start + step] = part.astype(BF16)
            else:
                outs[0][info_ref[1 + j] // 2, :, start : start + step] = part.astype(BF16)


def combine_kernel(at, targets, info_ref, mine_ref, sibling_ref, *refs):
    rets_ref, keep_ref, send_ref = refs
    chips = [info_ref[1 + j] // 2 for j in range(targets)]
    tokens = keep_ref.shape[0] - TAIL
    width = keep_ref.shape[1]
    _, rank = ranks(info_ref, (mine_ref, sibling_ref), 0, targets)
    picks = jnp.concatenate([pick(rank, j, at.group) for j in range(targets)], axis=0)
    step = next(s for s in (1024, 512, 256, 128) if width % s == 0)
    for start in range(0, width, step):
        rows = [rets_ref[chips[j], :, start : start + step] for j in range(targets)]
        total = lax.dot_general(
            picks, jnp.concatenate(rows, axis=0), TN, preferred_element_type=F32
        )
        keep_ref[:tokens, start : start + step] = total[:tokens].astype(BF16)
        send_ref[:tokens, start : start + step] = total[tokens:].astype(BF16)
    row = iota((TAIL, LANES), 0)
    for n in range(width // LANES):
        keep = send = jnp.zeros((TAIL, LANES), F32)
        if n < targets:
            tail = rets_ref[chips[n], at.group - 8 :, :LANES]
            line = jnp.dot(tail, pick(rank, n, LANES), preferred_element_type=F32)[7:8]
            keep = jnp.where(row == 0, line[:, :tokens], keep)
            send = jnp.where(row == 1, line[:, tokens:], send)
        keep_ref[tokens:, n * LANES : (n + 1) * LANES] = keep.astype(BF16)
        send_ref[tokens:, n * LANES : (n + 1) * LANES] = send.astype(BF16)


def expert_kernel(at, sources, aliased, info_ref, *refs):
    joined = len(refs[0].shape) == 3
    if joined:
        msgs, refs = [refs[0].at[i] for i in range(sources)], refs[1:]
    else:
        msgs, refs = refs[:sources], refs[sources:]
    stored, refs = refs[:5], refs[5 + aliased :]
    ret_ref, x_all, dy_all, hp_ref, du_ref, dg_ref = refs[:6]
    held, (moved_ref, sems) = refs[6:11], refs[11:]
    rows, hidden = hp_ref.shape
    width = x_all.shape[1]
    group, shift = at.group, at.shift
    copies = [
        pltpu.make_async_copy(src, dst, sems.at[i]) for i, (src, dst) in enumerate(zip(stored, held))
    ]
    for copy in copies:
        copy.start()
    x_all[...] = jnp.concatenate([m[:group, :] for m in msgs], axis=0)
    dy_all[...] = jnp.concatenate([m[at.base : at.base + group, :] for m in msgs], axis=0)
    first = at.prob // 8 * 8
    line = at.prob - first
    p = jnp.concatenate(
        [
            lax.dot_general(
                eye(group), m[first : first + 8, :LANES], NT, preferred_element_type=F32
            )[:, line : line + 1]
            for m in msgs
        ],
        axis=0,
    )
    copies[0].wait()
    g = jnp.dot(x_all[...], held[0][0], preferred_element_type=F32)
    copies[1].wait()
    u = jnp.dot(x_all[...], held[1][0], preferred_element_type=F32)
    copies[2].wait()
    moved_ref[:rows, :] = jnp.dot(dy_all[...], held[2][...], preferred_element_type=F32)
    moved_ref[rows:, :] = jnp.zeros((8, hidden), F32)
    dh = moved_ref[shift : shift + rows, :]
    s = jax.nn.sigmoid(g)
    a = g * s
    h = a * u
    sd = dh * p
    pg = jnp.sum(dh * h, axis=1, keepdims=True)
    du_ref[...] = (sd * a).astype(BF16)
    dg_ref[...] = (sd * u * s * (1.0 + g * (1.0 - s))).astype(BF16)
    moved_ref[:8, :] = jnp.zeros((8, hidden), F32)
    moved_ref[shift : shift + rows, :] = h * p
    hp_ref[...] = moved_ref[:rows, :].astype(BF16)
    pg = (pg + jnp.zeros((rows, LANES), F32)).astype(BF16)
    last = iota((8, LANES), 0) == 7
    copies[3].wait()
    copies[4].wait()
    step = next(s for s in (1024, 512, 256, 128) if width % s == 0)
    for start in range(0, width, step):
        cols = slice(start, start + step)
        dx = jnp.dot(dg_ref[...], held[3][:, cols], preferred_element_type=F32)
        dx = dx + jnp.dot(du_ref[...], held[4][:, cols], preferred_element_type=F32)
        for i in range(sources):
            chip = i if joined else info_ref[1 + i] // 2
            part = slice(i * group, (i + 1) * group)
            ret_ref[chip, :, cols] = dx[part, :].astype(BF16)
            if start == 0:
                grads = lax.dot_general(
                    pg[part, :], eye(group), TN, preferred_element_type=F32
                )[:1]
                tail = jnp.where(last, grads, dx[(i + 1) * group - 8 : (i + 1) * group, :LANES])
                ret_ref[chip, group - 8 :, :LANES] = tail.astype(BF16)


def whole(shape):
    return pl.BlockSpec(shape, lambda *_: (0,) * len(shape), pipeline_mode=pl.Buffered(1))


def params(mib):
    return pltpu.CompilerParams(vmem_limit_bytes=mib * 1024 * 1024)


COST = pl.CostEstimate(flops=1024, bytes_accessed=1024, transcendentals=0)


SMEM = pl.BlockSpec(memory_space=pltpu.SMEM)


def call(kernel, info, operands, out_shape, in_specs=None, mib=60):
    return pl.pallas_call(
        kernel,
        grid=(1,),
        in_specs=([SMEM] if info is not None else [])
        + (in_specs or [whole(a.shape) for a in operands]),
        out_specs=[whole(s.shape) for s in out_shape],
        out_shape=out_shape,
        compiler_params=params(mib),
        cost_estimate=COST,
    )(*([info] if info is not None else []), *operands)


def pack(x, dy, ids, probs, nodes, locals_):
    tokens, width = x.shape
    shape = jax.ShapeDtypeStruct((2 * tokens + EXTRA, width), BF16)
    kernel = functools.partial(pack_kernel, nodes, locals_)
    return call(kernel, None, [x, dy, ids, probs], [shape])[0]


def finish(info, ids_t, totals, chips, locals_):
    tokens, width = totals[0].shape[0] - TAIL, totals[0].shape[1]
    shapes = [
        jax.ShapeDtypeStruct((tokens, width), BF16),
        jax.ShapeDtypeStruct(ids_t.shape, BF16),
    ]
    kernel = functools.partial(finish_kernel, chips, locals_)
    grad_x, grad_probs = call(kernel, info, [ids_t, *totals], shapes, mib=24)
    return grad_x, grad_probs.T


def dispatch(at, targets, info, mine, sibling, joined):
    height, width = mine.shape
    if joined:
        shapes = [jax.ShapeDtypeStruct((targets, at.message, width), BF16)]
    else:
        shapes = [jax.ShapeDtypeStruct((at.message, width), BF16)] * targets
    kernel = functools.partial(dispatch_kernel, at, targets)
    out = call(kernel, info, [mine, sibling], shapes)
    return out[0] if joined else out


def combine(at, info, mine, sibling, rets):
    height, width = mine.shape
    tokens = (height - EXTRA) // 2
    shapes = [jax.ShapeDtypeStruct((tokens + TAIL, width), BF16)] * 2
    kernel = functools.partial(combine_kernel, at, rets.shape[0])
    extra = pl.BlockSpec((EXTRA, width), lambda *_: (2 * tokens // EXTRA, 0))
    specs = [extra, extra, whole(rets.shape)]
    return call(kernel, info, [mine, sibling, rets], shapes, specs, 24)


def expert(at, info, msgs, weights, saved, chunk, chunks):
    sources = sum(m.size // (at.message * m.shape[-1]) for m in msgs)
    width = msgs[0].shape[-1]
    hidden = weights[0].shape[2]
    rows = sources * at.group
    wide_spec, thin_spec = (
        pl.BlockSpec((rows, n), lambda *_: (chunk, 0), pipeline_mode=pl.Buffered(1))
        for n in (width, hidden)
    )
    out_shape = [jax.ShapeDtypeStruct((sources, at.group, width), BF16)]
    out_specs = [whole(s.shape) for s in out_shape] + [wide_spec] * 2 + [thin_spec] * 3
    out_shape += [jax.ShapeDtypeStruct((chunks * rows, width), BF16)] * 2
    out_shape += [jax.ShapeDtypeStruct((chunks * rows, hidden), BF16)] * 3
    in_specs = [SMEM] + [whole(m.shape) for m in msgs]
    in_specs += [pl.BlockSpec(memory_space=pl.ANY)] * (5 + len(saved))
    aliases = {1 + len(msgs) + 5 + i: 1 + i for i in range(len(saved))}
    out = pl.pallas_call(
        functools.partial(expert_kernel, at, sources, len(saved)),
        grid=(1,),
        in_specs=in_specs,
        out_specs=out_specs,
        out_shape=out_shape,
        input_output_aliases=aliases,
        scratch_shapes=[pltpu.VMEM(w.shape, BF16) for w in weights]
        + [pltpu.VMEM((rows + 8, hidden), F32), pltpu.SemaphoreType.DMA((5,))],
        compiler_params=params(60),
        cost_estimate=COST,
    )(info, *msgs, *weights, *saved)
    return out[0], out[1:]


def shards(tokens_x, grad_out, expert_ids, probs, w_gate, w_up, w_down):
    nodes, locals_ = lax.axis_size("node"), lax.axis_size("local")
    experts = nodes * locals_
    tokens, top = expert_ids.shape
    width = tokens_x.shape[1]
    at = Rows(tokens * top // experts + 1)
    node, local = lax.axis_index("node"), lax.axis_index("local")
    both = ("node", "local")
    chips = list(range(0, nodes, 2))
    targets = len(chips)

    def swap(value, dn=0, dz=0):
        pairs = [
            (n * locals_ + z, (n ^ dn) * locals_ + (z ^ dz))
            for n in range(nodes)
            for z in range(locals_)
        ]
        return lax.ppermute(value, both, pairs)

    def along(value, moves):
        pairs = [(n * locals_ + a, n * locals_ + b) for n in range(nodes) for a, b in moves]
        return lax.ppermute(value, both, pairs)

    middle = (local == 1) | (local == 2)
    same_core = [list(range(core, nodes, 2)) for core in range(2)]

    def back(value):
        return lax.all_to_all(
            value, "node", split_axis=0, concat_axis=0, axis_index_groups=same_core, tiled=True
        )

    def fence(*values):
        return lax.optimization_barrier(values)

    ids_t = expert_ids.T
    info = jnp.concatenate([local[None], node ^ jnp.array(chips, jnp.int32)]).astype(jnp.int32)
    payload = pack(tokens_x, grad_out, ids_t, probs.T, nodes, locals_)

    def sisters(block):
        return swap(block, 1)

    def fill(block, sister, joined):
        return dispatch(at, targets, info, block, sister, joined)

    def send(msgs):
        return [msgs[0]] + [swap(msgs[j], chips[j]) for j in range(1, targets)]

    def turn(token):
        down, gate, up, _ = fence(w_down, w_gate, w_up, token)
        return [w_gate, w_up, down[0].T, gate[0].T, up[0].T]

    def work(c, msgs, weights, saved):
        return expert(at, info, msgs, weights, saved, c, locals_)

    def merge(block, sister, ret):
        return combine(at, info, block, sister, ret)

    (go,) = fence(node < nodes)

    def at_once(step, *args):
        shapes = jax.eval_shape(step, *args)
        idle = lambda *_: jax.tree.map(lambda v: jnp.zeros(v.shape, v.dtype), shapes)
        return lax.cond(go, step, idle, *args)

    def prepare(block, joined=False):
        def step(block):
            sister = sisters(block)
            return sister, fill(block, sister, joined)

        return at_once(step, block)

    def home(parts):
        def step(keep, other):
            return (keep.astype(F32) + swap(other, 1).astype(F32)).astype(BF16)

        return at_once(step, *parts)

    def wgrad(a, b):
        return lax.dot_general(a, b, TN, preferred_element_type=F32).astype(BF16)

    if locals_ == 4:
        b0 = payload
        b1, inner = swap(b0, 0, 1), along(b0, [(1, 2), (2, 1)])
        s0, m0 = prepare(b0, joined=True)
        p0 = back(m0)
        weights = turn(m0)
        b1, inner, weights = fence(b1, inner, weights)
        outward, inner2 = along(inner, [(1, 0), (2, 3)]), along(b1, [(1, 2), (2, 1)])
        s1, m1 = prepare(b1)
        p0, m1 = fence(p0, m1)
        p1 = send(m1)
        r0, saved = work(0, [p0], weights, ())
        outward, inner2, r0 = fence(outward, inner2, r0)
        b2 = jnp.where(middle, inner2, outward)
        s2, m2 = prepare(b2)
        p1, m2, b2, r0, saved = fence(p1, m2, b2, r0, saved)
        p2 = send(m2)
        b3 = swap(b2, 0, 1)
        r1, saved = work(1, p1, weights, saved)
        b3, r1 = fence(b3, r1)
        s3, m3 = prepare(b3)
        p2, m3, r1, saved = fence(p2, m3, r1, saved)
        p3 = send(m3)
        r2, saved = work(2, p2, weights, saved)
        p3, r2, saved = fence(p3, r2, saved)
        r2 = back(r2)
        r3, saved = work(3, p3, weights, saved)
        r2, r3, saved = fence(r2, r3, saved)
        t2 = home(merge(b2, s2, r2))
        t2, r3, saved = fence(t2, r3, saved)
        r3 = back(r3)
        t2 = swap(t2, 0, 2)
        x_all, dy_all, hp, du, dg = saved
        gate_wgrad = wgrad(x_all, dg)
        r3, gate_wgrad = fence(r3, gate_wgrad)
        t3 = home(merge(b3, s3, r3))
        t3, r0, r1, x_all, dy_all, hp, du = fence(t3, r0, r1, x_all, dy_all, hp, du)
        t3 = swap(t3, 0, 3)
        r1 = back(r1)
        up_wgrad, down_wgrad = wgrad(x_all, du), wgrad(hp, dy_all)
        r1, r0, t2, up_wgrad, down_wgrad = fence(r1, r0, t2, up_wgrad, down_wgrad)
        r0 = back(r0)
        r1, t3 = fence(r1, t3)
        t1 = swap(home(merge(b1, s1, r1)), 0, 1)
        t0 = home(merge(b0, s0, r0))
        t0, t1, t2, t3 = fence(t0, t1, t2, t3)
        totals = [t0, t1, t2, t3]
    else:
        weights, saved, totals = turn(payload), (), []
        for c in range(locals_):
            block = swap(payload, 0, c) if c else payload
            sister, msgs = prepare(block)
            ret, saved = work(c, send(msgs), weights, saved)
            total = home(merge(block, sister, back(ret)))
            totals.append(swap(total, 0, c) if c else total)
        x_all, dy_all, hp, du, dg = saved
        gate_wgrad, up_wgrad = wgrad(x_all, dg), wgrad(x_all, du)
        down_wgrad = wgrad(hp, dy_all)

    me = (node * locals_ + local)[None].astype(jnp.int32)
    grad_x, grad_probs = finish(me, ids_t, totals, chips, locals_)
    return (grad_x, grad_probs, gate_wgrad[None], up_wgrad[None], down_wgrad[None])


def solution(mesh):
    row, cube = P(("node", "local"), None), P(("node", "local"), None, None)
    return jax.shard_map(
        shards,
        mesh=mesh,
        in_specs=(row, row, row, row, cube, cube, cube),
        out_specs=(row, row, cube, cube, cube),
        check_vma=False,
    )
```

time: 285 us -> 243 us (0.85)
  local copies, waits for them, and re-layouts: 64.8 us -> 13.3 us
  starting transfers between devices: 41.5 us -> 51.1 us
  Pallas kernels: 86.1 us -> 77.6 us
  waiting for transfers between devices: 59.7 us -> 66.1 us
    unnamed x90 -> x14, local copies, waits for them, and re-layouts: 50.4 us -> 1.07 us
    all_to_all x4 -> x5, waiting for transfers between devices: 0.01 us -> 14.8 us  [back(): lax.all_to_all(value, 'node', split_axis=0, concat_axis=0, axis_index_gro...]
    pallas_call x4, Pallas kernels: 56.2 us -> 47.6 us  [expert(): pl.pallas_call(functools.partial(expert_kernel, at, sources, len(saved)),...]
    ppermute x26 -> x22, waiting for transfers between devices: 59.7 us -> 51.2 us  [swap(): return lax.ppermute(value, both, pairs)]
    ppermute x0 -> x3, starting transfers between devices: none -> 4.24 us  [along(): return lax.ppermute(value, both, pairs)]
    convert_element_type x3 -> x0, other arithmetic: 3.82 us -> none  [the longest x1 2.48 us: shards(): grad_x = total.astype(BF16)]
    all_to_all x4 -> x5, starting transfers between devices: 16.9 us -> 19.7 us  [back(): lax.all_to_all(value, 'node', split_axis=0, concat_axis=0, axis_index_gro...]
    ppermute x26 -> x22, starting transfers between devices: 24.6 us -> 27.1 us  [swap(): return lax.ppermute(value, both, pairs)]
  transfers between devices with their start and end apart: 30 -> 30, of which waited for: 12 -> 18; matrix products, arithmetic and copies ran while one was open for 13% -> 17% of each run, Pallas kernels for 29% -> 30%
where the time goes in v2:
time: 243 us; the launch traced here: 239 us
  Pallas kernels  77.6 us (32%)
  waiting for transfers between devices  66.1 us (27%)
  starting transfers between devices  51.1 us (21%)
  matrix products  25 us (10%)
  local copies, waits for them, and re-layouts  13.3 us (5%)
  other arithmetic  4.5 us (2%)
    ppermute x22, waiting for transfers between devices, swap(): return lax.ppermute(value, both, pairs)  51.2 us
    pallas_call x4, Pallas kernels, expert(): pl.pallas_call(functools.partial(expert_kernel, at, sources, len(saved)),...  47.6 us
    pallas_call x10, Pallas kernels, call(): pl.pallas_call(kernel, grid=(1,), in_specs=([SMEM] if info is not None el...  30 us
    ppermute x22, starting transfers between devices, swap(): return lax.ppermute(value, both, pairs)  27.1 us
    dot_general x3, matrix products, wgrad(): return lax.dot_general(a, b, TN, preferred_element_type=F32).astype(BF16)  25 us
    all_to_all x5, starting transfers between devices, back(): lax.all_to_all(value, 'node', split_axis=0, concat_axis=0, axis_index_gro...  19.7 us
    all_to_all x5, waiting for transfers between devices, back(): lax.all_to_all(value, 'node', split_axis=0, concat_axis=0, axis_index_gro...  14.8 us
    optimization_barrier x3, local copies, waits for them, and re-layouts, fence(): return lax.optimization_barrier(values)  12.3 us
  transfers between devices with their start and end apart: 30, of which 18 were waited for; matrix products, arithmetic and copies ran while one was open for 17% of the time, Pallas kernels for 30%

profile of v2, /device:TPU:0, one launch (start us, length us, event | category | flops | bytes accessed | tf_op | source)
XLA Modules:
  0.0 238.8 jit_solution(12603185390277819879)
XLA Ops:
  0.6 2.4 shard_map.119.mine_ref
  4.7 4.9 %collective-permute-start.8 = (bf16[272,2048]{1,0:T(8,128)(2,1)}, bf16[272,2048]{1,0:T(8,128)(2,1)}, u32[]{:S(2)}, u32[]{:S(2)}) collective-permute-start(bf16[272,2048]{1,0:T(8,128)(2,1)} %shard_map.119.mine_ref), channel_id=1, source_target_pairs={{0,1},{1,0},{2,3},{3,2},{4,5},{5,4},{6,7},{7,6},{8,9},{9,8},{10,11... | collective-permute-start | bytes 3342344 | tf_op jit(solution)/shard_map/ppermute | solution.py:344
  9.6 7.7 %conditional.8 = (bf16[272,2048]{1,0:T(8,128)(2,1)}, bf16[4,136,2048]{2,1,0:T(8,128)(2,1)}) conditional(s32[]{:T(128)} %convert_element_type.55, () %tuple.76, (bf16[272,2048]{1,0:T(8,128)(2,1)}, s32[5]{0:T(128)S(1)}) %tuple.77), branch_computations={%region_0.0_spmd, %region_1.0_spmd} | conditional | flops 1024 | bytes 4457528 | solution.py:389
  9.7 3.1 %collective-permute-done.sibling_ref = bf16[272,2048]{1,0:T(8,128)(2,1)} collective-permute-done((bf16[272,2048]{1,0:T(8,128)(2,1)}, bf16[272,2048]{1,0:T(8,128)(2,1)}, u32[]{:S(2)}, u32[]{:S(2)}) %collective-permute-start) | collective-permute-done | bytes 1114144 | tf_op jit(solution)/shard_map/cond/branch_1_fun/ppermute | solution.py:344
  12.7 4.6 %branch_1_fun.4 = bf16[4,136,2048]{2,1,0:T(8,128)(2,1)} custom-call(s32[5]{0:T(128)S(1)} %get-tuple-element.42.info_ref, bf16[272,2048]{1,0:T(8,128)(2,1)} %get-tuple-element.40.mine_ref, bf16[272,2048]{1,0:T(8,128)(2,1)} %collective-permute-done.sibling_ref), custom_call_target="tpu_custom_call" | custom-call | flops 1024 | bytes 1024 | tf_op jit(solution)/shard_map/cond/branch_1_fun/pallas_call | solution.py:245
  17.4 4.5 %all-to-all-start = ((bf16[4,136,2048]{2,1,0:T(8,128)(2,1)}), bf16[4,136,2048]{2,1,0:T(8,128)(2,1)}, u32[]{:S(2)}, u32[]{:S(2)}) async-start(bf16[4,136,2048]{2,1,0:T(8,128)(2,1)} %get-tuple-element.214), calls=%async_computation | async-start | bytes 4456448 | tf_op jit(solution)/shard_map/all_to_all | solution.py:354
  21.9 4.8 %copy.28 = bf16[1,768,2048]{1,2,0:T(8,128)(2,1)} copy(bf16[1,768,2048]{2,1,0:T(8,128)(2,1)} %param.30) | data formatting | bytes 6291456 | tf_op jit(solution)/shard_map/optimization_barrier | solution.py:359
  26.7 2.9 %copy.29 = bf16[1,2048,768]{1,2,0:T(8,128)(2,1)} copy(bf16[1,2048,768]{2,1,0:T(8,128)(2,1)S(1)} %copy-done.1) | data formatting | bytes 6291456 | tf_op jit(solution)/shard_map/optimization_barrier | solution.py:359
  29.5 4.6 %copy.30 = bf16[1,2048,768]{1,2,0:T(8,128)(2,1)} copy(bf16[1,2048,768]{2,1,0:T(8,128)(2,1)} %refs_5_.2) | data formatting | bytes 6291456 | tf_op jit(solution)/shard_map/optimization_barrier | solution.py:359
  36.7 7.4 %conditional.9 = (bf16[272,2048]{1,0:T(8,128)(2,1)}, bf16[136,2048]{1,0:T(8,128)(2,1)S(1)}, bf16[136,2048]{1,0:T(8,128)(2,1)}, bf16[136,2048]{1,0:T(8,128)(2,1)}, bf16[136,2048]{1,0:T(8,128)(2,1)}) conditional(s32[]{:T(128)} %convert_element_type.55, () %tuple.79, (bf16[272,2048]{1,0:T(8,128)(2,1)}, s32[5]{0:T(128)S(1)}) %tuple.82), branch_computations={%region_2.0_spmd, %region_3.0_spmd} | conditional | flops 1024 | bytes 4457552 | solution.py:389
  36.9 3.0 %collective-permute-done.1.sibling_ref = bf16[272,2048]{1,0:T(8,128)(2,1)} collective-permute-done((bf16[272,2048]{1,0:T(8,128)(2,1)}, bf16[272,2048]{1,0:T(8,128)(2,1)}, u32[]{:S(2)}, u32[]{:S(2)}) %collective-permute-start.1) | collective-permute-done | bytes 1114144 | tf_op jit(solution)/shard_map/cond/branch_1_fun/ppermute | solution.py:344
  39.9 4.3 %branch_1_fun.5 = (bf16[136,2048]{1,0:T(8,128)(2,1)S(1)}, bf16[136,2048]{1,0:T(8,128)(2,1)}, bf16[136,2048]{1,0:T(8,128)(2,1)}, bf16[136,2048]{1,0:T(8,128)(2,1)}) custom-call(s32[5]{0:T(128)S(1)} %get-tuple-element.44.info_ref, bf16[272,2048]{1,0:T(8,128)(2,1)} %get-tuple-element.43.mine_ref, bf16[272,2048]{1,0:T(8,128)(2,1)} %collective-permute-done.1.sibling_ref), custom_call_target="tpu_custom_call" | custom-call | flops 1024 | bytes 1024 | tf_op jit(solution)/shard_map/cond/branch_1_fun/pallas_call | solution.py:245
  44.2 4.6 %all-to-all-done.refs_0_ = bf16[4,136,2048]{2,1,0:T(8,128)(2,1)} async-done(((bf16[4,136,2048]{2,1,0:T(8,128)(2,1)}), bf16[4,136,2048]{2,1,0:T(8,128)(2,1)}, u32[]{:S(2)}, u32[]{:S(2)}) %all-to-all-start) | async-done | bytes 2228256 | tf_op jit(solution)/shard_map/all_to_all | solution.py:354
  52.3 11.8 %shard_map.120 = (bf16[4,72,2048]{2,1,0:T(8,128)(2,1)}, bf16[1152,2048]{1,0:T(8,128)(2,1)}, bf16[1152,2048]{1,0:T(8,128)(2,1)}, bf16[1152,768]{1,0:T(8,128)(2,1)...) custom-call(s32[5]{0:T(128)S(1)} %pad_add_fusion.info_ref, bf16[4,136,2048]{2,1,0:T(8,128)(2,1)} %all-to-all-done.refs_0_, ...), custom_call_target="tpu_custom_call" | custom-call | flops 1024 | bytes 1024 | tf_op jit(solution)/shard_map/pallas_call | solution.py:312
  65.2 6.7 %conditional.10 = (bf16[272,2048]{1,0:T(8,128)(2,1)}, bf16[136,2048]{1,0:T(8,128)(2,1)S(1)}, bf16[136,2048]{1,0:T(8,128)(2,1)}, bf16[136,2048]{1,0:T(8,128)(2,1)}, bf16[136,2048]{1,0:T(8,128)(2,1)S(1)}) conditional(s32[]{:T(128)} %convert_element_type.55, () %tuple.84, (bf16[272,2048]{1,0:T(8,128)(2,1)S(1)}, s32[5]{0:T(128)S(1)}) %tuple.86), branch_computations={%region_4.5_spmd, %region_5.6_spmd} | conditional | flops 1024 | bytes 4457552 | solution.py:389
  65.3 2.9 %collective-permute-done.2.sibling_ref = bf16[272,2048]{1,0:T(8,128)(2,1)} collective-permute-done((bf16[272,2048]{1,0:T(8,128)(2,1)S(1)}, bf16[272,2048]{1,0:T(8,128)(2,1)}, u32[]{:S(2)}, u32[]{:S(2)}) %collective-permute-start.2) | collective-permute-done | bytes 1114144 | tf_op jit(solution)/shard_map/cond/branch_1_fun/ppermute | solution.py:344
  68.2 3.8 %branch_1_fun.6 = (bf16[136,2048]{1,0:T(8,128)(2,1)S(1)}, bf16[136,2048]{1,0:T(8,128)(2,1)}, bf16[136,2048]{1,0:T(8,128)(2,1)}, bf16[136,2048]{1,0:T(8,128)(2,1)S(1)}) custom-call(s32[5]{0:T(128)S(1)} %get-tuple-element.53.info_ref, bf16[272,2048]{1,0:T(8,128)(2,1)S(1)} %get-tuple-element.52.mine_ref, bf16[272,2048]{1,0:T(8,128)(2,1)} %collective-permute-done.2.sibling_ref), custom_call_target="tpu_custom_call" | custom-call | flops 1024 | bytes 1024 | tf_op jit(solution)/shard_map/cond/branch_1_fun/pallas_call | solution.py:245
  72.0 4.0 %collective-permute-done.11.refs_2_ = bf16[136,2048]{1,0:T(8,128)(2,1)} collective-permute-done((bf16[136,2048]{1,0:T(8,128)(2,1)}, bf16[136,2048]{1,0:T(8,128)(2,1)}, u32[]{:S(2)}, u32[]{:S(2)}) %collective-permute-start.11) | collective-permute-done | bytes 557088 | tf_op jit(solution)/shard_map/ppermute | solution.py:344
  81.0 12.1 %shard_map.121 = (bf16[4,72,2048]{2,1,0:T(8,128)(2,1)}, bf16[1152,2048]{1,0:T(8,128)(2,1)}, bf16[1152,2048]{1,0:T(8,128)(2,1)}, bf16[1152,768]{1,0:T(8,128)(2,1)...) custom-call(s32[5]{0:T(128)S(1)} %pad_add_fusion.info_ref, ...), custom_call_target="tpu_custom_call", output_to_operand_aliasing={{1}: (10, {}), {2}: (11, {}), {3}: (12, {}), {4}: (13, {}),... | custom-call | flops 1024 | bytes 1024 | tf_op jit(solution)/shard_map/pallas_call | solution.py:312
  93.1 8.3 %collective-permute-done.15.mine_ref = bf16[272,2048]{1,0:T(8,128)(2,1)} collective-permute-done((bf16[272,2048]{1,0:T(8,128)(2,1)S(1)}, bf16[272,2048]{1,0:T(8,128)(2,1)}, u32[]{:S(2)}, u32[]{:S(2)}) %collective-permute-start.15) | collective-permute-done | bytes 1114144 | tf_op jit(solution)/shard_map/ppermute | solution.py:344
  101.4 7.0 %conditional.11 = (bf16[272,2048]{1,0:T(8,128)(2,1)}, bf16[136,2048]{1,0:T(8,128)(2,1)S(1)}, bf16[136,2048]{1,0:T(8,128)(2,1)}, bf16[136,2048]{1,0:T(8,128)(2,1)S(1)}, bf16[136,2048]{1,0:T(8,128)(2,1)S(1)}) conditional(s32[]{:T(128)} %convert_element_type.55, () %tuple.89, (bf16[272,2048]{1,0:T(8,128)(2,1)}, s32[5]{0:T(128)S(1)}) %tuple.90), branch_computations={%region_6.7_spmd, %region_7.8_spmd} | conditional | flops 1024 | bytes 4457552 | solution.py:389
  101.4 3.1 %collective-permute-done.3.sibling_ref = bf16[272,2048]{1,0:T(8,128)(2,1)} collective-permute-done((bf16[272,2048]{1,0:T(8,128)(2,1)}, bf16[272,2048]{1,0:T(8,128)(2,1)}, u32[]{:S(2)}, u32[]{:S(2)}) %collective-permute-start.3) | collective-permute-done | bytes 1114144 | tf_op jit(solution)/shard_map/cond/branch_1_fun/ppermute | solution.py:344
  104.5 3.9 %branch_1_fun.7 = (bf16[136,2048]{1,0:T(8,128)(2,1)S(1)}, bf16[136,2048]{1,0:T(8,128)(2,1)}, bf16[136,2048]{1,0:T(8,128)(2,1)S(1)}, bf16[136,2048]{1,0:T(8,128)(2,1)S(1)}) custom-call(s32[5]{0:T(128)S(1)} %get-tuple-element.59.info_ref, bf16[272,2048]{1,0:T(8,128)(2,1)} %get-tuple-element.58.mine_ref, bf16[272,2048]{1,0:T(8,128)(2,1)} %collective-permute-done.3.sibling_ref), custom_call_target="tpu_custom_call" | custom-call | flops 1024 | bytes 1024 | tf_op jit(solution)/shard_map/cond/branch_1_fun/pallas_call | solution.py:245
  112.0 11.9 %shard_map.122 = (bf16[4,72,2048]{2,1,0:T(8,128)(2,1)}, bf16[1152,2048]{1,0:T(8,128)(2,1)}, bf16[1152,2048]{1,0:T(8,128)(2,1)}, bf16[1152,768]{1,0:T(8,128)(2,1)...) custom-call(s32[5]{0:T(128)S(1)} %pad_add_fusion.info_ref, ...), custom_call_target="tpu_custom_call", output_to_operand_aliasing={{1}: (10, {}), {2}: (11, {}), {3}: (12, {}), {4}: (13, {}),... | custom-call | flops 1024 | bytes 1024 | tf_op jit(solution)/shard_map/pallas_call | solution.py:312
  124.2 10.7 %collective-permute-done.20.refs_2_ = bf16[136,2048]{1,0:T(8,128)(2,1)} collective-permute-done((bf16[136,2048]{1,0:T(8,128)(2,1)S(1)}, bf16[136,2048]{1,0:T(8,128)(2,1)}, u32[]{:S(2)}, u32[]{:S(2)}) %collective-permute-start.20) | collective-permute-done | bytes 557088 | tf_op jit(solution)/shard_map/ppermute | solution.py:344
  136.4 3.7 %all-to-all-start.1 = ((bf16[4,72,2048]{2,1,0:T(8,128)(2,1)}), bf16[4,72,2048]{2,1,0:T(8,128)(2,1)S(1)}, u32[]{:S(2)}, u32[]{:S(2)}) async-start(bf16[4,72,2048]{2,1,0:T(8,128)(2,1)} %get-tuple-element.294), calls=%async_computation.1 | async-start | bytes 2359296 | tf_op jit(solution)/shard_map/all_to_all | solution.py:354
  140.1 11.9 %shard_map.123 = (bf16[4,72,2048]{2,1,0:T(8,128)(2,1)}, bf16[1152,2048]{1,0:T(8,128)(2,1)}, bf16[1152,2048]{1,0:T(8,128)(2,1)}, bf16[1152,768]{1,0:T(8,128)(2,1)...) custom-call(s32[5]{0:T(128)S(1)} %pad_add_fusion.info_ref, ...), custom_call_target="tpu_custom_call", output_to_operand_aliasing={{1}: (10, {}), {2}: (11, {}), {3}: (12, {}), {4}: (13, {}),... | custom-call | flops 1024 | bytes 1024 | tf_op jit(solution)/shard_map/pallas_call | solution.py:312
  152.0 2.8 %all-to-all-done.1.refs_0_ = bf16[4,72,2048]{2,1,0:T(8,128)(2,1)S(1)} async-done(((bf16[4,72,2048]{2,1,0:T(8,128)(2,1)}), bf16[4,72,2048]{2,1,0:T(8,128)(2,1)S(1)}, u32[]{:S(2)}, u32[]{:S(2)}) %all-to-all-start.1) | async-done | bytes 1179680 | tf_op jit(solution)/shard_map/all_to_all | solution.py:354
  154.8 2.8 %shard_map.124 = (bf16[136,2048]{1,0:T(8,128)(2,1)}, bf16[136,2048]{1,0:T(8,128)(2,1)}) custom-call(s32[5]{0:T(128)S(1)} %pad_add_fusion.info_ref, bf16[272,2048]{1,0:T(8,128)(2,1)S(1)} %broadcast_select_fusion.mine_ref, bf16[272,2048]{1,0:T(8,128)(2,1)} %get-tuple-element.260.sibling_ref, bf16[4,72,2048]{2,1,0:T(8,128)(2,1)S(1)} %all-to-all-done.1.refs_0_), custom_call_target="tpu_custom_call" | custom-call | flops 1024 | bytes 1024 | tf_op jit(solution)/shard_map/pallas_call | solution.py:245
  157.6 3.4 %conditional.12 = (bf16[136,2048]{1,0:T(8,128)(2,1)S(1)}) conditional(s32[]{:T(128)} %convert_element_type.55, () %tuple.91, (bf16[136,2048]{1,0:T(8,128)(2,1)}, bf16[136,2048]{1,0:T(8,128)(2,1)}) %shard_map.124), branch_computations={%region_8.9_spmd, %region_9.10_spmd} | conditional | flops 1114112 | bytes 3899440 | solution.py:389
  157.6 2.2 collective-permute-done.4
  161.0 3.5 %all-to-all-start.2 = ((bf16[4,72,2048]{2,1,0:T(8,128)(2,1)}), bf16[4,72,2048]{2,1,0:T(8,128)(2,1)S(1)}, u32[]{:S(2)}, u32[]{:S(2)}) async-start(bf16[4,72,2048]{2,1,0:T(8,128)(2,1)} %get-tuple-element.317), calls=%async_computation.2 | async-start | bytes 2359296 | tf_op jit(solution)/shard_map/all_to_all | solution.py:354
  164.5 2.4 collective-permute-start.22
  166.9 8.1 %convolution_convert_fusion.2 = bf16[2048,768]{1,0:T(8,128)(2,1)} fusion(bf16[1152,2048]{1,0:T(8,128)(2,1)} %get-tuple-element.329, bf16[1152,768]{1,0:T(8,128)(2,1)S(1)} %copy-done.3), kind=kOutput, calls=%fused_computation.6 | convolution fusion | flops 3625451520 | bytes 9633792 | tf_op jit(solution)/shard_map/dot_general | solution.py:405
  175.0 5.1 %all-to-all-done.2.refs_0_ = bf16[4,72,2048]{2,1,0:T(8,128)(2,1)S(1)} async-done(((bf16[4,72,2048]{2,1,0:T(8,128)(2,1)}), bf16[4,72,2048]{2,1,0:T(8,128)(2,1)S(1)}, u32[]{:S(2)}, u32[]{:S(2)}) %all-to-all-start.2) | async-done | bytes 1179680 | tf_op jit(solution)/shard_map/all_to_all | solution.py:354
  181.9 3.0 %conditional.13 = (bf16[136,2048]{1,0:T(8,128)(2,1)}) conditional(s32[]{:T(128)} %convert_element_type.55, () %tuple.78, (bf16[136,2048]{1,0:T(8,128)(2,1)S(1)}, bf16[136,2048]{1,0:T(8,128)(2,1)S(1)}) %shard_map.125), branch_computations={%region_10.11_spmd, %region_11.12_spmd} | conditional | flops 1114112 | bytes 3899440 | solution.py:389
  184.9 3.8 %all-to-all-start.3 = ((bf16[4,72,2048]{2,1,0:T(8,128)(2,1)}), bf16[4,72,2048]{2,1,0:T(8,128)(2,1)S(1)}, u32[]{:S(2)}, u32[]{:S(2)}) async-start(bf16[4,72,2048]{2,1,0:T(8,128)(2,1)} %get-tuple-element.326), calls=%async_computation.3 | async-start | bytes 2359296 | tf_op jit(solution)/shard_map/all_to_all | solution.py:354
  190.8 8.9 %convolution_convert_fusion.1 = bf16[2048,768]{1,0:T(8,128)(2,1)} fusion(bf16[1152,2048]{1,0:T(8,128)(2,1)} %get-tuple-element.329, bf16[1152,768]{1,0:T(8,128)(2,1)} %get-tuple-element.330), kind=kOutput, calls=%fused_computation.5 | convolution fusion | flops 3625451520 | bytes 9633792 | tf_op jit(solution)/shard_map/dot_general | solution.py:405
  199.7 8.0 %convolution_convert_fusion = bf16[768,2048]{1,0:T(8,128)(2,1)} fusion(bf16[1152,768]{1,0:T(8,128)(2,1)S(1)} %copy-done.2, bf16[1152,2048]{1,0:T(8,128)(2,1)} %get-tuple-element.332), kind=kOutput, calls=%fused_computation.4 | convolution fusion | flops 3625451520 | bytes 9633792 | tf_op jit(solution)/shard_map/dot_general | solution.py:405
  207.7 4.2 %all-to-all-start.4 = ((bf16[4,72,2048]{2,1,0:T(8,128)(2,1)}), bf16[4,72,2048]{2,1,0:T(8,128)(2,1)S(1)}, u32[]{:S(2)}, u32[]{:S(2)}) async-start(bf16[4,72,2048]{2,1,0:T(8,128)(2,1)} %get-tuple-element.333), calls=%async_computation.4 | async-start | bytes 2359296 | tf_op jit(solution)/shard_map/all_to_all | solution.py:354
  211.8 2.8 %shard_map.127 = (bf16[136,2048]{1,0:T(8,128)(2,1)}, bf16[136,2048]{1,0:T(8,128)(2,1)}) custom-call(s32[5]{0:T(128)S(1)} %pad_add_fusion.info_ref, bf16[272,2048]{1,0:T(8,128)(2,1)} %collective-permute-done.8.mine_ref, bf16[272,2048]{1,0:T(8,128)(2,1)} %get-tuple-element.334.sibling_ref, bf16[4,72,2048]{2,1,0:T(8,128)(2,1)S(1)} %all-to-all-done.3.refs_0_), custom_call_target="tpu_custom_call" | custom-call | flops 1024 | bytes 1024 | tf_op jit(solution)/shard_map/pallas_call | solution.py:245
  214.6 4.2 %conditional.15 = (bf16[136,2048]{1,0:T(8,128)(2,1)}) conditional(s32[]{:T(128)} %convert_element_type.55, () %tuple.99, (bf16[136,2048]{1,0:T(8,128)(2,1)}, bf16[136,2048]{1,0:T(8,128)(2,1)}) %shard_map.127), branch_computations={%region_14.15_spmd, %region_15.16_spmd} | conditional | flops 1114112 | bytes 3899440 | solution.py:389
  214.7 2.2 collective-permute-done.7
  218.8 5.5 %collective-permute-start.24 = (bf16[136,2048]{1,0:T(8,128)(2,1)}, bf16[136,2048]{1,0:T(8,128)(2,1)S(1)}, u32[]{:S(2)}, u32[]{:S(2)}) collective-permute-start(bf16[136,2048]{1,0:T(8,128)(2,1)} %get-tuple-element.386), channel_id=1, source_target_pairs={{0,1},{1,0},{2,3},{3,2},{4,5},{5,4},{6,7},{7,6},{8,9},{9,8},{10,11... | collective-permute-start | bytes 1671176 | tf_op jit(solution)/shard_map/ppermute | solution.py:344
  224.3 2.3 all-to-all-done.4.refs_0_
  226.6 2.6 %shard_map.126 = (bf16[136,2048]{1,0:T(8,128)(2,1)S(1)}, bf16[136,2048]{1,0:T(8,128)(2,1)}) custom-call(s32[5]{0:T(128)S(1)} %pad_add_fusion.info_ref, bf16[272,2048]{1,0:T(8,128)(2,1)} %shard_map.119.mine_ref, bf16[272,2048]{1,0:T(8,128)(2,1)} %get-tuple-element.213.sibling_ref, bf16[4,72,2048]{2,1,0:T(8,128)(2,1)S(1)} %all-to-all-done.4.refs_0_), custom_call_target="tpu_custom_call" | custom-call | flops 1024 | bytes 1024 | tf_op jit(solution)/shard_map/pallas_call | solution.py:245
  229.2 2.3 conditional.14
  231.6 5.9 %collective-permute-done.24.refs_1_ = bf16[136,2048]{1,0:T(8,128)(2,1)S(1)} collective-permute-done((bf16[136,2048]{1,0:T(8,128)(2,1)}, bf16[136,2048]{1,0:T(8,128)(2,1)S(1)}, u32[]{:S(2)}, u32[]{:S(2)}) %collective-permute-start.24) | collective-permute-done | bytes 557088 | tf_op jit(solution)/shard_map/ppermute | solution.py:344
  (61 shorter events, 33.1 us)
Async XLA Ops:
  3.0 31.2 %collective-permute-start.9 = (bf16[272,2048]{1,0:T(8,128)(2,1)}, bf16[272,2048]{1,0:T(8,128)(2,1)}, u32[]{:S(2)}, u32[]{:S(2)}) collective-permute-start(bf16[272,2048]{1,0:T(8,128)(2,1)} %shard_map.119.mine_ref), channel_id=1, source_target_pairs={{1,2},{2,1},{5,6},{6,5},{9,10},{10,9},{13,14},{14,13},{17,18},{18,... | collective-permute-start | bytes 3342344 | tf_op jit(solution)/shard_map/ppermute | solution.py:348
  4.7 29.5 %collective-permute-start.8 = (bf16[272,2048]{1,0:T(8,128)(2,1)}, bf16[272,2048]{1,0:T(8,128)(2,1)}, u32[]{:S(2)}, u32[]{:S(2)}) collective-permute-start(bf16[272,2048]{1,0:T(8,128)(2,1)} %shard_map.119.mine_ref), channel_id=1, source_target_pairs={{0,1},{1,0},{2,3},{3,2},{4,5},{5,4},{6,7},{7,6},{8,9},{9,8},{10,11... | collective-permute-start | bytes 3342344 | tf_op jit(solution)/shard_map/ppermute | solution.py:344
  9.6 3.1 %collective-permute-start = (bf16[272,2048]{1,0:T(8,128)(2,1)}, bf16[272,2048]{1,0:T(8,128)(2,1)}, u32[]{:S(2)}, u32[]{:S(2)}) collective-permute-start(bf16[272,2048]{1,0:T(8,128)(2,1)} %get-tuple-element.40.mine_ref), channel_id=1, source_target_pairs={{0,4},{1,5},{2,6},{3,7},{4,0},{5,1},{6,2},{7,3},{8,12},{9,13},{10,... | collective-permute-start | bytes 3342344 | tf_op jit(solution)/shard_map/cond/branch_1_fun/ppermute | solution.py:344
  17.4 31.4 %all-to-all-start = ((bf16[4,136,2048]{2,1,0:T(8,128)(2,1)}), bf16[4,136,2048]{2,1,0:T(8,128)(2,1)}, u32[]{:S(2)}, u32[]{:S(2)}) async-start(bf16[4,136,2048]{2,1,0:T(8,128)(2,1)} %get-tuple-element.214), calls=%async_computation | async-start | bytes 4456448 | tf_op jit(solution)/shard_map/all_to_all | solution.py:354
  21.9 4.8 %copy-start.1 = (bf16[1,2048,768]{2,1,0:T(8,128)(2,1)S(1)}, bf16[1,2048,768]{2,1,0:T(8,128)(2,1)}, u32[]{:S(2)}) copy-start(bf16[1,2048,768]{2,1,0:T(8,128)(2,1)} %refs_4_.2) | copy-start | bytes 9437188
  34.2 29.9 %collective-permute-start.13 = (bf16[272,2048]{1,0:T(8,128)(2,1)}, bf16[272,2048]{1,0:T(8,128)(2,1)S(1)}, u32[]{:S(2)}, u32[]{:S(2)}) collective-permute-start(bf16[272,2048]{1,0:T(8,128)(2,1)} %collective-permute-done.9), channel_id=1, source_target_pairs={{1,0},{2,3},{5,4},{6,7},{9,8},{10,11},{13,12},{14,15},{17,16},{18,... | collective-permute-start | bytes 3342344 | tf_op jit(solution)/shard_map/ppermute | solution.py:348
  35.4 28.6 %collective-permute-start.14 = (bf16[272,2048]{1,0:T(8,128)(2,1)}, bf16[272,2048]{1,0:T(8,128)(2,1)S(1)}, u32[]{:S(2)}, u32[]{:S(2)}) collective-permute-start(bf16[272,2048]{1,0:T(8,128)(2,1)} %collective-permute-done.8.mine_ref), channel_id=1, source_target_pairs={{1,2},{2,1},{5,6},{6,5},{9,10},{10,9},{13,14},{14,13},{17,18},{18,... | collective-permute-start | bytes 3342344 | tf_op jit(solution)/shard_map/ppermute | solution.py:348
  36.7 3.2 %collective-permute-start.1 = (bf16[272,2048]{1,0:T(8,128)(2,1)}, bf16[272,2048]{1,0:T(8,128)(2,1)}, u32[]{:S(2)}, u32[]{:S(2)}) collective-permute-start(bf16[272,2048]{1,0:T(8,128)(2,1)} %get-tuple-element.43.mine_ref), channel_id=1, source_target_pairs={{0,4},{1,5},{2,6},{3,7},{4,0},{5,1},{6,2},{7,3},{8,12},{9,13},{10,... | collective-permute-start | bytes 3342344 | tf_op jit(solution)/shard_map/cond/branch_1_fun/ppermute | solution.py:344
  48.8 23.2 %collective-permute-start.10 = (bf16[136,2048]{1,0:T(8,128)(2,1)}, bf16[136,2048]{1,0:T(8,128)(2,1)}, u32[]{:S(2)}, u32[]{:S(2)}) collective-permute-start(bf16[136,2048]{1,0:T(8,128)(2,1)} %get-tuple-element.224), channel_id=1, source_target_pairs={{0,8},{1,9},{2,10},{3,11},{4,12},{5,13},{6,14},{7,15},{8,0},{9,1},... | collective-permute-start | bytes 1671176 | tf_op jit(solution)/shard_map/ppermute | solution.py:344
  50.2 25.8 %collective-permute-start.11 = (bf16[136,2048]{1,0:T(8,128)(2,1)}, bf16[136,2048]{1,0:T(8,128)(2,1)}, u32[]{:S(2)}, u32[]{:S(2)}) collective-permute-start(bf16[136,2048]{1,0:T(8,128)(2,1)} %get-tuple-element.225), channel_id=1, source_target_pairs={{0,16},{1,17},{2,18},{3,19},{4,20},{5,21},{6,22},{7,23},{8,24},{9,... | collective-permute-start | bytes 1671176 | tf_op jit(solution)/shard_map/ppermute | solution.py:344
  50.8 25.3 %collective-permute-start.12 = (bf16[136,2048]{1,0:T(8,128)(2,1)}, bf16[136,2048]{1,0:T(8,128)(2,1)}, u32[]{:S(2)}, u32[]{:S(2)}) collective-permute-start(bf16[136,2048]{1,0:T(8,128)(2,1)} %get-tuple-element.226), channel_id=1, source_target_pairs={{0,24},{1,25},{2,26},{3,27},{4,28},{5,29},{6,30},{7,31},{8,16},{9,... | collective-permute-start | bytes 1671176 | tf_op jit(solution)/shard_map/ppermute | solution.py:344
  64.1 1.0 copy-start.4
  65.2 3.0 %collective-permute-start.2 = (bf16[272,2048]{1,0:T(8,128)(2,1)S(1)}, bf16[272,2048]{1,0:T(8,128)(2,1)}, u32[]{:S(2)}, u32[]{:S(2)}) collective-permute-start(bf16[272,2048]{1,0:T(8,128)(2,1)S(1)} %get-tuple-element.52.mine_ref), channel_id=1, source_target_pairs={{0,4},{1,5},{2,6},{3,7},{4,0},{5,1},{6,2},{7,3},{8,12},{9,13},{10,... | collective-permute-start | bytes 3342344 | tf_op jit(solution)/shard_map/cond/branch_1_fun/ppermute | solution.py:344
  76.0 25.4 %collective-permute-start.15 = (bf16[272,2048]{1,0:T(8,128)(2,1)S(1)}, bf16[272,2048]{1,0:T(8,128)(2,1)}, u32[]{:S(2)}, u32[]{:S(2)}) collective-permute-start(bf16[272,2048]{1,0:T(8,128)(2,1)S(1)} %broadcast_select_fusion.mine_ref), channel_id=1, source_target_pairs={{0,1},{1,0},{2,3},{3,2},{4,5},{5,4},{6,7},{7,6},{8,9},{9,8},{10,11... | collective-permute-start | bytes 3342344 | tf_op jit(solution)/shard_map/ppermute | solution.py:344
  77.5 30.9 %collective-permute-start.16 = (bf16[136,2048]{1,0:T(8,128)(2,1)}, bf16[136,2048]{1,0:T(8,128)(2,1)}, u32[]{:S(2)}, u32[]{:S(2)}) collective-permute-start(bf16[136,2048]{1,0:T(8,128)(2,1)} %get-tuple-element.262), channel_id=1, source_target_pairs={{0,8},{1,9},{2,10},{3,11},{4,12},{5,13},{6,14},{7,15},{8,0},{9,1},... | collective-permute-start | bytes 1671176 | tf_op jit(solution)/shard_map/ppermute | solution.py:344
  78.7 29.7 %collective-permute-start.17 = (bf16[136,2048]{1,0:T(8,128)(2,1)}, bf16[136,2048]{1,0:T(8,128)(2,1)}, u32[]{:S(2)}, u32[]{:S(2)}) collective-permute-start(bf16[136,2048]{1,0:T(8,128)(2,1)} %get-tuple-element.263), channel_id=1, source_target_pairs={{0,16},{1,17},{2,18},{3,19},{4,20},{5,21},{6,22},{7,23},{8,24},{9,... | collective-permute-start | bytes 1671176 | tf_op jit(solution)/shard_map/ppermute | solution.py:344
  79.5 28.9 %collective-permute-start.18 = (bf16[136,2048]{1,0:T(8,128)(2,1)S(1)}, bf16[136,2048]{1,0:T(8,128)(2,1)}, u32[]{:S(2)}, u32[]{:S(2)}) collective-permute-start(bf16[136,2048]{1,0:T(8,128)(2,1)S(1)} %get-tuple-element.264), channel_id=1, source_target_pairs={{0,24},{1,25},{2,26},{3,27},{4,28},{5,29},{6,30},{7,31},{8,16},{9,... | collective-permute-start | bytes 1671176 | tf_op jit(solution)/shard_map/ppermute | solution.py:344
  101.4 3.1 %collective-permute-start.3 = (bf16[272,2048]{1,0:T(8,128)(2,1)}, bf16[272,2048]{1,0:T(8,128)(2,1)}, u32[]{:S(2)}, u32[]{:S(2)}) collective-permute-start(bf16[272,2048]{1,0:T(8,128)(2,1)} %get-tuple-element.58.mine_ref), channel_id=1, source_target_pairs={{0,4},{1,5},{2,6},{3,7},{4,0},{5,1},{6,2},{7,3},{8,12},{9,13},{10,... | collective-permute-start | bytes 3342344 | tf_op jit(solution)/shard_map/cond/branch_1_fun/ppermute | solution.py:344
  108.4 15.7 %collective-permute-start.19 = (bf16[136,2048]{1,0:T(8,128)(2,1)}, bf16[136,2048]{1,0:T(8,128)(2,1)S(1)}, u32[]{:S(2)}, u32[]{:S(2)}) collective-permute-start(bf16[136,2048]{1,0:T(8,128)(2,1)} %get-tuple-element.276), channel_id=1, source_target_pairs={{0,8},{1,9},{2,10},{3,11},{4,12},{5,13},{6,14},{7,15},{8,0},{9,1},... | collective-permute-start | bytes 1671176 | tf_op jit(solution)/shard_map/ppermute | solution.py:344
  110.0 25.0 %collective-permute-start.20 = (bf16[136,2048]{1,0:T(8,128)(2,1)S(1)}, bf16[136,2048]{1,0:T(8,128)(2,1)}, u32[]{:S(2)}, u32[]{:S(2)}) collective-permute-start(bf16[136,2048]{1,0:T(8,128)(2,1)S(1)} %get-tuple-element.277), channel_id=1, source_target_pairs={{0,16},{1,17},{2,18},{3,19},{4,20},{5,21},{6,22},{7,23},{8,24},{9,... | collective-permute-start | bytes 1671176 | tf_op jit(solution)/shard_map/ppermute | solution.py:344
  111.0 25.4 %collective-permute-start.21 = (bf16[136,2048]{1,0:T(8,128)(2,1)S(1)}, bf16[136,2048]{1,0:T(8,128)(2,1)}, u32[]{:S(2)}, u32[]{:S(2)}) collective-permute-start(bf16[136,2048]{1,0:T(8,128)(2,1)S(1)} %get-tuple-element.278), channel_id=1, source_target_pairs={{0,24},{1,25},{2,26},{3,27},{4,28},{5,29},{6,30},{7,31},{8,16},{9,... | collective-permute-start | bytes 1671176 | tf_op jit(solution)/shard_map/ppermute | solution.py:344
  124.2 16.0 %copy-start.6 = (bf16[136,2048]{1,0:T(8,128)(2,1)}, bf16[136,2048]{1,0:T(8,128)(2,1)S(1)}, u32[]{:S(2)}) copy-start(bf16[136,2048]{1,0:T(8,128)(2,1)S(1)} %collective-permute-done.19.refs_1_) | copy-start | bytes 1671172
  136.4 18.4 %all-to-all-start.1 = ((bf16[4,72,2048]{2,1,0:T(8,128)(2,1)}), bf16[4,72,2048]{2,1,0:T(8,128)(2,1)S(1)}, u32[]{:S(2)}, u32[]{:S(2)}) async-start(bf16[4,72,2048]{2,1,0:T(8,128)(2,1)} %get-tuple-element.294), calls=%async_computation.1 | async-start | bytes 2359296 | tf_op jit(solution)/shard_map/all_to_all | solution.py:354
  157.6 9.3 %copy-start.3 = (bf16[1152,768]{1,0:T(8,128)(2,1)S(1)}, bf16[1152,768]{1,0:T(8,128)(2,1)}, u32[]{:S(2)}) copy-start(bf16[1152,768]{1,0:T(8,128)(2,1)} %get-tuple-element.319) | copy-start | bytes 5308420
  157.6 2.2 collective-permute-start.4
  160.9 3.6 %copy-start.5 = (bf16[136,2048]{1,0:T(8,128)(2,1)}, bf16[136,2048]{1,0:T(8,128)(2,1)S(1)}, u32[]{:S(2)}) copy-start(bf16[136,2048]{1,0:T(8,128)(2,1)S(1)} %get-tuple-element.383) | copy-start | bytes 1671172
  161.0 19.1 %all-to-all-start.2 = ((bf16[4,72,2048]{2,1,0:T(8,128)(2,1)}), bf16[4,72,2048]{2,1,0:T(8,128)(2,1)S(1)}, u32[]{:S(2)}, u32[]{:S(2)}) async-start(bf16[4,72,2048]{2,1,0:T(8,128)(2,1)} %get-tuple-element.317), calls=%async_computation.2 | async-start | bytes 2359296 | tf_op jit(solution)/shard_map/all_to_all | solution.py:354
  164.5 43.2 %collective-permute-start.22 = (bf16[136,2048]{1,0:T(8,128)(2,1)}, bf16[136,2048]{1,0:T(8,128)(2,1)S(1)}, u32[]{:S(2)}, u32[]{:S(2)}) collective-permute-start(bf16[136,2048]{1,0:T(8,128)(2,1)} %copy-done.5), channel_id=1, source_target_pairs={{0,2},{1,3},{2,0},{3,1},{4,6},{5,7},{6,4},{7,5},{8,10},{9,11},{10,... | collective-permute-start | bytes 1671176 | tf_op jit(solution)/shard_map/ppermute | solution.py:344
  181.9 2.0 collective-permute-start.5
  184.9 22.8 %all-to-all-start.3 = ((bf16[4,72,2048]{2,1,0:T(8,128)(2,1)}), bf16[4,72,2048]{2,1,0:T(8,128)(2,1)S(1)}, u32[]{:S(2)}, u32[]{:S(2)}) async-start(bf16[4,72,2048]{2,1,0:T(8,128)(2,1)} %get-tuple-element.326), calls=%async_computation.3 | async-start | bytes 2359296 | tf_op jit(solution)/shard_map/all_to_all | solution.py:354
  188.7 11.0 %copy-start.2 = (bf16[1152,768]{1,0:T(8,128)(2,1)S(1)}, bf16[1152,768]{1,0:T(8,128)(2,1)}, u32[]{:S(2)}) copy-start(bf16[1152,768]{1,0:T(8,128)(2,1)} %get-tuple-element.331) | copy-start | bytes 5308420
  188.7 23.2 %collective-permute-start.23 = (bf16[136,2048]{1,0:T(8,128)(2,1)}, bf16[136,2048]{1,0:T(8,128)(2,1)S(1)}, u32[]{:S(2)}, u32[]{:S(2)}) collective-permute-start(bf16[136,2048]{1,0:T(8,128)(2,1)} %get-tuple-element.384), channel_id=1, source_target_pairs={{0,3},{1,2},{2,1},{3,0},{4,7},{5,6},{6,5},{7,4},{8,11},{9,10},{10,... | collective-permute-start | bytes 1671176 | tf_op jit(solution)/shard_map/ppermute | solution.py:344
  207.7 18.9 %all-to-all-start.4 = ((bf16[4,72,2048]{2,1,0:T(8,128)(2,1)}), bf16[4,72,2048]{2,1,0:T(8,128)(2,1)S(1)}, u32[]{:S(2)}, u32[]{:S(2)}) async-start(bf16[4,72,2048]{2,1,0:T(8,128)(2,1)} %get-tuple-element.333), calls=%async_computation.4 | async-start | bytes 2359296 | tf_op jit(solution)/shard_map/all_to_all | solution.py:354
  214.6 2.2 collective-permute-start.7
  218.8 18.6 %collective-permute-start.24 = (bf16[136,2048]{1,0:T(8,128)(2,1)}, bf16[136,2048]{1,0:T(8,128)(2,1)S(1)}, u32[]{:S(2)}, u32[]{:S(2)}) collective-permute-start(bf16[136,2048]{1,0:T(8,128)(2,1)} %get-tuple-element.386), channel_id=1, source_target_pairs={{0,1},{1,0},{2,3},{3,2},{4,5},{5,4},{6,7},{7,6},{8,9},{9,8},{10,11... | collective-permute-start | bytes 1671176 | tf_op jit(solution)/shard_map/ppermute | solution.py:344
  229.2 8.2 %copy-start = (s32[128,8]{0,1:T(8,128)S(1)}, s32[128,8]{0,1:T(8,128)}, u32[]{:S(2)}) copy-start(s32[128,8]{0,1:T(8,128)} %param.26) | copy-start | bytes 12292
  229.2 2.2 collective-permute-start.6

commit v3 on v2

--- a/solution.py
+++ b/solution.py
@@ -140,7 +140,7 @@
     picks = jnp.concatenate([pick(rank, j, at.group) for j in range(targets)], axis=0)
     step = next(s for s in (1024, 512, 256, 128) if width % s == 0)
     for start in range(0, width, step):
-        rows = [rets_ref[chips[j], :, start : start + step] for j in range(targets)]
+        rows = [rets_ref[chips[j], 0, :, start : start + step] for j in range(targets)]
         total = lax.dot_general(
             picks, jnp.concatenate(rows, axis=0), TN, preferred_element_type=F32
         )
@@ -150,7 +150,7 @@
     for n in range(width // LANES):
         keep = send = jnp.zeros((TAIL, LANES), F32)
         if n < targets:
-            tail = rets_ref[chips[n], at.group - 8 :, :LANES]
+            tail = rets_ref[chips[n], 0, at.group - 8 :, :LANES]
             line = jnp.dot(tail, pick(rank, n, LANES), preferred_element_type=F32)[7:8]
             keep = jnp.where(row == 0, line[:, :tokens], keep)
             send = jnp.where(row == 1, line[:, tokens:], send)
@@ -218,13 +218,13 @@
         for i in range(sources):
             chip = i if joined else info_ref[1 + i] // 2
             part = slice(i * group, (i + 1) * group)
-            ret_ref[chip, :, cols] = dx[part, :].astype(BF16)
+            ret_ref[chip, 0, :, cols] = dx[part, :].astype(BF16)
             if start == 0:
                 grads = lax.dot_general(
                     pg[part, :], eye(group), TN, preferred_element_type=F32
                 )[:1]
                 tail = jnp.where(last, grads, dx[(i + 1) * group - 8 : (i + 1) * group, :LANES])
-                ret_ref[chip, group - 8 :, :LANES] = tail.astype(BF16)
+                ret_ref[chip, 0, group - 8 :, :LANES] = tail.astype(BF16)
 
 
 def whole(shape):
@@ -283,17 +283,21 @@
     return out[0] if joined else out
 
 
-def combine(at, info, mine, sibling, rets):
+def combine(at, info, mine, sibling, rets, slot):
     height, width = mine.shape
     tokens = (height - EXTRA) // 2
     shapes = [jax.ShapeDtypeStruct((tokens + TAIL, width), BF16)] * 2
     kernel = functools.partial(combine_kernel, at, rets.shape[0])
     extra = pl.BlockSpec((EXTRA, width), lambda *_: (2 * tokens // EXTRA, 0))
-    specs = [extra, extra, whole(rets.shape)]
+    targets, _, group, _ = rets.shape
+    ret = pl.BlockSpec(
+        (targets, 1, group, width), lambda *_: (0, slot, 0, 0), pipeline_mode=pl.Buffered(1)
+    )
+    specs = [extra, extra, ret]
     return call(kernel, info, [mine, sibling, rets], shapes, specs, 24)
 
 
-def expert(at, info, msgs, weights, saved, chunk, chunks):
+def expert(at, info, msgs, weights, saved, chunk, chunks, slot, slots, ret):
     sources = sum(m.size // (at.message * m.shape[-1]) for m in msgs)
     width = msgs[0].shape[-1]
     hidden = weights[0].shape[2]
@@ -302,15 +306,23 @@
         pl.BlockSpec((rows, n), lambda *_: (chunk, 0), pipeline_mode=pl.Buffered(1))
         for n in (width, hidden)
     )
-    out_shape = [jax.ShapeDtypeStruct((sources, at.group, width), BF16)]
-    out_specs = [whole(s.shape) for s in out_shape] + [wide_spec] * 2 + [thin_spec] * 3
+    out_shape = [jax.ShapeDtypeStruct((sources, slots, at.group, width), BF16)]
+    ret_spec = pl.BlockSpec(
+        (sources, 1, at.group, width), lambda *_: (0, slot, 0, 0), pipeline_mode=pl.Buffered(1)
+    )
+    out_specs = [ret_spec] + [wide_spec] * 2 + [thin_spec] * 3
     out_shape += [jax.ShapeDtypeStruct((chunks * rows, width), BF16)] * 2
     out_shape += [jax.ShapeDtypeStruct((chunks * rows, hidden), BF16)] * 3
     in_specs = [SMEM] + [whole(m.shape) for m in msgs]
-    in_specs += [pl.BlockSpec(memory_space=pl.ANY)] * (5 + len(saved))
-    aliases = {1 + len(msgs) + 5 + i: 1 + i for i in range(len(saved))}
+    first = 1 + len(msgs) + 5
+    aliases = {first + i: 1 + i for i in range(len(saved))}
+    kept = list(saved)
+    if ret is not None:
+        aliases[first + len(saved)] = 0
+        kept.append(ret)
+    in_specs += [pl.BlockSpec(memory_space=pl.ANY)] * (5 + len(kept))
     out = pl.pallas_call(
-        functools.partial(expert_kernel, at, sources, len(saved)),
+        functools.partial(expert_kernel, at, sources, len(kept)),
         grid=(1,),
         in_specs=in_specs,
         out_specs=out_specs,
@@ -320,7 +332,7 @@
         + [pltpu.VMEM((rows + 8, hidden), F32), pltpu.SemaphoreType.DMA((5,))],
         compiler_params=params(60),
         cost_estimate=COST,
-    )(info, *msgs, *weights, *saved)
+    )(info, *msgs, *weights, *kept)
     return out[0], out[1:]
 
 
@@ -375,11 +387,11 @@
         down, gate, up, _ = fence(w_down, w_gate, w_up, token)
         return [w_gate, w_up, down[0].T, gate[0].T, up[0].T]
 
-    def work(c, msgs, weights, saved):
-        return expert(at, info, msgs, weights, saved, c, locals_)
-
-    def merge(block, sister, ret):
-        return combine(at, info, block, sister, ret)
+    def work(c, msgs, weights, saved, slot=0, slots=1, ret=None):
+        return expert(at, info, msgs, weights, saved, c, locals_, slot, slots, ret)
+
+    def merge(block, sister, ret, slot=0):
+        return combine(at, info, block, sister, ret, slot)
 
     (go,) = fence(node < nodes)
 
@@ -395,11 +407,15 @@
 
         return at_once(step, block)
 
-    def home(parts):
-        def step(keep, other):
-            return (keep.astype(F32) + swap(other, 1).astype(F32)).astype(BF16)
-
-        return at_once(step, *parts)
+    def home(*parts):
+        def step(parts):
+            moved = [swap(other, 1) for _, other in parts]
+            return [
+                (keep.astype(F32) + other.astype(F32)).astype(BF16)
+                for (keep, _), other in zip(parts, moved)
+            ]
+
+        return at_once(step, parts)
 
     def wgrad(a, b):
         return lax.dot_general(a, b, TN, preferred_element_type=F32).astype(BF16)
@@ -422,7 +438,7 @@
         p1, m2, b2, r0, saved = fence(p1, m2, b2, r0, saved)
         p2 = send(m2)
         b3 = swap(b2, 0, 1)
-        r1, saved = work(1, p1, weights, saved)
+        r1, saved = work(1, p1, weights, saved, 0, 2)
         b3, r1 = fence(b3, r1)
         s3, m3 = prepare(b3)
         p2, m3, r1, saved = fence(p2, m3, r1, saved)
@@ -430,25 +446,23 @@
         r2, saved = work(2, p2, weights, saved)
         p3, r2, saved = fence(p3, r2, saved)
         r2 = back(r2)
-        r3, saved = work(3, p3, weights, saved)
-        r2, r3, saved = fence(r2, r3, saved)
-        t2 = home(merge(b2, s2, r2))
-        t2, r3, saved = fence(t2, r3, saved)
-        r3 = back(r3)
+        r13, saved = work(3, p3, weights, saved, 1, 2, r1)
+        r2, r13, saved = fence(r2, r13, saved)
+        (t2,) = home(merge(b2, s2, r2))
+        t2, r13, saved = fence(t2, r13, saved)
+        r13 = back(r13)
         t2 = swap(t2, 0, 2)
         x_all, dy_all, hp, du, dg = saved
-        gate_wgrad = wgrad(x_all, dg)
-        r3, gate_wgrad = fence(r3, gate_wgrad)
-        t3 = home(merge(b3, s3, r3))
-        t3, r0, r1, x_all, dy_all, hp, du = fence(t3, r0, r1, x_all, dy_all, hp, du)
+        gate_wgrad, up_wgrad = wgrad(x_all, dg), wgrad(x_all, du)
+        r13, gate_wgrad, up_wgrad = fence(r13, gate_wgrad, up_wgrad)
+        t3, t1 = home(merge(b3, s3, r13, 1), merge(b1, s1, r13, 0))
+        t3, t1, t2, r0, dy_all, hp = fence(t3, t1, t2, r0, dy_all, hp)
         t3 = swap(t3, 0, 3)
-        r1 = back(r1)
-        up_wgrad, down_wgrad = wgrad(x_all, du), wgrad(hp, dy_all)
-        r1, r0, t2, up_wgrad, down_wgrad = fence(r1, r0, t2, up_wgrad, down_wgrad)
+        t1 = swap(t1, 0, 1)
         r0 = back(r0)
-        r1, t3 = fence(r1, t3)
-        t1 = swap(home(merge(b1, s1, r1)), 0, 1)
-        t0 = home(merge(b0, s0, r0))
+        down_wgrad = wgrad(hp, dy_all)
+        r0, down_wgrad = fence(r0, down_wgrad)
+        (t0,) = home(merge(b0, s0, r0))
         t0, t1, t2, t3 = fence(t0, t1, t2, t3)
         totals = [t0, t1, t2, t3]
     else:
@@ -457,7 +471,7 @@
             block = swap(payload, 0, c) if c else payload
             sister, msgs = prepare(block)
             ret, saved = work(c, send(msgs), weights, saved)
-            total = home(merge(block, sister, back(ret)))
+            (total,) = home(merge(block, sister, back(ret)))
             totals.append(swap(total, 0, c) if c else total)
         x_all, dy_all, hp, du, dg = saved
         gate_wgrad, up_wgrad = wgrad(x_all, dg), wgrad(x_all, du)

time: 243 us -> 237 us (0.975)
  starting transfers between devices: 51.1 us -> 43.5 us
  waiting for transfers between devices: 66.1 us -> 71.2 us
  other arithmetic: 4.5 us -> 1.56 us
    all_to_all x5 -> x4, waiting for transfers between devices: 14.8 us -> 20.7 us  [back(): lax.all_to_all(value, 'node', split_axis=0, concat_axis=0, axis_index_gro...]
    all_to_all x5 -> x4, starting transfers between devices: 19.7 us -> 16 us  [back(): lax.all_to_all(value, 'node', split_axis=0, concat_axis=0, axis_index_gro...]
    ppermute x22, starting transfers between devices: 27.1 us -> 23.6 us  [swap(): return lax.ppermute(value, both, pairs)]
    convert_element_type x4, other arithmetic: 4.3 us -> 1.36 us  [step(): (keep.astype(F32) + other.astype(F32)).astype(BF16)]
  transfers between devices with their start and end apart: 30 -> 29, of which waited for: 18 -> 19; matrix products, arithmetic and copies ran while one was open for 17% -> 16% of each run, Pallas kernels for 30% -> 31%
where the time goes in v3:
time: 237 us; the launch traced here: 233 us
  Pallas kernels  77.5 us (33%)
  waiting for transfers between devices  71.2 us (30%)
  starting transfers between devices  43.5 us (18%)
  matrix products  23.5 us (10%)
  local copies, waits for them, and re-layouts  14.3 us (6%)
    ppermute x22, waiting for transfers between devices, swap(): return lax.ppermute(value, both, pairs)  50.4 us
    pallas_call x4, Pallas kernels, expert(): pl.pallas_call(functools.partial(expert_kernel, at, sources, len(kept)),...  49.5 us
    pallas_call x10, Pallas kernels, call(): pl.pallas_call(kernel, grid=(1,), in_specs=([SMEM] if info is not None el...  27.9 us
    ppermute x22, starting transfers between devices, swap(): return lax.ppermute(value, both, pairs)  23.6 us
    dot_general x3, matrix products, wgrad(): return lax.dot_general(a, b, TN, preferred_element_type=F32).astype(BF16)  23.5 us
    all_to_all x4, waiting for transfers between devices, back(): lax.all_to_all(value, 'node', split_axis=0, concat_axis=0, axis_index_gro...  20.7 us
    all_to_all x4, starting transfers between devices, back(): lax.all_to_all(value, 'node', split_axis=0, concat_axis=0, axis_index_gro...  16 us
    optimization_barrier x3, local copies, waits for them, and re-layouts, fence(): return lax.optimization_barrier(values)  12.3 us
  transfers between devices with their start and end apart: 29, of which 19 were waited for; matrix products, arithmetic and copies ran while one was open for 16% of the time, Pallas kernels for 31%

profile of v3, /device:TPU:0, one launch (start us, length us, event | category | flops | bytes accessed | tf_op | source)
XLA Modules:
  0.0 232.6 jit_solution(17400521779841261405)
XLA Ops:
  0.6 2.3 shard_map.119.mine_ref
  4.6 4.9 %collective-permute-start.8 = (bf16[272,2048]{1,0:T(8,128)(2,1)}, bf16[272,2048]{1,0:T(8,128)(2,1)}, u32[]{:S(2)}, u32[]{:S(2)}) collective-permute-start(bf16[272,2048]{1,0:T(8,128)(2,1)} %shard_map.119.mine_ref), channel_id=1, source_target_pairs={{0,1},{1,0},{2,3},{3,2},{4,5},{5,4},{6,7},{7,6},{8,9},{9,8},{10,11... | collective-permute-start | bytes 3342344 | tf_op jit(solution)/shard_map/ppermute | solution.py:356
  9.6 7.6 %conditional.7 = (bf16[272,2048]{1,0:T(8,128)(2,1)}, bf16[4,136,2048]{2,1,0:T(8,128)(2,1)}) conditional(s32[]{:T(128)} %convert_element_type.54, () %tuple.73, (bf16[272,2048]{1,0:T(8,128)(2,1)}, s32[5]{0:T(128)S(1)}) %tuple.74), branch_computations={%region_0.0_spmd, %region_1.0_spmd} | conditional | flops 1024 | bytes 4457528 | solution.py:401
  9.6 3.1 %collective-permute-done.sibling_ref = bf16[272,2048]{1,0:T(8,128)(2,1)} collective-permute-done((bf16[272,2048]{1,0:T(8,128)(2,1)}, bf16[272,2048]{1,0:T(8,128)(2,1)}, u32[]{:S(2)}, u32[]{:S(2)}) %collective-permute-start) | collective-permute-done | bytes 1114144 | tf_op jit(solution)/shard_map/cond/branch_1_fun/ppermute | solution.py:356
  12.7 4.5 %branch_1_fun.4 = bf16[4,136,2048]{2,1,0:T(8,128)(2,1)} custom-call(s32[5]{0:T(128)S(1)} %get-tuple-element.36.info_ref, bf16[272,2048]{1,0:T(8,128)(2,1)} %get-tuple-element.35.mine_ref, bf16[272,2048]{1,0:T(8,128)(2,1)} %collective-permute-done.sibling_ref), custom_call_target="tpu_custom_call" | custom-call | flops 1024 | bytes 1024 | tf_op jit(solution)/shard_map/cond/branch_1_fun/pallas_call | solution.py:245
  17.3 4.5 %all-to-all-start = ((bf16[4,136,2048]{2,1,0:T(8,128)(2,1)}), bf16[4,136,2048]{2,1,0:T(8,128)(2,1)}, u32[]{:S(2)}, u32[]{:S(2)}) async-start(bf16[4,136,2048]{2,1,0:T(8,128)(2,1)} %get-tuple-element.209), calls=%async_computation | async-start | bytes 4456448 | tf_op jit(solution)/shard_map/all_to_all | solution.py:366
  21.8 4.8 %copy.29 = bf16[1,768,2048]{1,2,0:T(8,128)(2,1)} copy(bf16[1,768,2048]{2,1,0:T(8,128)(2,1)} %param.28) | data formatting | bytes 6291456 | tf_op jit(solution)/shard_map/optimization_barrier | solution.py:371
  26.6 2.9 %copy.30 = bf16[1,2048,768]{1,2,0:T(8,128)(2,1)} copy(bf16[1,2048,768]{2,1,0:T(8,128)(2,1)S(1)} %copy-done.1) | data formatting | bytes 6291456 | tf_op jit(solution)/shard_map/optimization_barrier | solution.py:371
  29.4 4.6 %copy.31 = bf16[1,2048,768]{1,2,0:T(8,128)(2,1)} copy(bf16[1,2048,768]{2,1,0:T(8,128)(2,1)} %refs_5_.2) | data formatting | bytes 6291456 | tf_op jit(solution)/shard_map/optimization_barrier | solution.py:371
  36.3 7.5 %conditional.8 = (bf16[272,2048]{1,0:T(8,128)(2,1)}, bf16[136,2048]{1,0:T(8,128)(2,1)S(1)}, bf16[136,2048]{1,0:T(8,128)(2,1)}, bf16[136,2048]{1,0:T(8,128)(2,1)}, bf16[136,2048]{1,0:T(8,128)(2,1)}) conditional(s32[]{:T(128)} %convert_element_type.54, () %tuple.76, (bf16[272,2048]{1,0:T(8,128)(2,1)}, s32[5]{0:T(128)S(1)}) %tuple.79), branch_computations={%region_2.0_spmd, %region_3.0_spmd} | conditional | flops 1024 | bytes 4457552 | solution.py:401
  36.5 3.0 %collective-permute-done.1.sibling_ref = bf16[272,2048]{1,0:T(8,128)(2,1)} collective-permute-done((bf16[272,2048]{1,0:T(8,128)(2,1)}, bf16[272,2048]{1,0:T(8,128)(2,1)}, u32[]{:S(2)}, u32[]{:S(2)}) %collective-permute-start.1) | collective-permute-done | bytes 1114144 | tf_op jit(solution)/shard_map/cond/branch_1_fun/ppermute | solution.py:356
  39.5 4.3 %branch_1_fun.5 = (bf16[136,2048]{1,0:T(8,128)(2,1)S(1)}, bf16[136,2048]{1,0:T(8,128)(2,1)}, bf16[136,2048]{1,0:T(8,128)(2,1)}, bf16[136,2048]{1,0:T(8,128)(2,1)}) custom-call(s32[5]{0:T(128)S(1)} %get-tuple-element.41.info_ref, bf16[272,2048]{1,0:T(8,128)(2,1)} %get-tuple-element.40.mine_ref, bf16[272,2048]{1,0:T(8,128)(2,1)} %collective-permute-done.1.sibling_ref), custom_call_target="tpu_custom_call" | custom-call | flops 1024 | bytes 1024 | tf_op jit(solution)/shard_map/cond/branch_1_fun/pallas_call | solution.py:245
  43.8 4.8 %all-to-all-done.refs_0_ = bf16[4,136,2048]{2,1,0:T(8,128)(2,1)} async-done(((bf16[4,136,2048]{2,1,0:T(8,128)(2,1)}), bf16[4,136,2048]{2,1,0:T(8,128)(2,1)}, u32[]{:S(2)}, u32[]{:S(2)}) %all-to-all-start) | async-done | bytes 2228256 | tf_op jit(solution)/shard_map/all_to_all | solution.py:366
  52.1 11.7 %shard_map.120 = (bf16[4,1,72,2048]{3,2,1,0:T(8,128)(2,1)}, bf16[1152,2048]{1,0:T(8,128)(2,1)}, bf16[1152,2048]{1,0:T(8,128)(2,1)}, bf16[1152,768]{1,0:T(8,128)(...) custom-call(s32[5]{0:T(128)S(1)} %pad_add_fusion.info_ref, bf16[4,136,2048]{2,1,0:T(8,128)(2,1)} %all-to-all-done.refs_0_, ...), custom_call_target="tpu_custom_call" | custom-call | flops 1024 | bytes 1024 | tf_op jit(solution)/shard_map/pallas_call | solution.py:324
  65.0 6.7 %conditional.9 = (bf16[272,2048]{1,0:T(8,128)(2,1)}, bf16[136,2048]{1,0:T(8,128)(2,1)S(1)}, bf16[136,2048]{1,0:T(8,128)(2,1)}, bf16[136,2048]{1,0:T(8,128)(2,1)}, bf16[136,2048]{1,0:T(8,128)(2,1)S(1)}) conditional(s32[]{:T(128)} %convert_element_type.54, () %tuple.81, (bf16[272,2048]{1,0:T(8,128)(2,1)S(1)}, s32[5]{0:T(128)S(1)}) %tuple.83), branch_computations={%region_4.5_spmd, %region_5.6_spmd} | conditional | flops 1024 | bytes 4457552 | solution.py:401
  65.1 2.9 %collective-permute-done.2.sibling_ref = bf16[272,2048]{1,0:T(8,128)(2,1)} collective-permute-done((bf16[272,2048]{1,0:T(8,128)(2,1)S(1)}, bf16[272,2048]{1,0:T(8,128)(2,1)}, u32[]{:S(2)}, u32[]{:S(2)}) %collective-permute-start.2) | collective-permute-done | bytes 1114144 | tf_op jit(solution)/shard_map/cond/branch_1_fun/ppermute | solution.py:356
  68.0 3.8 %branch_1_fun.6 = (bf16[136,2048]{1,0:T(8,128)(2,1)S(1)}, bf16[136,2048]{1,0:T(8,128)(2,1)}, bf16[136,2048]{1,0:T(8,128)(2,1)}, bf16[136,2048]{1,0:T(8,128)(2,1)S(1)}) custom-call(s32[5]{0:T(128)S(1)} %get-tuple-element.47.info_ref, bf16[272,2048]{1,0:T(8,128)(2,1)S(1)} %get-tuple-element.46.mine_ref, bf16[272,2048]{1,0:T(8,128)(2,1)} %collective-permute-done.2.sibling_ref), custom_call_target="tpu_custom_call" | custom-call | flops 1024 | bytes 1024 | tf_op jit(solution)/shard_map/cond/branch_1_fun/pallas_call | solution.py:245
  71.8 4.1 %collective-permute-done.11.refs_2_ = bf16[136,2048]{1,0:T(8,128)(2,1)} collective-permute-done((bf16[136,2048]{1,0:T(8,128)(2,1)}, bf16[136,2048]{1,0:T(8,128)(2,1)}, u32[]{:S(2)}, u32[]{:S(2)}) %collective-permute-start.11) | collective-permute-done | bytes 557088 | tf_op jit(solution)/shard_map/ppermute | solution.py:356
  80.6 13.0 %shard_map.121 = (bf16[4,2,72,2048]{3,2,1,0:T(8,128)(2,1)}, bf16[1152,2048]{1,0:T(8,128)(2,1)}, bf16[1152,2048]{1,0:T(8,128)(2,1)}, bf16[1152,768]{1,0:T(8,128)(...) custom-call(s32[5]{0:T(128)S(1)} %pad_add_fusion.info_ref, ...), custom_call_target="tpu_custom_call", output_to_operand_aliasing={{1}: (10, {}), {2}: (11, {}), {3}: (12, {}), {4}: (13, {}),... | custom-call | flops 1024 | bytes 1024 | tf_op jit(solution)/shard_map/pallas_call | solution.py:324
  93.7 7.4 %collective-permute-done.15.mine_ref = bf16[272,2048]{1,0:T(8,128)(2,1)} collective-permute-done((bf16[272,2048]{1,0:T(8,128)(2,1)S(1)}, bf16[272,2048]{1,0:T(8,128)(2,1)}, u32[]{:S(2)}, u32[]{:S(2)}) %collective-permute-start.15) | collective-permute-done | bytes 1114144 | tf_op jit(solution)/shard_map/ppermute | solution.py:356
  101.1 7.0 %conditional.10 = (bf16[272,2048]{1,0:T(8,128)(2,1)}, bf16[136,2048]{1,0:T(8,128)(2,1)S(1)}, bf16[136,2048]{1,0:T(8,128)(2,1)}, bf16[136,2048]{1,0:T(8,128)(2,1)S(1)}, bf16[136,2048]{1,0:T(8,128)(2,1)S(1)}) conditional(s32[]{:T(128)} %convert_element_type.54, () %tuple.86, (bf16[272,2048]{1,0:T(8,128)(2,1)}, s32[5]{0:T(128)S(1)}) %tuple.87), branch_computations={%region_6.7_spmd, %region_7.8_spmd} | conditional | flops 1024 | bytes 4457552 | solution.py:401
  101.1 3.1 %collective-permute-done.3.sibling_ref = bf16[272,2048]{1,0:T(8,128)(2,1)} collective-permute-done((bf16[272,2048]{1,0:T(8,128)(2,1)}, bf16[272,2048]{1,0:T(8,128)(2,1)}, u32[]{:S(2)}, u32[]{:S(2)}) %collective-permute-start.3) | collective-permute-done | bytes 1114144 | tf_op jit(solution)/shard_map/cond/branch_1_fun/ppermute | solution.py:356
  104.2 3.9 %branch_1_fun.7 = (bf16[136,2048]{1,0:T(8,128)(2,1)S(1)}, bf16[136,2048]{1,0:T(8,128)(2,1)}, bf16[136,2048]{1,0:T(8,128)(2,1)S(1)}, bf16[136,2048]{1,0:T(8,128)(2,1)S(1)}) custom-call(s32[5]{0:T(128)S(1)} %get-tuple-element.53.info_ref, bf16[272,2048]{1,0:T(8,128)(2,1)} %get-tuple-element.52.mine_ref, bf16[272,2048]{1,0:T(8,128)(2,1)} %collective-permute-done.3.sibling_ref), custom_call_target="tpu_custom_call" | custom-call | flops 1024 | bytes 1024 | tf_op jit(solution)/shard_map/cond/branch_1_fun/pallas_call | solution.py:245
  111.6 11.9 %shard_map.122 = (bf16[4,1,72,2048]{3,2,1,0:T(8,128)(2,1)}, bf16[1152,2048]{1,0:T(8,128)(2,1)}, bf16[1152,2048]{1,0:T(8,128)(2,1)}, bf16[1152,768]{1,0:T(8,128)(...) custom-call(s32[5]{0:T(128)S(1)} %pad_add_fusion.info_ref, ...), custom_call_target="tpu_custom_call", output_to_operand_aliasing={{1}: (10, {}), {2}: (11, {}), {3}: (12, {}), {4}: (13, {}),... | custom-call | flops 1024 | bytes 1024 | tf_op jit(solution)/shard_map/pallas_call | solution.py:324
  123.8 10.9 %collective-permute-done.20.refs_2_ = bf16[136,2048]{1,0:T(8,128)(2,1)} collective-permute-done((bf16[136,2048]{1,0:T(8,128)(2,1)S(1)}, bf16[136,2048]{1,0:T(8,128)(2,1)}, u32[]{:S(2)}, u32[]{:S(2)}) %collective-permute-start.20) | collective-permute-done | bytes 557088 | tf_op jit(solution)/shard_map/ppermute | solution.py:356
  136.0 3.9 %all-to-all-start.1 = ((bf16[4,1,72,2048]{3,2,1,0:T(8,128)(2,1)}), bf16[4,1,72,2048]{3,2,1,0:T(8,128)(2,1)S(1)}, u32[]{:S(2)}, u32[]{:S(2)}) async-start(bf16[4,1,72,2048]{3,2,1,0:T(8,128)(2,1)} %get-tuple-element.289), calls=%async_computation.1 | async-start | bytes 2359296 | tf_op jit(solution)/shard_map/all_to_all | solution.py:366
  139.9 12.9 %shard_map.123 = (bf16[4,2,72,2048]{3,2,1,0:T(8,128)(2,1)}, bf16[1152,2048]{1,0:T(8,128)(2,1)}, bf16[1152,2048]{1,0:T(8,128)(2,1)}, bf16[1152,768]{1,0:T(8,128)(...) custom-call(s32[5]{0:T(128)S(1)} %pad_add_fusion.info_ref, ...), custom_call_target="tpu_custom_call", output_to_operand_aliasing={{1}: (10, {}), {2}: (11, {}), {3}: (12, {}), {4}: (13, {}),... | custom-call | flops 1024 | bytes 1024 | tf_op jit(solution)/shard_map/pallas_call | solution.py:324
  152.8 1.8 all-to-all-done.1.refs_0_
  154.6 1.8 shard_map.124
  156.4 3.0 %conditional.11 = (bf16[136,2048]{1,0:T(8,128)(2,1)}) conditional(s32[]{:T(128)} %convert_element_type.54, () %tuple.88, (bf16[136,2048]{1,0:T(8,128)(2,1)S(1)}, bf16[136,2048]{1,0:T(8,128)(2,1)S(1)}) %shard_map.124), branch_computations={%region_8.9_spmd, %region_9.10_spmd} | conditional | flops 1114112 | bytes 3899440 | solution.py:401
  156.5 1.9 collective-permute-done.4
  159.4 3.8 %all-to-all-start.2 = ((bf16[4,2,72,2048]{3,2,1,0:T(8,128)(2,1)}), bf16[4,2,72,2048]{3,2,1,0:T(8,128)(2,1)S(1)}, u32[]{:S(2)}, u32[]{:S(2)}) async-start(bf16[4,2,72,2048]{3,2,1,0:T(8,128)(2,1)} %get-tuple-element.313), calls=%async_computation.2 | async-start | bytes 4718592 | tf_op jit(solution)/shard_map/all_to_all | solution.py:366
  163.2 2.3 %collective-permute-start.22 = (bf16[136,2048]{1,0:T(8,128)(2,1)}, bf16[136,2048]{1,0:T(8,128)(2,1)S(1)}, u32[]{:S(2)}, u32[]{:S(2)}) collective-permute-start(bf16[136,2048]{1,0:T(8,128)(2,1)} %get-tuple-element.383), channel_id=1, source_target_pairs={{0,2},{1,3},{2,0},{3,1},{4,6},{5,7},{6,4},{7,5},{8,10},{9,11},{10,... | collective-permute-start | bytes 1671176 | tf_op jit(solution)/shard_map/ppermute | solution.py:356
  165.5 8.9 %convolution_convert_fusion.2 = bf16[2048,768]{1,0:T(8,128)(2,1)} fusion(bf16[1152,2048]{1,0:T(8,128)(2,1)} %get-tuple-element.314, bf16[1152,768]{1,0:T(8,128)(2,1)} %get-tuple-element.315), kind=kOutput, calls=%fused_computation.6 | convolution fusion | flops 3625451520 | bytes 9633792 | tf_op jit(solution)/shard_map/dot_general | solution.py:421
  174.5 5.7 %convolution_convert_fusion.1 = bf16[2048,768]{1,0:T(8,128)(2,1)} fusion(bf16[1152,2048]{1,0:T(8,128)(2,1)S(1)} %bitcast.38, bf16[1152,768]{1,0:T(8,128)(2,1)S(1)} %copy-done.2), kind=kOutput, calls=%fused_computation.5 | convolution fusion | flops 3625451520 | bytes 9633792 | tf_op jit(solution)/shard_map/dot_general | solution.py:421
  180.2 11.2 %all-to-all-done.2.refs_0_ = bf16[4,2,72,2048]{3,2,1,0:T(8,128)(2,1)S(1)} async-done(((bf16[4,2,72,2048]{3,2,1,0:T(8,128)(2,1)}), bf16[4,2,72,2048]{3,2,1,0:T(8,128)(2,1)S(1)}, u32[]{:S(2)}, u32[]{:S(2)}) %all-to-all-start.2) | async-done | bytes 2359328 | tf_op jit(solution)/shard_map/all_to_all | solution.py:366
  191.4 1.8 shard_map.126
  193.2 1.8 shard_map.125
  195.0 3.0 %conditional.12 = (bf16[136,2048]{1,0:T(8,128)(2,1)S(1)}, bf16[136,2048]{1,0:T(8,128)(2,1)S(1)}) conditional(s32[]{:T(128)} %convert_element_type.54, () %tuple.75, (bf16[136,2048]{1,0:T(8,128)(2,1)S(1)}, bf16[136,2048]{1,0:T(8,128)(2,1)S(1)}, bf16[136,2048]{1,0:T(8,128)(2,1)S(1)}, bf16[136,2048]{1,0:T(8,128)(2,1)S(1)}) %tuple.94), branch_computations={%region_10.11_spmd, %region_11.12_spmd} | conditional | flops 2228224 | bytes 7798880 | solution.py:401
  199.0 3.7 %all-to-all-start.3 = ((bf16[4,1,72,2048]{3,2,1,0:T(8,128)(2,1)}), bf16[4,1,72,2048]{3,2,1,0:T(8,128)(2,1)S(1)}, u32[]{:S(2)}, u32[]{:S(2)}) async-start(bf16[4,1,72,2048]{3,2,1,0:T(8,128)(2,1)} %get-tuple-element.329), calls=%async_computation.3 | async-start | bytes 2359296 | tf_op jit(solution)/shard_map/all_to_all | solution.py:366
  202.7 1.8 collective-permute-start.23
  204.5 2.0 collective-permute-start.24
  206.5 8.8 %convolution_convert_fusion = bf16[768,2048]{1,0:T(8,128)(2,1)} fusion(bf16[1152,768]{1,0:T(8,128)(2,1)} %get-tuple-element.330, bf16[1152,2048]{1,0:T(8,128)(2,1)} %get-tuple-element.331), kind=kOutput, calls=%fused_computation.4 | convolution fusion | flops 3625451520 | bytes 9633792 | tf_op jit(solution)/shard_map/dot_general | solution.py:421
  215.4 2.9 %all-to-all-done.3.refs_0_ = bf16[4,1,72,2048]{3,2,1,0:T(8,128)(2,1)S(1)} async-done(((bf16[4,1,72,2048]{3,2,1,0:T(8,128)(2,1)}), bf16[4,1,72,2048]{3,2,1,0:T(8,128)(2,1)S(1)}, u32[]{:S(2)}, u32[]{:S(2)}) %all-to-all-start.3) | async-done | bytes 1179680 | tf_op jit(solution)/shard_map/all_to_all | solution.py:366
  218.3 2.6 %shard_map.127 = (bf16[136,2048]{1,0:T(8,128)(2,1)S(1)}, bf16[136,2048]{1,0:T(8,128)(2,1)}) custom-call(s32[5]{0:T(128)S(1)} %pad_add_fusion.info_ref, bf16[272,2048]{1,0:T(8,128)(2,1)} %shard_map.119.mine_ref, bf16[272,2048]{1,0:T(8,128)(2,1)} %get-tuple-element.208.sibling_ref, bf16[4,1,72,2048]{3,2,1,0:T(8,128)(2,1)S(1)} %all-to-all-done.3.refs_0_), custom_call_target="tpu_custom_call" | custom-call | flops 1024 | bytes 1024 | tf_op jit(solution)/shard_map/pallas_call | solution.py:245
  220.9 2.3 conditional.13
  220.9 2.2 collective-permute-done.7
  223.3 8.1 %collective-permute-done.24.refs_3_ = bf16[136,2048]{1,0:T(8,128)(2,1)S(1)} collective-permute-done((bf16[136,2048]{1,0:T(8,128)(2,1)}, bf16[136,2048]{1,0:T(8,128)(2,1)S(1)}, u32[]{:S(2)}, u32[]{:S(2)}) %collective-permute-start.24) | collective-permute-done | bytes 557088 | tf_op jit(solution)/shard_map/ppermute | solution.py:356
  (63 shorter events, 24.9 us)
Async XLA Ops:
  3.0 31.1 %collective-permute-start.9 = (bf16[272,2048]{1,0:T(8,128)(2,1)}, bf16[272,2048]{1,0:T(8,128)(2,1)}, u32[]{:S(2)}, u32[]{:S(2)}) collective-permute-start(bf16[272,2048]{1,0:T(8,128)(2,1)} %shard_map.119.mine_ref), channel_id=1, source_target_pairs={{1,2},{2,1},{5,6},{6,5},{9,10},{10,9},{13,14},{14,13},{17,18},{18,... | collective-permute-start | bytes 3342344 | tf_op jit(solution)/shard_map/ppermute | solution.py:360
  4.6 29.5 %collective-permute-start.8 = (bf16[272,2048]{1,0:T(8,128)(2,1)}, bf16[272,2048]{1,0:T(8,128)(2,1)}, u32[]{:S(2)}, u32[]{:S(2)}) collective-permute-start(bf16[272,2048]{1,0:T(8,128)(2,1)} %shard_map.119.mine_ref), channel_id=1, source_target_pairs={{0,1},{1,0},{2,3},{3,2},{4,5},{5,4},{6,7},{7,6},{8,9},{9,8},{10,11... | collective-permute-start | bytes 3342344 | tf_op jit(solution)/shard_map/ppermute | solution.py:356
  9.6 3.1 %collective-permute-start = (bf16[272,2048]{1,0:T(8,128)(2,1)}, bf16[272,2048]{1,0:T(8,128)(2,1)}, u32[]{:S(2)}, u32[]{:S(2)}) collective-permute-start(bf16[272,2048]{1,0:T(8,128)(2,1)} %get-tuple-element.35.mine_ref), channel_id=1, source_target_pairs={{0,4},{1,5},{2,6},{3,7},{4,0},{5,1},{6,2},{7,3},{8,12},{9,13},{10,... | collective-permute-start | bytes 3342344 | tf_op jit(solution)/shard_map/cond/branch_1_fun/ppermute | solution.py:356
  17.3 31.4 %all-to-all-start = ((bf16[4,136,2048]{2,1,0:T(8,128)(2,1)}), bf16[4,136,2048]{2,1,0:T(8,128)(2,1)}, u32[]{:S(2)}, u32[]{:S(2)}) async-start(bf16[4,136,2048]{2,1,0:T(8,128)(2,1)} %get-tuple-element.209), calls=%async_computation | async-start | bytes 4456448 | tf_op jit(solution)/shard_map/all_to_all | solution.py:366
  21.8 4.8 %copy-start.1 = (bf16[1,2048,768]{2,1,0:T(8,128)(2,1)S(1)}, bf16[1,2048,768]{2,1,0:T(8,128)(2,1)}, u32[]{:S(2)}) copy-start(bf16[1,2048,768]{2,1,0:T(8,128)(2,1)} %refs_4_.2) | copy-start | bytes 9437188
  34.1 29.8 %collective-permute-start.13 = (bf16[272,2048]{1,0:T(8,128)(2,1)}, bf16[272,2048]{1,0:T(8,128)(2,1)S(1)}, u32[]{:S(2)}, u32[]{:S(2)}) collective-permute-start(bf16[272,2048]{1,0:T(8,128)(2,1)} %collective-permute-done.9), channel_id=1, source_target_pairs={{1,0},{2,3},{5,4},{6,7},{9,8},{10,11},{13,12},{14,15},{17,16},{18,... | collective-permute-start | bytes 3342344 | tf_op jit(solution)/shard_map/ppermute | solution.py:360
  35.4 28.5 %collective-permute-start.14 = (bf16[272,2048]{1,0:T(8,128)(2,1)}, bf16[272,2048]{1,0:T(8,128)(2,1)S(1)}, u32[]{:S(2)}, u32[]{:S(2)}) collective-permute-start(bf16[272,2048]{1,0:T(8,128)(2,1)} %collective-permute-done.8.mine_ref), channel_id=1, source_target_pairs={{1,2},{2,1},{5,6},{6,5},{9,10},{10,9},{13,14},{14,13},{17,18},{18,... | collective-permute-start | bytes 3342344 | tf_op jit(solution)/shard_map/ppermute | solution.py:360
  36.3 3.2 %collective-permute-start.1 = (bf16[272,2048]{1,0:T(8,128)(2,1)}, bf16[272,2048]{1,0:T(8,128)(2,1)}, u32[]{:S(2)}, u32[]{:S(2)}) collective-permute-start(bf16[272,2048]{1,0:T(8,128)(2,1)} %get-tuple-element.40.mine_ref), channel_id=1, source_target_pairs={{0,4},{1,5},{2,6},{3,7},{4,0},{5,1},{6,2},{7,3},{8,12},{9,13},{10,... | collective-permute-start | bytes 3342344 | tf_op jit(solution)/shard_map/cond/branch_1_fun/ppermute | solution.py:356
  48.7 23.1 %collective-permute-start.10 = (bf16[136,2048]{1,0:T(8,128)(2,1)}, bf16[136,2048]{1,0:T(8,128)(2,1)}, u32[]{:S(2)}, u32[]{:S(2)}) collective-permute-start(bf16[136,2048]{1,0:T(8,128)(2,1)} %get-tuple-element.219), channel_id=1, source_target_pairs={{0,8},{1,9},{2,10},{3,11},{4,12},{5,13},{6,14},{7,15},{8,0},{9,1},... | collective-permute-start | bytes 1671176 | tf_op jit(solution)/shard_map/ppermute | solution.py:356
  50.1 25.8 %collective-permute-start.11 = (bf16[136,2048]{1,0:T(8,128)(2,1)}, bf16[136,2048]{1,0:T(8,128)(2,1)}, u32[]{:S(2)}, u32[]{:S(2)}) collective-permute-start(bf16[136,2048]{1,0:T(8,128)(2,1)} %get-tuple-element.220), channel_id=1, source_target_pairs={{0,16},{1,17},{2,18},{3,19},{4,20},{5,21},{6,22},{7,23},{8,24},{9,... | collective-permute-start | bytes 1671176 | tf_op jit(solution)/shard_map/ppermute | solution.py:356
  50.6 25.2 %collective-permute-start.12 = (bf16[136,2048]{1,0:T(8,128)(2,1)}, bf16[136,2048]{1,0:T(8,128)(2,1)}, u32[]{:S(2)}, u32[]{:S(2)}) collective-permute-start(bf16[136,2048]{1,0:T(8,128)(2,1)} %get-tuple-element.221), channel_id=1, source_target_pairs={{0,24},{1,25},{2,26},{3,27},{4,28},{5,29},{6,30},{7,31},{8,16},{9,... | collective-permute-start | bytes 1671176 | tf_op jit(solution)/shard_map/ppermute | solution.py:356
  63.9 1.0 copy-start.3
  65.0 3.0 %collective-permute-start.2 = (bf16[272,2048]{1,0:T(8,128)(2,1)S(1)}, bf16[272,2048]{1,0:T(8,128)(2,1)}, u32[]{:S(2)}, u32[]{:S(2)}) collective-permute-start(bf16[272,2048]{1,0:T(8,128)(2,1)S(1)} %get-tuple-element.46.mine_ref), channel_id=1, source_target_pairs={{0,4},{1,5},{2,6},{3,7},{4,0},{5,1},{6,2},{7,3},{8,12},{9,13},{10,... | collective-permute-start | bytes 3342344 | tf_op jit(solution)/shard_map/cond/branch_1_fun/ppermute | solution.py:356
  75.9 25.2 %collective-permute-start.15 = (bf16[272,2048]{1,0:T(8,128)(2,1)S(1)}, bf16[272,2048]{1,0:T(8,128)(2,1)}, u32[]{:S(2)}, u32[]{:S(2)}) collective-permute-start(bf16[272,2048]{1,0:T(8,128)(2,1)S(1)} %broadcast_select_fusion.mine_ref), channel_id=1, source_target_pairs={{0,1},{1,0},{2,3},{3,2},{4,5},{5,4},{6,7},{7,6},{8,9},{9,8},{10,11... | collective-permute-start | bytes 3342344 | tf_op jit(solution)/shard_map/ppermute | solution.py:356
  77.1 30.9 %collective-permute-start.16 = (bf16[136,2048]{1,0:T(8,128)(2,1)}, bf16[136,2048]{1,0:T(8,128)(2,1)}, u32[]{:S(2)}, u32[]{:S(2)}) collective-permute-start(bf16[136,2048]{1,0:T(8,128)(2,1)} %get-tuple-element.257), channel_id=1, source_target_pairs={{0,8},{1,9},{2,10},{3,11},{4,12},{5,13},{6,14},{7,15},{8,0},{9,1},... | collective-permute-start | bytes 1671176 | tf_op jit(solution)/shard_map/ppermute | solution.py:356
  78.4 29.7 %collective-permute-start.17 = (bf16[136,2048]{1,0:T(8,128)(2,1)}, bf16[136,2048]{1,0:T(8,128)(2,1)}, u32[]{:S(2)}, u32[]{:S(2)}) collective-permute-start(bf16[136,2048]{1,0:T(8,128)(2,1)} %get-tuple-element.258), channel_id=1, source_target_pairs={{0,16},{1,17},{2,18},{3,19},{4,20},{5,21},{6,22},{7,23},{8,24},{9,... | collective-permute-start | bytes 1671176 | tf_op jit(solution)/shard_map/ppermute | solution.py:356
  79.2 28.9 %collective-permute-start.18 = (bf16[136,2048]{1,0:T(8,128)(2,1)S(1)}, bf16[136,2048]{1,0:T(8,128)(2,1)}, u32[]{:S(2)}, u32[]{:S(2)}) collective-permute-start(bf16[136,2048]{1,0:T(8,128)(2,1)S(1)} %get-tuple-element.259), channel_id=1, source_target_pairs={{0,24},{1,25},{2,26},{3,27},{4,28},{5,29},{6,30},{7,31},{8,16},{9,... | collective-permute-start | bytes 1671176 | tf_op jit(solution)/shard_map/ppermute | solution.py:356
  101.1 3.1 %collective-permute-start.3 = (bf16[272,2048]{1,0:T(8,128)(2,1)}, bf16[272,2048]{1,0:T(8,128)(2,1)}, u32[]{:S(2)}, u32[]{:S(2)}) collective-permute-start(bf16[272,2048]{1,0:T(8,128)(2,1)} %get-tuple-element.52.mine_ref), channel_id=1, source_target_pairs={{0,4},{1,5},{2,6},{3,7},{4,0},{5,1},{6,2},{7,3},{8,12},{9,13},{10,... | collective-permute-start | bytes 3342344 | tf_op jit(solution)/shard_map/cond/branch_1_fun/ppermute | solution.py:356
  108.1 15.7 %collective-permute-start.19 = (bf16[136,2048]{1,0:T(8,128)(2,1)}, bf16[136,2048]{1,0:T(8,128)(2,1)S(1)}, u32[]{:S(2)}, u32[]{:S(2)}) collective-permute-start(bf16[136,2048]{1,0:T(8,128)(2,1)} %get-tuple-element.271), channel_id=1, source_target_pairs={{0,8},{1,9},{2,10},{3,11},{4,12},{5,13},{6,14},{7,15},{8,0},{9,1},... | collective-permute-start | bytes 1671176 | tf_op jit(solution)/shard_map/ppermute | solution.py:356
  109.6 25.1 %collective-permute-start.20 = (bf16[136,2048]{1,0:T(8,128)(2,1)S(1)}, bf16[136,2048]{1,0:T(8,128)(2,1)}, u32[]{:S(2)}, u32[]{:S(2)}) collective-permute-start(bf16[136,2048]{1,0:T(8,128)(2,1)S(1)} %get-tuple-element.272), channel_id=1, source_target_pairs={{0,16},{1,17},{2,18},{3,19},{4,20},{5,21},{6,22},{7,23},{8,24},{9,... | collective-permute-start | bytes 1671176 | tf_op jit(solution)/shard_map/ppermute | solution.py:356
  110.8 25.2 %collective-permute-start.21 = (bf16[136,2048]{1,0:T(8,128)(2,1)S(1)}, bf16[136,2048]{1,0:T(8,128)(2,1)}, u32[]{:S(2)}, u32[]{:S(2)}) collective-permute-start(bf16[136,2048]{1,0:T(8,128)(2,1)S(1)} %get-tuple-element.273), channel_id=1, source_target_pairs={{0,24},{1,25},{2,26},{3,27},{4,28},{5,29},{6,30},{7,31},{8,16},{9,... | collective-permute-start | bytes 1671176 | tf_op jit(solution)/shard_map/ppermute | solution.py:356
  123.8 16.1 %copy-start.4 = (bf16[136,2048]{1,0:T(8,128)(2,1)}, bf16[136,2048]{1,0:T(8,128)(2,1)S(1)}, u32[]{:S(2)}) copy-start(bf16[136,2048]{1,0:T(8,128)(2,1)S(1)} %collective-permute-done.19.refs_1_) | copy-start | bytes 1671172
  136.0 18.6 %all-to-all-start.1 = ((bf16[4,1,72,2048]{3,2,1,0:T(8,128)(2,1)}), bf16[4,1,72,2048]{3,2,1,0:T(8,128)(2,1)S(1)}, u32[]{:S(2)}, u32[]{:S(2)}) async-start(bf16[4,1,72,2048]{3,2,1,0:T(8,128)(2,1)} %get-tuple-element.289), calls=%async_computation.1 | async-start | bytes 2359296 | tf_op jit(solution)/shard_map/all_to_all | solution.py:366
  156.4 2.0 collective-permute-start.4
  159.4 32.0 %all-to-all-start.2 = ((bf16[4,2,72,2048]{3,2,1,0:T(8,128)(2,1)}), bf16[4,2,72,2048]{3,2,1,0:T(8,128)(2,1)S(1)}, u32[]{:S(2)}, u32[]{:S(2)}) async-start(bf16[4,2,72,2048]{3,2,1,0:T(8,128)(2,1)} %get-tuple-element.313), calls=%async_computation.2 | async-start | bytes 4718592 | tf_op jit(solution)/shard_map/all_to_all | solution.py:366
  163.2 11.3 %slice-start = ((s8[4718592]{0:T(1024)(128)(4,1)}), s8[4194304]{0:T(1024)(128)(4,1)S(1)}, s32[]{:S(2)}) async-start(s8[4718592]{0:T(1024)(128)(4,1)} %bitcast.37), calls=%async_computation.4 | async-start | bytes 8388608
  163.2 11.3 %slice-start.1 = ((s8[4718592]{0:T(1024)(128)(4,1)}), s8[524288]{0:T(1024)(128)(4,1)S(1)}, s32[]{:S(2)}) async-start(s8[4718592]{0:T(1024)(128)(4,1)} %bitcast.37), calls=%async_computation.5 | async-start | bytes 1048576
  163.2 11.3 %copy-start.2 = (bf16[1152,768]{1,0:T(8,128)(2,1)S(1)}, bf16[1152,768]{1,0:T(8,128)(2,1)}, u32[]{:S(2)}) copy-start(bf16[1152,768]{1,0:T(8,128)(2,1)} %get-tuple-element.316) | copy-start | bytes 5308420
  163.2 34.8 %collective-permute-start.22 = (bf16[136,2048]{1,0:T(8,128)(2,1)}, bf16[136,2048]{1,0:T(8,128)(2,1)S(1)}, u32[]{:S(2)}, u32[]{:S(2)}) collective-permute-start(bf16[136,2048]{1,0:T(8,128)(2,1)} %get-tuple-element.383), channel_id=1, source_target_pairs={{0,2},{1,3},{2,0},{3,1},{4,6},{5,7},{6,4},{7,5},{8,10},{9,11},{10,... | collective-permute-start | bytes 1671176 | tf_op jit(solution)/shard_map/ppermute | solution.py:356
  195.0 2.0 collective-permute-start.5
  195.1 2.7 %collective-permute-start.6 = (bf16[136,2048]{1,0:T(8,128)(2,1)S(1)}, bf16[136,2048]{1,0:T(8,128)(2,1)S(1)}, u32[]{:S(2)}, u32[]{:S(2)}) collective-permute-start(bf16[136,2048]{1,0:T(8,128)(2,1)S(1)} %get-tuple-element.63), channel_id=1, source_target_pairs={{0,4},{1,5},{2,6},{3,7},{4,0},{5,1},{6,2},{7,3},{8,12},{9,13},{10,... | collective-permute-start | bytes 1671176 | tf_op jit(solution)/shard_map/cond/branch_1_fun/ppermute | solution.py:356
  198.0 0.8 copy-start.5
  198.0 1.0 copy-start.6
  199.0 19.3 %all-to-all-start.3 = ((bf16[4,1,72,2048]{3,2,1,0:T(8,128)(2,1)}), bf16[4,1,72,2048]{3,2,1,0:T(8,128)(2,1)S(1)}, u32[]{:S(2)}, u32[]{:S(2)}) async-start(bf16[4,1,72,2048]{3,2,1,0:T(8,128)(2,1)} %get-tuple-element.329), calls=%async_computation.3 | async-start | bytes 2359296 | tf_op jit(solution)/shard_map/all_to_all | solution.py:366
  202.7 20.5 %collective-permute-start.23 = (bf16[136,2048]{1,0:T(8,128)(2,1)}, bf16[136,2048]{1,0:T(8,128)(2,1)S(1)}, u32[]{:S(2)}, u32[]{:S(2)}) collective-permute-start(bf16[136,2048]{1,0:T(8,128)(2,1)} %copy-done.5), channel_id=1, source_target_pairs={{0,1},{1,0},{2,3},{3,2},{4,5},{5,4},{6,7},{7,6},{8,9},{9,8},{10,11... | collective-permute-start | bytes 1671176 | tf_op jit(solution)/shard_map/ppermute | solution.py:356
  204.5 26.8 %collective-permute-start.24 = (bf16[136,2048]{1,0:T(8,128)(2,1)}, bf16[136,2048]{1,0:T(8,128)(2,1)S(1)}, u32[]{:S(2)}, u32[]{:S(2)}) collective-permute-start(bf16[136,2048]{1,0:T(8,128)(2,1)} %copy-done.6), channel_id=1, source_target_pairs={{0,3},{1,2},{2,1},{3,0},{4,7},{5,6},{6,5},{7,4},{8,11},{9,10},{10,... | collective-permute-start | bytes 1671176 | tf_op jit(solution)/shard_map/ppermute | solution.py:356
  220.9 10.4 %copy-start = (s32[128,8]{0,1:T(8,128)S(1)}, s32[128,8]{0,1:T(8,128)}, u32[]{:S(2)}) copy-start(s32[128,8]{0,1:T(8,128)} %param.24) | copy-start | bytes 12292
  220.9 2.2 collective-permute-start.7

commit v4 on v3

--- a/solution.py
+++ b/solution.py
@@ -434,10 +434,10 @@
         r0, saved = work(0, [p0], weights, ())
         outward, inner2, r0 = fence(outward, inner2, r0)
         b2 = jnp.where(middle, inner2, outward)
+        b3 = swap(b2, 0, 1)
         s2, m2 = prepare(b2)
-        p1, m2, b2, r0, saved = fence(p1, m2, b2, r0, saved)
+        p1, m2, r0, saved = fence(p1, m2, r0, saved)
         p2 = send(m2)
-        b3 = swap(b2, 0, 1)
         r1, saved = work(1, p1, weights, saved, 0, 2)
         b3, r1 = fence(b3, r1)
         s3, m3 = prepare(b3)

time: 237 us -> 228 us (0.962)
  waiting for transfers between devices: 71.2 us -> 65 us
    ppermute x22, waiting for transfers between devices: 50.4 us -> 41.1 us  [swap(): return lax.ppermute(value, both, pairs)]
    all_to_all x4, waiting for transfers between devices: 20.7 us -> 23.9 us  [back(): lax.all_to_all(value, 'node', split_axis=0, concat_axis=0, axis_index_gro...]
  transfers between devices with their start and end apart: 29 -> 29, of which waited for: 19 -> 20; matrix products, arithmetic and copies ran while one was open for 16% -> 16% of each run, Pallas kernels for 31% -> 32%
where the time goes in v4:
time: 228 us; the launch traced here: 224 us
  Pallas kernels  77.4 us (34%)
  waiting for transfers between devices  65 us (29%)
  starting transfers between devices  41.4 us (18%)
  matrix products  23.6 us (10%)
  local copies, waits for them, and re-layouts  14.3 us (6%)
    pallas_call x4, Pallas kernels, expert(): pl.pallas_call(functools.partial(expert_kernel, at, sources, len(kept)),...  49.5 us
    ppermute x22, waiting for transfers between devices, swap(): return lax.ppermute(value, both, pairs)  41.1 us
    pallas_call x10, Pallas kernels, call(): pl.pallas_call(kernel, grid=(1,), in_specs=([SMEM] if info is not None el...  27.9 us
    all_to_all x4, waiting for transfers between devices, back(): lax.all_to_all(value, 'node', split_axis=0, concat_axis=0, axis_index_gro...  23.9 us
    dot_general x3, matrix products, wgrad(): return lax.dot_general(a, b, TN, preferred_element_type=F32).astype(BF16)  23.6 us
    ppermute x22, starting transfers between devices, swap(): return lax.ppermute(value, both, pairs)  21.5 us
    all_to_all x4, starting transfers between devices, back(): lax.all_to_all(value, 'node', split_axis=0, concat_axis=0, axis_index_gro...  16 us
    optimization_barrier x3, local copies, waits for them, and re-layouts, fence(): return lax.optimization_barrier(values)  12.3 us
  transfers between devices with their start and end apart: 29, of which 20 were waited for; matrix products, arithmetic and copies ran while one was open for 16% of the time, Pallas kernels for 32%

profile of v4, /device:TPU:0, one launch (start us, length us, event | category | flops | bytes accessed | tf_op | source)
XLA Modules:
  0.0 224.4 jit_solution(12469396234068487249)
XLA Ops:
  0.6 2.3 %shard_map.119.mine_ref = bf16[272,2048]{1,0:T(8,128)(2,1)} custom-call(bf16[128,2048]{1,0:T(8,128)(2,1)} %x_ref.1, bf16[128,2048]{1,0:T(8,128)(2,1)} %dy_ref.1, s32[8,128]{1,0:T(8,128)} %bitcast.23, bf16[8,128]{1,0:T(8,128)(2,1)} %bitcast.39), custom_call_target="tpu_custom_call" | custom-call | flops 1024 | bytes 1024 | tf_op jit(solution)/shard_map/pallas_call | solution.py:245
  3.0 1.7 collective-permute-start.9
  4.6 4.9 %collective-permute-start.8 = (bf16[272,2048]{1,0:T(8,128)(2,1)}, bf16[272,2048]{1,0:T(8,128)(2,1)}, u32[]{:S(2)}, u32[]{:S(2)}) collective-permute-start(bf16[272,2048]{1,0:T(8,128)(2,1)} %shard_map.119.mine_ref), channel_id=1, source_target_pairs={{0,1},{1,0},{2,3},{3,2},{4,5},{5,4},{6,7},{7,6},{8,9},{9,8},{10,11... | collective-permute-start | bytes 3342344 | tf_op jit(solution)/shard_map/ppermute | solution.py:356
  9.6 7.6 %conditional.7 = (bf16[272,2048]{1,0:T(8,128)(2,1)}, bf16[4,136,2048]{2,1,0:T(8,128)(2,1)}) conditional(s32[]{:T(128)} %convert_element_type.54, () %tuple.73, (bf16[272,2048]{1,0:T(8,128)(2,1)}, s32[5]{0:T(128)S(1)}) %tuple.74), branch_computations={%region_0.0_spmd, %region_1.0_spmd} | conditional | flops 1024 | bytes 4457528 | solution.py:401
  9.6 3.1 %collective-permute-done.sibling_ref = bf16[272,2048]{1,0:T(8,128)(2,1)} collective-permute-done((bf16[272,2048]{1,0:T(8,128)(2,1)}, bf16[272,2048]{1,0:T(8,128)(2,1)}, u32[]{:S(2)}, u32[]{:S(2)}) %collective-permute-start) | collective-permute-done | bytes 1114144 | tf_op jit(solution)/shard_map/cond/branch_1_fun/ppermute | solution.py:356
  12.7 4.5 %branch_1_fun.4 = bf16[4,136,2048]{2,1,0:T(8,128)(2,1)} custom-call(s32[5]{0:T(128)S(1)} %get-tuple-element.36.info_ref, bf16[272,2048]{1,0:T(8,128)(2,1)} %get-tuple-element.35.mine_ref, bf16[272,2048]{1,0:T(8,128)(2,1)} %collective-permute-done.sibling_ref), custom_call_target="tpu_custom_call" | custom-call | flops 1024 | bytes 1024 | tf_op jit(solution)/shard_map/cond/branch_1_fun/pallas_call | solution.py:245
  17.3 4.5 %all-to-all-start = ((bf16[4,136,2048]{2,1,0:T(8,128)(2,1)}), bf16[4,136,2048]{2,1,0:T(8,128)(2,1)}, u32[]{:S(2)}, u32[]{:S(2)}) async-start(bf16[4,136,2048]{2,1,0:T(8,128)(2,1)} %get-tuple-element.208), calls=%async_computation | async-start | bytes 4456448 | tf_op jit(solution)/shard_map/all_to_all | solution.py:366
  21.8 4.8 %copy.29 = bf16[1,768,2048]{1,2,0:T(8,128)(2,1)} copy(bf16[1,768,2048]{2,1,0:T(8,128)(2,1)} %param.28) | data formatting | bytes 6291456 | tf_op jit(solution)/shard_map/optimization_barrier | solution.py:371
  26.6 2.9 %copy.30 = bf16[1,2048,768]{1,2,0:T(8,128)(2,1)} copy(bf16[1,2048,768]{2,1,0:T(8,128)(2,1)S(1)} %copy-done.1) | data formatting | bytes 6291456 | tf_op jit(solution)/shard_map/optimization_barrier | solution.py:371
  29.4 4.6 %copy.31 = bf16[1,2048,768]{1,2,0:T(8,128)(2,1)} copy(bf16[1,2048,768]{2,1,0:T(8,128)(2,1)} %refs_5_.2) | data formatting | bytes 6291456 | tf_op jit(solution)/shard_map/optimization_barrier | solution.py:371
  36.3 7.5 %conditional.8 = (bf16[272,2048]{1,0:T(8,128)(2,1)}, bf16[136,2048]{1,0:T(8,128)(2,1)S(1)}, bf16[136,2048]{1,0:T(8,128)(2,1)}, bf16[136,2048]{1,0:T(8,128)(2,1)}, bf16[136,2048]{1,0:T(8,128)(2,1)}) conditional(s32[]{:T(128)} %convert_element_type.54, () %tuple.78, (bf16[272,2048]{1,0:T(8,128)(2,1)}, s32[5]{0:T(128)S(1)}) %tuple.79), branch_computations={%region_2.0_spmd, %region_3.0_spmd} | conditional | flops 1024 | bytes 4457552 | solution.py:401
  36.5 3.0 %collective-permute-done.1.sibling_ref = bf16[272,2048]{1,0:T(8,128)(2,1)} collective-permute-done((bf16[272,2048]{1,0:T(8,128)(2,1)}, bf16[272,2048]{1,0:T(8,128)(2,1)}, u32[]{:S(2)}, u32[]{:S(2)}) %collective-permute-start.1) | collective-permute-done | bytes 1114144 | tf_op jit(solution)/shard_map/cond/branch_1_fun/ppermute | solution.py:356
  39.5 4.3 %branch_1_fun.5 = (bf16[136,2048]{1,0:T(8,128)(2,1)S(1)}, bf16[136,2048]{1,0:T(8,128)(2,1)}, bf16[136,2048]{1,0:T(8,128)(2,1)}, bf16[136,2048]{1,0:T(8,128)(2,1)}) custom-call(s32[5]{0:T(128)S(1)} %get-tuple-element.41.info_ref, bf16[272,2048]{1,0:T(8,128)(2,1)} %get-tuple-element.40.mine_ref, bf16[272,2048]{1,0:T(8,128)(2,1)} %collective-permute-done.1.sibling_ref), custom_call_target="tpu_custom_call" | custom-call | flops 1024 | bytes 1024 | tf_op jit(solution)/shard_map/cond/branch_1_fun/pallas_call | solution.py:245
  43.8 4.8 %all-to-all-done.refs_0_ = bf16[4,136,2048]{2,1,0:T(8,128)(2,1)} async-done(((bf16[4,136,2048]{2,1,0:T(8,128)(2,1)}), bf16[4,136,2048]{2,1,0:T(8,128)(2,1)}, u32[]{:S(2)}, u32[]{:S(2)}) %all-to-all-start) | async-done | bytes 2228256 | tf_op jit(solution)/shard_map/all_to_all | solution.py:366
  50.6 1.5 collective-permute-start.15
  52.1 11.7 %shard_map.120 = (bf16[4,1,72,2048]{3,2,1,0:T(8,128)(2,1)}, bf16[1152,2048]{1,0:T(8,128)(2,1)}, bf16[1152,2048]{1,0:T(8,128)(2,1)}, bf16[1152,768]{1,0:T(8,128)(...) custom-call(s32[5]{0:T(128)S(1)} %pad_add_fusion.info_ref, bf16[4,136,2048]{2,1,0:T(8,128)(2,1)} %all-to-all-done.refs_0_, ...), custom_call_target="tpu_custom_call" | custom-call | flops 1024 | bytes 1024 | tf_op jit(solution)/shard_map/pallas_call | solution.py:324
  65.0 3.9 %collective-permute-start.12 = (bf16[272,2048]{1,0:T(8,128)(2,1)S(1)}, bf16[272,2048]{1,0:T(8,128)(2,1)}, u32[]{:S(2)}, u32[]{:S(2)}) collective-permute-start(bf16[272,2048]{1,0:T(8,128)(2,1)S(1)} %broadcast_select_fusion.mine_ref), channel_id=1, source_target_pairs={{0,1},{1,0},{2,3},{3,2},{4,5},{5,4},{6,7},{7,6},{8,9},{9,8},{10,11... | collective-permute-start | bytes 3342344 | tf_op jit(solution)/shard_map/ppermute | solution.py:356
  68.9 6.7 %conditional.9 = (bf16[272,2048]{1,0:T(8,128)(2,1)}, bf16[136,2048]{1,0:T(8,128)(2,1)S(1)}, bf16[136,2048]{1,0:T(8,128)(2,1)}, bf16[136,2048]{1,0:T(8,128)(2,1)}, bf16[136,2048]{1,0:T(8,128)(2,1)S(1)}) conditional(s32[]{:T(128)} %convert_element_type.54, () %tuple.82, (bf16[272,2048]{1,0:T(8,128)(2,1)S(1)}, s32[5]{0:T(128)S(1)}) %tuple.83), branch_computations={%region_4.5_spmd, %region_5.6_spmd} | conditional | flops 1024 | bytes 4457552 | solution.py:401
  68.9 2.9 %collective-permute-done.2.sibling_ref = bf16[272,2048]{1,0:T(8,128)(2,1)} collective-permute-done((bf16[272,2048]{1,0:T(8,128)(2,1)S(1)}, bf16[272,2048]{1,0:T(8,128)(2,1)}, u32[]{:S(2)}, u32[]{:S(2)}) %collective-permute-start.2) | collective-permute-done | bytes 1114144 | tf_op jit(solution)/shard_map/cond/branch_1_fun/ppermute | solution.py:356
  71.8 3.8 %branch_1_fun.6 = (bf16[136,2048]{1,0:T(8,128)(2,1)S(1)}, bf16[136,2048]{1,0:T(8,128)(2,1)}, bf16[136,2048]{1,0:T(8,128)(2,1)}, bf16[136,2048]{1,0:T(8,128)(2,1)S(1)}) custom-call(s32[5]{0:T(128)S(1)} %get-tuple-element.47.info_ref, bf16[272,2048]{1,0:T(8,128)(2,1)S(1)} %get-tuple-element.46.mine_ref, bf16[272,2048]{1,0:T(8,128)(2,1)} %collective-permute-done.2.sibling_ref), custom_call_target="tpu_custom_call" | custom-call | flops 1024 | bytes 1024 | tf_op jit(solution)/shard_map/cond/branch_1_fun/pallas_call | solution.py:245
  77.3 1.5 collective-permute-start.17
  79.4 13.0 %shard_map.121 = (bf16[4,2,72,2048]{3,2,1,0:T(8,128)(2,1)}, bf16[1152,2048]{1,0:T(8,128)(2,1)}, bf16[1152,2048]{1,0:T(8,128)(2,1)}, bf16[1152,768]{1,0:T(8,128)(...) custom-call(s32[5]{0:T(128)S(1)} %pad_add_fusion.info_ref, ...), custom_call_target="tpu_custom_call", output_to_operand_aliasing={{1}: (10, {}), {2}: (11, {}), {3}: (12, {}), {4}: (13, {}),... | custom-call | flops 1024 | bytes 1024 | tf_op jit(solution)/shard_map/pallas_call | solution.py:324
  92.7 7.0 %conditional.10 = (bf16[272,2048]{1,0:T(8,128)(2,1)}, bf16[136,2048]{1,0:T(8,128)(2,1)S(1)}, bf16[136,2048]{1,0:T(8,128)(2,1)}, bf16[136,2048]{1,0:T(8,128)(2,1)S(1)}, bf16[136,2048]{1,0:T(8,128)(2,1)S(1)}) conditional(s32[]{:T(128)} %convert_element_type.54, () %tuple.86, (bf16[272,2048]{1,0:T(8,128)(2,1)}, s32[5]{0:T(128)S(1)}) %tuple.87), branch_computations={%region_6.7_spmd, %region_7.8_spmd} | conditional | flops 1024 | bytes 4457552 | solution.py:401
  92.7 3.1 %collective-permute-done.3.sibling_ref = bf16[272,2048]{1,0:T(8,128)(2,1)} collective-permute-done((bf16[272,2048]{1,0:T(8,128)(2,1)}, bf16[272,2048]{1,0:T(8,128)(2,1)}, u32[]{:S(2)}, u32[]{:S(2)}) %collective-permute-start.3) | collective-permute-done | bytes 1114144 | tf_op jit(solution)/shard_map/cond/branch_1_fun/ppermute | solution.py:356
  95.8 3.9 %branch_1_fun.7 = (bf16[136,2048]{1,0:T(8,128)(2,1)S(1)}, bf16[136,2048]{1,0:T(8,128)(2,1)}, bf16[136,2048]{1,0:T(8,128)(2,1)S(1)}, bf16[136,2048]{1,0:T(8,128)(2,1)S(1)}) custom-call(s32[5]{0:T(128)S(1)} %get-tuple-element.53.info_ref, bf16[272,2048]{1,0:T(8,128)(2,1)} %get-tuple-element.52.mine_ref, bf16[272,2048]{1,0:T(8,128)(2,1)} %collective-permute-done.3.sibling_ref), custom_call_target="tpu_custom_call" | custom-call | flops 1024 | bytes 1024 | tf_op jit(solution)/shard_map/cond/branch_1_fun/pallas_call | solution.py:245
  99.7 4.3 %collective-permute-done.17.refs_2_ = bf16[136,2048]{1,0:T(8,128)(2,1)} collective-permute-done((bf16[136,2048]{1,0:T(8,128)(2,1)}, bf16[136,2048]{1,0:T(8,128)(2,1)}, u32[]{:S(2)}, u32[]{:S(2)}) %collective-permute-start.17) | collective-permute-done | bytes 557088 | tf_op jit(solution)/shard_map/ppermute | solution.py:356
  106.0 1.5 collective-permute-start.21
  107.5 11.9 %shard_map.122 = (bf16[4,1,72,2048]{3,2,1,0:T(8,128)(2,1)}, bf16[1152,2048]{1,0:T(8,128)(2,1)}, bf16[1152,2048]{1,0:T(8,128)(2,1)}, bf16[1152,768]{1,0:T(8,128)(...) custom-call(s32[5]{0:T(128)S(1)} %pad_add_fusion.info_ref, ...), custom_call_target="tpu_custom_call", output_to_operand_aliasing={{1}: (10, {}), {2}: (11, {}), {3}: (12, {}), {4}: (13, {}),... | custom-call | flops 1024 | bytes 1024 | tf_op jit(solution)/shard_map/pallas_call | solution.py:324
  120.9 9.9 %collective-permute-done.21.refs_3_ = bf16[136,2048]{1,0:T(8,128)(2,1)} collective-permute-done((bf16[136,2048]{1,0:T(8,128)(2,1)S(1)}, bf16[136,2048]{1,0:T(8,128)(2,1)}, u32[]{:S(2)}, u32[]{:S(2)}) %collective-permute-start.21) | collective-permute-done | bytes 557088 | tf_op jit(solution)/shard_map/ppermute | solution.py:356
  130.7 3.9 %all-to-all-start.1 = ((bf16[4,1,72,2048]{3,2,1,0:T(8,128)(2,1)}), bf16[4,1,72,2048]{3,2,1,0:T(8,128)(2,1)S(1)}, u32[]{:S(2)}, u32[]{:S(2)}) async-start(bf16[4,1,72,2048]{3,2,1,0:T(8,128)(2,1)} %get-tuple-element.287), calls=%async_computation.1 | async-start | bytes 2359296 | tf_op jit(solution)/shard_map/all_to_all | solution.py:366
  134.7 12.9 %shard_map.123 = (bf16[4,2,72,2048]{3,2,1,0:T(8,128)(2,1)}, bf16[1152,2048]{1,0:T(8,128)(2,1)}, bf16[1152,2048]{1,0:T(8,128)(2,1)}, bf16[1152,768]{1,0:T(8,128)(...) custom-call(s32[5]{0:T(128)S(1)} %pad_add_fusion.info_ref, ...), custom_call_target="tpu_custom_call", output_to_operand_aliasing={{1}: (10, {}), {2}: (11, {}), {3}: (12, {}), {4}: (13, {}),... | custom-call | flops 1024 | bytes 1024 | tf_op jit(solution)/shard_map/pallas_call | solution.py:324
  148.1 1.8 shard_map.124
  149.9 3.0 %conditional.11 = (bf16[136,2048]{1,0:T(8,128)(2,1)}) conditional(s32[]{:T(128)} %convert_element_type.54, () %tuple.88, (bf16[136,2048]{1,0:T(8,128)(2,1)S(1)}, bf16[136,2048]{1,0:T(8,128)(2,1)S(1)}) %shard_map.124), branch_computations={%region_8.9_spmd, %region_9.10_spmd} | conditional | flops 1114112 | bytes 3899440 | solution.py:401
  150.0 1.9 collective-permute-done.4
  152.9 3.8 %all-to-all-start.2 = ((bf16[4,2,72,2048]{3,2,1,0:T(8,128)(2,1)}), bf16[4,2,72,2048]{3,2,1,0:T(8,128)(2,1)S(1)}, u32[]{:S(2)}, u32[]{:S(2)}) async-start(bf16[4,2,72,2048]{3,2,1,0:T(8,128)(2,1)} %get-tuple-element.311), calls=%async_computation.2 | async-start | bytes 4718592 | tf_op jit(solution)/shard_map/all_to_all | solution.py:366
  156.8 9.1 %convolution_convert_fusion.2 = bf16[2048,768]{1,0:T(8,128)(2,1)} fusion(bf16[1152,2048]{1,0:T(8,128)(2,1)} %get-tuple-element.312, bf16[1152,768]{1,0:T(8,128)(2,1)} %get-tuple-element.313), kind=kOutput, calls=%fused_computation.6 | convolution fusion | flops 3625451520 | bytes 9633792 | tf_op jit(solution)/shard_map/dot_general | solution.py:421
  165.9 5.7 %convolution_convert_fusion.1 = bf16[2048,768]{1,0:T(8,128)(2,1)} fusion(bf16[1152,2048]{1,0:T(8,128)(2,1)S(1)} %bitcast.38, bf16[1152,768]{1,0:T(8,128)(2,1)S(1)} %copy-done.2), kind=kOutput, calls=%fused_computation.5 | convolution fusion | flops 3625451520 | bytes 9633792 | tf_op jit(solution)/shard_map/dot_general | solution.py:421
  171.6 13.3 %all-to-all-done.2.refs_0_ = bf16[4,2,72,2048]{3,2,1,0:T(8,128)(2,1)S(1)} async-done(((bf16[4,2,72,2048]{3,2,1,0:T(8,128)(2,1)}), bf16[4,2,72,2048]{3,2,1,0:T(8,128)(2,1)S(1)}, u32[]{:S(2)}, u32[]{:S(2)}) %all-to-all-start.2) | async-done | bytes 2359328 | tf_op jit(solution)/shard_map/all_to_all | solution.py:366
  184.9 1.8 shard_map.126
  186.7 1.8 shard_map.125
  188.5 3.0 %conditional.12 = (bf16[136,2048]{1,0:T(8,128)(2,1)S(1)}, bf16[136,2048]{1,0:T(8,128)(2,1)S(1)}) conditional(s32[]{:T(128)} %convert_element_type.54, () %tuple.75, (bf16[136,2048]{1,0:T(8,128)(2,1)S(1)}, bf16[136,2048]{1,0:T(8,128)(2,1)S(1)}, bf16[136,2048]{1,0:T(8,128)(2,1)S(1)}, bf16[136,2048]{1,0:T(8,128)(2,1)S(1)}) %tuple.94), branch_computations={%region_10.11_spmd, %region_11.12_spmd} | conditional | flops 2228224 | bytes 7798880 | solution.py:401
  192.5 3.7 %all-to-all-start.3 = ((bf16[4,1,72,2048]{3,2,1,0:T(8,128)(2,1)}), bf16[4,1,72,2048]{3,2,1,0:T(8,128)(2,1)S(1)}, u32[]{:S(2)}, u32[]{:S(2)}) async-start(bf16[4,1,72,2048]{3,2,1,0:T(8,128)(2,1)} %get-tuple-element.327), calls=%async_computation.3 | async-start | bytes 2359296 | tf_op jit(solution)/shard_map/all_to_all | solution.py:366
  197.7 8.8 %convolution_convert_fusion = bf16[768,2048]{1,0:T(8,128)(2,1)} fusion(bf16[1152,768]{1,0:T(8,128)(2,1)} %get-tuple-element.328, bf16[1152,2048]{1,0:T(8,128)(2,1)} %get-tuple-element.329), kind=kOutput, calls=%fused_computation.4 | convolution fusion | flops 3625451520 | bytes 9633792 | tf_op jit(solution)/shard_map/dot_general | solution.py:421
  206.6 5.2 %all-to-all-done.3.refs_0_ = bf16[4,1,72,2048]{3,2,1,0:T(8,128)(2,1)S(1)} async-done(((bf16[4,1,72,2048]{3,2,1,0:T(8,128)(2,1)}), bf16[4,1,72,2048]{3,2,1,0:T(8,128)(2,1)S(1)}, u32[]{:S(2)}, u32[]{:S(2)}) %all-to-all-start.3) | async-done | bytes 1179680 | tf_op jit(solution)/shard_map/all_to_all | solution.py:366
  211.8 2.6 %shard_map.127 = (bf16[136,2048]{1,0:T(8,128)(2,1)S(1)}, bf16[136,2048]{1,0:T(8,128)(2,1)}) custom-call(s32[5]{0:T(128)S(1)} %pad_add_fusion.info_ref, bf16[272,2048]{1,0:T(8,128)(2,1)} %shard_map.119.mine_ref, bf16[272,2048]{1,0:T(8,128)(2,1)} %get-tuple-element.207.sibling_ref, bf16[4,1,72,2048]{3,2,1,0:T(8,128)(2,1)S(1)} %all-to-all-done.3.refs_0_), custom_call_target="tpu_custom_call" | custom-call | flops 1024 | bytes 1024 | tf_op jit(solution)/shard_map/pallas_call | solution.py:245
  214.4 2.3 %conditional.13 = (bf16[136,2048]{1,0:T(8,128)(2,1)S(1)}) conditional(s32[]{:T(128)} %convert_element_type.54, () %tuple.72, (bf16[136,2048]{1,0:T(8,128)(2,1)S(1)}, bf16[136,2048]{1,0:T(8,128)(2,1)}) %shard_map.127), branch_computations={%region_12.13_spmd, %region_13.14_spmd} | conditional | flops 1114112 | bytes 3899440 | solution.py:401
  214.4 2.2 collective-permute-done.7
  216.8 6.4 %collective-permute-done.23.refs_1_ = bf16[136,2048]{1,0:T(8,128)(2,1)S(1)} collective-permute-done((bf16[136,2048]{1,0:T(8,128)(2,1)}, bf16[136,2048]{1,0:T(8,128)(2,1)S(1)}, u32[]{:S(2)}, u32[]{:S(2)}) %collective-permute-start.23) | collective-permute-done | bytes 557088 | tf_op jit(solution)/shard_map/ppermute | solution.py:356
  (63 shorter events, 20.1 us)
Async XLA Ops:
  3.0 31.1 %collective-permute-start.9 = (bf16[272,2048]{1,0:T(8,128)(2,1)}, bf16[272,2048]{1,0:T(8,128)(2,1)}, u32[]{:S(2)}, u32[]{:S(2)}) collective-permute-start(bf16[272,2048]{1,0:T(8,128)(2,1)} %shard_map.119.mine_ref), channel_id=1, source_target_pairs={{1,2},{2,1},{5,6},{6,5},{9,10},{10,9},{13,14},{14,13},{17,18},{18,... | collective-permute-start | bytes 3342344 | tf_op jit(solution)/shard_map/ppermute | solution.py:360
  4.6 29.5 %collective-permute-start.8 = (bf16[272,2048]{1,0:T(8,128)(2,1)}, bf16[272,2048]{1,0:T(8,128)(2,1)}, u32[]{:S(2)}, u32[]{:S(2)}) collective-permute-start(bf16[272,2048]{1,0:T(8,128)(2,1)} %shard_map.119.mine_ref), channel_id=1, source_target_pairs={{0,1},{1,0},{2,3},{3,2},{4,5},{5,4},{6,7},{7,6},{8,9},{9,8},{10,11... | collective-permute-start | bytes 3342344 | tf_op jit(solution)/shard_map/ppermute | solution.py:356
  9.6 3.1 %collective-permute-start = (bf16[272,2048]{1,0:T(8,128)(2,1)}, bf16[272,2048]{1,0:T(8,128)(2,1)}, u32[]{:S(2)}, u32[]{:S(2)}) collective-permute-start(bf16[272,2048]{1,0:T(8,128)(2,1)} %get-tuple-element.35.mine_ref), channel_id=1, source_target_pairs={{0,4},{1,5},{2,6},{3,7},{4,0},{5,1},{6,2},{7,3},{8,12},{9,13},{10,... | collective-permute-start | bytes 3342344 | tf_op jit(solution)/shard_map/cond/branch_1_fun/ppermute | solution.py:356
  17.3 31.4 %all-to-all-start = ((bf16[4,136,2048]{2,1,0:T(8,128)(2,1)}), bf16[4,136,2048]{2,1,0:T(8,128)(2,1)}, u32[]{:S(2)}, u32[]{:S(2)}) async-start(bf16[4,136,2048]{2,1,0:T(8,128)(2,1)} %get-tuple-element.208), calls=%async_computation | async-start | bytes 4456448 | tf_op jit(solution)/shard_map/all_to_all | solution.py:366
  21.8 4.8 %copy-start.1 = (bf16[1,2048,768]{2,1,0:T(8,128)(2,1)S(1)}, bf16[1,2048,768]{2,1,0:T(8,128)(2,1)}, u32[]{:S(2)}) copy-start(bf16[1,2048,768]{2,1,0:T(8,128)(2,1)} %refs_4_.2) | copy-start | bytes 9437188
  34.1 29.8 %collective-permute-start.10 = (bf16[272,2048]{1,0:T(8,128)(2,1)}, bf16[272,2048]{1,0:T(8,128)(2,1)S(1)}, u32[]{:S(2)}, u32[]{:S(2)}) collective-permute-start(bf16[272,2048]{1,0:T(8,128)(2,1)} %collective-permute-done.9), channel_id=1, source_target_pairs={{1,0},{2,3},{5,4},{6,7},{9,8},{10,11},{13,12},{14,15},{17,16},{18,... | collective-permute-start | bytes 3342344 | tf_op jit(solution)/shard_map/ppermute | solution.py:360
  35.4 28.5 %collective-permute-start.11 = (bf16[272,2048]{1,0:T(8,128)(2,1)}, bf16[272,2048]{1,0:T(8,128)(2,1)S(1)}, u32[]{:S(2)}, u32[]{:S(2)}) collective-permute-start(bf16[272,2048]{1,0:T(8,128)(2,1)} %collective-permute-done.8.mine_ref), channel_id=1, source_target_pairs={{1,2},{2,1},{5,6},{6,5},{9,10},{10,9},{13,14},{14,13},{17,18},{18,... | collective-permute-start | bytes 3342344 | tf_op jit(solution)/shard_map/ppermute | solution.py:360
  36.3 3.2 %collective-permute-start.1 = (bf16[272,2048]{1,0:T(8,128)(2,1)}, bf16[272,2048]{1,0:T(8,128)(2,1)}, u32[]{:S(2)}, u32[]{:S(2)}) collective-permute-start(bf16[272,2048]{1,0:T(8,128)(2,1)} %get-tuple-element.40.mine_ref), channel_id=1, source_target_pairs={{0,4},{1,5},{2,6},{3,7},{4,0},{5,1},{6,2},{7,3},{8,12},{9,13},{10,... | collective-permute-start | bytes 3342344 | tf_op jit(solution)/shard_map/cond/branch_1_fun/ppermute | solution.py:356
  48.7 26.9 %collective-permute-start.13 = (bf16[136,2048]{1,0:T(8,128)(2,1)}, bf16[136,2048]{1,0:T(8,128)(2,1)}, u32[]{:S(2)}, u32[]{:S(2)}) collective-permute-start(bf16[136,2048]{1,0:T(8,128)(2,1)} %get-tuple-element.228), channel_id=1, source_target_pairs={{0,8},{1,9},{2,10},{3,11},{4,12},{5,13},{6,14},{7,15},{8,0},{9,1},... | collective-permute-start | bytes 1671176 | tf_op jit(solution)/shard_map/ppermute | solution.py:356
  50.1 25.8 %collective-permute-start.14 = (bf16[136,2048]{1,0:T(8,128)(2,1)}, bf16[136,2048]{1,0:T(8,128)(2,1)}, u32[]{:S(2)}, u32[]{:S(2)}) collective-permute-start(bf16[136,2048]{1,0:T(8,128)(2,1)} %get-tuple-element.229), channel_id=1, source_target_pairs={{0,16},{1,17},{2,18},{3,19},{4,20},{5,21},{6,22},{7,23},{8,24},{9,... | collective-permute-start | bytes 1671176 | tf_op jit(solution)/shard_map/ppermute | solution.py:356
  50.6 25.2 %collective-permute-start.15 = (bf16[136,2048]{1,0:T(8,128)(2,1)}, bf16[136,2048]{1,0:T(8,128)(2,1)}, u32[]{:S(2)}, u32[]{:S(2)}) collective-permute-start(bf16[136,2048]{1,0:T(8,128)(2,1)} %get-tuple-element.230), channel_id=1, source_target_pairs={{0,24},{1,25},{2,26},{3,27},{4,28},{5,29},{6,30},{7,31},{8,16},{9,... | collective-permute-start | bytes 1671176 | tf_op jit(solution)/shard_map/ppermute | solution.py:356
  63.9 1.0 copy-start.3
  65.0 27.7 %collective-permute-start.12 = (bf16[272,2048]{1,0:T(8,128)(2,1)S(1)}, bf16[272,2048]{1,0:T(8,128)(2,1)}, u32[]{:S(2)}, u32[]{:S(2)}) collective-permute-start(bf16[272,2048]{1,0:T(8,128)(2,1)S(1)} %broadcast_select_fusion.mine_ref), channel_id=1, source_target_pairs={{0,1},{1,0},{2,3},{3,2},{4,5},{5,4},{6,7},{7,6},{8,9},{9,8},{10,11... | collective-permute-start | bytes 3342344 | tf_op jit(solution)/shard_map/ppermute | solution.py:356
  68.9 2.9 %collective-permute-start.2 = (bf16[272,2048]{1,0:T(8,128)(2,1)S(1)}, bf16[272,2048]{1,0:T(8,128)(2,1)}, u32[]{:S(2)}, u32[]{:S(2)}) collective-permute-start(bf16[272,2048]{1,0:T(8,128)(2,1)S(1)} %get-tuple-element.46.mine_ref), channel_id=1, source_target_pairs={{0,4},{1,5},{2,6},{3,7},{4,0},{5,1},{6,2},{7,3},{8,12},{9,13},{10,... | collective-permute-start | bytes 3342344 | tf_op jit(solution)/shard_map/cond/branch_1_fun/ppermute | solution.py:356
  75.9 23.8 %collective-permute-start.16 = (bf16[136,2048]{1,0:T(8,128)(2,1)}, bf16[136,2048]{1,0:T(8,128)(2,1)}, u32[]{:S(2)}, u32[]{:S(2)}) collective-permute-start(bf16[136,2048]{1,0:T(8,128)(2,1)} %get-tuple-element.255), channel_id=1, source_target_pairs={{0,8},{1,9},{2,10},{3,11},{4,12},{5,13},{6,14},{7,15},{8,0},{9,1},... | collective-permute-start | bytes 1671176 | tf_op jit(solution)/shard_map/ppermute | solution.py:356
  77.3 26.6 %collective-permute-start.17 = (bf16[136,2048]{1,0:T(8,128)(2,1)}, bf16[136,2048]{1,0:T(8,128)(2,1)}, u32[]{:S(2)}, u32[]{:S(2)}) collective-permute-start(bf16[136,2048]{1,0:T(8,128)(2,1)} %get-tuple-element.256), channel_id=1, source_target_pairs={{0,16},{1,17},{2,18},{3,19},{4,20},{5,21},{6,22},{7,23},{8,24},{9,... | collective-permute-start | bytes 1671176 | tf_op jit(solution)/shard_map/ppermute | solution.py:356
  78.8 25.2 %collective-permute-start.18 = (bf16[136,2048]{1,0:T(8,128)(2,1)S(1)}, bf16[136,2048]{1,0:T(8,128)(2,1)}, u32[]{:S(2)}, u32[]{:S(2)}) collective-permute-start(bf16[136,2048]{1,0:T(8,128)(2,1)S(1)} %get-tuple-element.257), channel_id=1, source_target_pairs={{0,24},{1,25},{2,26},{3,27},{4,28},{5,29},{6,30},{7,31},{8,16},{9,... | collective-permute-start | bytes 1671176 | tf_op jit(solution)/shard_map/ppermute | solution.py:356
  92.7 3.1 %collective-permute-start.3 = (bf16[272,2048]{1,0:T(8,128)(2,1)}, bf16[272,2048]{1,0:T(8,128)(2,1)}, u32[]{:S(2)}, u32[]{:S(2)}) collective-permute-start(bf16[272,2048]{1,0:T(8,128)(2,1)} %get-tuple-element.52.mine_ref), channel_id=1, source_target_pairs={{0,4},{1,5},{2,6},{3,7},{4,0},{5,1},{6,2},{7,3},{8,12},{9,13},{10,... | collective-permute-start | bytes 3342344 | tf_op jit(solution)/shard_map/cond/branch_1_fun/ppermute | solution.py:356
  104.0 15.8 %collective-permute-start.19 = (bf16[136,2048]{1,0:T(8,128)(2,1)}, bf16[136,2048]{1,0:T(8,128)(2,1)S(1)}, u32[]{:S(2)}, u32[]{:S(2)}) collective-permute-start(bf16[136,2048]{1,0:T(8,128)(2,1)} %get-tuple-element.269), channel_id=1, source_target_pairs={{0,8},{1,9},{2,10},{3,11},{4,12},{5,13},{6,14},{7,15},{8,0},{9,1},... | collective-permute-start | bytes 1671176 | tf_op jit(solution)/shard_map/ppermute | solution.py:356
  105.1 15.7 %collective-permute-start.20 = (bf16[136,2048]{1,0:T(8,128)(2,1)S(1)}, bf16[136,2048]{1,0:T(8,128)(2,1)}, u32[]{:S(2)}, u32[]{:S(2)}) collective-permute-start(bf16[136,2048]{1,0:T(8,128)(2,1)S(1)} %get-tuple-element.270), channel_id=1, source_target_pairs={{0,16},{1,17},{2,18},{3,19},{4,20},{5,21},{6,22},{7,23},{8,24},{9,... | collective-permute-start | bytes 1671176 | tf_op jit(solution)/shard_map/ppermute | solution.py:356
  106.0 24.8 %collective-permute-start.21 = (bf16[136,2048]{1,0:T(8,128)(2,1)S(1)}, bf16[136,2048]{1,0:T(8,128)(2,1)}, u32[]{:S(2)}, u32[]{:S(2)}) collective-permute-start(bf16[136,2048]{1,0:T(8,128)(2,1)S(1)} %get-tuple-element.271), channel_id=1, source_target_pairs={{0,24},{1,25},{2,26},{3,27},{4,28},{5,29},{6,30},{7,31},{8,16},{9,... | collective-permute-start | bytes 1671176 | tf_op jit(solution)/shard_map/ppermute | solution.py:356
  119.7 15.0 %copy-start.4 = (bf16[136,2048]{1,0:T(8,128)(2,1)}, bf16[136,2048]{1,0:T(8,128)(2,1)S(1)}, u32[]{:S(2)}) copy-start(bf16[136,2048]{1,0:T(8,128)(2,1)S(1)} %collective-permute-done.19.refs_1_) | copy-start | bytes 1671172
  130.7 17.4 %all-to-all-start.1 = ((bf16[4,1,72,2048]{3,2,1,0:T(8,128)(2,1)}), bf16[4,1,72,2048]{3,2,1,0:T(8,128)(2,1)S(1)}, u32[]{:S(2)}, u32[]{:S(2)}) async-start(bf16[4,1,72,2048]{3,2,1,0:T(8,128)(2,1)} %get-tuple-element.287), calls=%async_computation.1 | async-start | bytes 2359296 | tf_op jit(solution)/shard_map/all_to_all | solution.py:366
  149.9 2.0 collective-permute-start.4
  152.9 32.0 %all-to-all-start.2 = ((bf16[4,2,72,2048]{3,2,1,0:T(8,128)(2,1)}), bf16[4,2,72,2048]{3,2,1,0:T(8,128)(2,1)S(1)}, u32[]{:S(2)}, u32[]{:S(2)}) async-start(bf16[4,2,72,2048]{3,2,1,0:T(8,128)(2,1)} %get-tuple-element.311), calls=%async_computation.2 | async-start | bytes 4718592 | tf_op jit(solution)/shard_map/all_to_all | solution.py:366
  156.7 9.2 %slice-start = ((s8[4718592]{0:T(1024)(128)(4,1)}), s8[4194304]{0:T(1024)(128)(4,1)S(1)}, s32[]{:S(2)}) async-start(s8[4718592]{0:T(1024)(128)(4,1)} %bitcast.37), calls=%async_computation.4 | async-start | bytes 8388608
  156.7 9.2 %slice-start.1 = ((s8[4718592]{0:T(1024)(128)(4,1)}), s8[524288]{0:T(1024)(128)(4,1)S(1)}, s32[]{:S(2)}) async-start(s8[4718592]{0:T(1024)(128)(4,1)} %bitcast.37), calls=%async_computation.5 | async-start | bytes 1048576
  156.7 9.2 %copy-start.2 = (bf16[1152,768]{1,0:T(8,128)(2,1)S(1)}, bf16[1152,768]{1,0:T(8,128)(2,1)}, u32[]{:S(2)}) copy-start(bf16[1152,768]{1,0:T(8,128)(2,1)} %get-tuple-element.314) | copy-start | bytes 5308420
  156.7 34.8 %collective-permute-start.22 = (bf16[136,2048]{1,0:T(8,128)(2,1)}, bf16[136,2048]{1,0:T(8,128)(2,1)S(1)}, u32[]{:S(2)}, u32[]{:S(2)}) collective-permute-start(bf16[136,2048]{1,0:T(8,128)(2,1)} %get-tuple-element.381), channel_id=1, source_target_pairs={{0,2},{1,3},{2,0},{3,1},{4,6},{5,7},{6,4},{7,5},{8,10},{9,11},{10,... | collective-permute-start | bytes 1671176 | tf_op jit(solution)/shard_map/ppermute | solution.py:356
  188.5 2.0 collective-permute-start.5
  188.6 2.7 %collective-permute-start.6 = (bf16[136,2048]{1,0:T(8,128)(2,1)S(1)}, bf16[136,2048]{1,0:T(8,128)(2,1)S(1)}, u32[]{:S(2)}, u32[]{:S(2)}) collective-permute-start(bf16[136,2048]{1,0:T(8,128)(2,1)S(1)} %get-tuple-element.63), channel_id=1, source_target_pairs={{0,4},{1,5},{2,6},{3,7},{4,0},{5,1},{6,2},{7,3},{8,12},{9,13},{10,... | collective-permute-start | bytes 1671176 | tf_op jit(solution)/shard_map/cond/branch_1_fun/ppermute | solution.py:356
  191.5 0.8 copy-start.5
  191.5 1.0 copy-start.6
  192.5 19.3 %all-to-all-start.3 = ((bf16[4,1,72,2048]{3,2,1,0:T(8,128)(2,1)}), bf16[4,1,72,2048]{3,2,1,0:T(8,128)(2,1)S(1)}, u32[]{:S(2)}, u32[]{:S(2)}) async-start(bf16[4,1,72,2048]{3,2,1,0:T(8,128)(2,1)} %get-tuple-element.327), calls=%async_computation.3 | async-start | bytes 2359296 | tf_op jit(solution)/shard_map/all_to_all | solution.py:366
  196.3 26.9 %collective-permute-start.23 = (bf16[136,2048]{1,0:T(8,128)(2,1)}, bf16[136,2048]{1,0:T(8,128)(2,1)S(1)}, u32[]{:S(2)}, u32[]{:S(2)}) collective-permute-start(bf16[136,2048]{1,0:T(8,128)(2,1)} %copy-done.5), channel_id=1, source_target_pairs={{0,1},{1,0},{2,3},{3,2},{4,5},{5,4},{6,7},{7,6},{8,9},{9,8},{10,11... | collective-permute-start | bytes 1671176 | tf_op jit(solution)/shard_map/ppermute | solution.py:356
  196.3 26.8 %collective-permute-start.24 = (bf16[136,2048]{1,0:T(8,128)(2,1)}, bf16[136,2048]{1,0:T(8,128)(2,1)S(1)}, u32[]{:S(2)}, u32[]{:S(2)}) collective-permute-start(bf16[136,2048]{1,0:T(8,128)(2,1)} %copy-done.6), channel_id=1, source_target_pairs={{0,3},{1,2},{2,1},{3,0},{4,7},{5,6},{6,5},{7,4},{8,11},{9,10},{10,... | collective-permute-start | bytes 1671176 | tf_op jit(solution)/shard_map/ppermute | solution.py:356
  214.4 8.7 %copy-start = (s32[128,8]{0,1:T(8,128)S(1)}, s32[128,8]{0,1:T(8,128)}, u32[]{:S(2)}) copy-start(s32[128,8]{0,1:T(8,128)} %param.24) | copy-start | bytes 12292
  214.4 2.2 collective-permute-start.7
